TPU v7x, 512 devices: a whole 4x4x16 slice. The times are simulated.
512 devices in a mesh: seq: 64 (over z, y), head: 8 (over x, core).
Axes of the slice: x: 4, y: 4, z: 16, core: 2. Of those that a mesh axis runs over, the one named last changes fastest.
Arguments:
- queries: bfloat16 [65536, 4096], P('seq', 'head'), may hold values from -120 to 120
- keys: bfloat16 [65536, 4096], P('seq', 'head'), may hold values from -6 to 6
- values: bfloat16 [65536, 4096], P('seq', 'head'), may hold values from -54 to 54
- head_temp: float32 [32], P('head'), may hold values from 0.5 to 3
- norm_gain: float32 [4096], P('head'), may hold values from 0.25 to 1.75
Outputs:
- normed: bfloat16 [65536, 4096], P('seq', 'head')
All inputs are finite; a program needn't handle non-finite values.
Results may differ from a plain program's by a relative error of at most 0.0034.
Values may be sent and summed in bfloat16 or wider, within the bound.
No kernel may reach another device: no remote copies, remote signals or barrier semaphores. Data moves between devices by JAX's collectives and lax.ppermute only.
A program may use at most 128 MiB of HBM per device.

v0:
```python
import math

import jax
import jax.numpy as jnp
from jax import lax
from jax.sharding import PartitionSpec as P

HEADS = 32
HEAD_DIM = 128
BLK = 128


EPS = 1e-06
LOG_FOUR = math.log(4.0)


def padded(value, sides, width):
    for axis, dim in sides:
        count, length = (lax.axis_size(axis), value.shape[dim])
        up = [(i, (i + 1) % count) for i in range(count - 1)]
        down = [(j, i) for i, j in up]
        last = lax.slice_in_dim(value, length - width, length, axis=dim)
        initial = lax.slice_in_dim(value, 0, width, axis=dim)
        before = lax.ppermute(last, axis, up)
        after = lax.ppermute(initial, axis, down)
        value = jnp.concatenate([before, value, after], axis=dim)
    return value


def from_behind(value, axis, by):
    count = lax.axis_size(axis)
    pairs = [(i, i + by) for i in range(count) if 0 <= i + by < count]
    return lax.ppermute(value, axis, pairs)


def coarsen(stacked, factor):
    leading, entries, columns = stacked.shape
    grouped = stacked.reshape(leading, entries // factor, factor, columns).astype(jnp.float32)
    return jnp.mean(grouped, axis=2).astype(jnp.bfloat16)


def level_scores(
    query_rows,
    extended,
    ext_start,
    first_row,
    span_tokens,
    group_size,
    level_index,
    score_scale,
    total_rows,
):
    rows_here = query_rows.shape[0]
    groups = max(1, rows_here // span_tokens)
    per_group = rows_here // groups
    block_first = first_row // span_tokens * span_tokens
    start_entry = (block_first - span_tokens - ext_start) // group_size
    window_piece = lax.dynamic_slice_in_dim(extended, start_entry, (groups + 2) * BLK, 1)
    block_parts = window_piece.reshape(2, groups + 2, BLK, extended.shape[2])
    windows = jnp.concatenate(
        (block_parts[:, :-2], block_parts[:, 1:-1], block_parts[:, 2:]), axis=2
    )
    grouped = query_rows.reshape(groups, per_group, query_rows.shape[1])
    raw_scores = jnp.einsum("gqd,gkd->gqk", grouped, windows[0], preferred_element_type=jnp.float32)
    entry_index = (
        (block_first // span_tokens - 1) * BLK
        + BLK * jnp.arange(groups, dtype=jnp.int32)[:, None]
        + jnp.arange(3 * BLK, dtype=jnp.int32)[None, :]
    )
    entry_token = (entry_index * group_size)[:, None, :]
    query_token = (first_row + jnp.arange(rows_here, dtype=jnp.int32)).reshape(groups, per_group, 1)
    usable = (entry_token >= 0) & (entry_token < total_rows)
    if level_index > 0:
        inner_span = span_tokens // 4
        inner_low = (query_token // inner_span - 1) * inner_span
        usable = usable & jnp.logical_not(
            (entry_token >= inner_low) & (entry_token < inner_low + 3 * inner_span)
        )
    scores = jnp.where(usable, raw_scores * score_scale + level_index * LOG_FOUR, -jnp.inf)
    return (scores, usable, windows[1])


def far_scores(query_rows, farthest, first_row, score_scale, total_rows):
    rows_here = query_rows.shape[0]
    raw_scores = jnp.einsum(
        "qd,kd->qk", query_rows, farthest[0], preferred_element_type=jnp.float32
    )
    entry_token = (jnp.arange(farthest.shape[1], dtype=jnp.int32) * 64)[None, :]
    query_token = (first_row + jnp.arange(rows_here, dtype=jnp.int32))[:, None]
    outer_span = 16 * BLK
    outer_low = (query_token // outer_span - 1) * outer_span
    usable = jnp.logical_not(
        (entry_token >= outer_low) & (entry_token < outer_low + 3 * outer_span)
    )
    usable = usable & (entry_token < total_rows)
    scores = jnp.where(usable, raw_scores * score_scale + 3.0 * LOG_FOUR, -jnp.inf)
    return (scores[None], usable[None], farthest[1][None])


def attend(levels, rows_here):
    row_max = None
    for scores, usable, unused_values in levels:
        level_max = jnp.max(scores, axis=-1).reshape(rows_here)
        row_max = level_max if row_max is None else jnp.maximum(row_max, level_max)
    denominator = jnp.zeros((rows_here,), jnp.float32)
    numerator = None
    for scores, usable, entry_values in levels:
        groups, per_group, unused_dim = scores.shape
        shifted = row_max.reshape(groups, per_group, 1)
        weights = jnp.where(usable, jnp.exp(scores - shifted), 0.0)
        denominator = denominator + jnp.sum(weights, axis=-1).reshape(rows_here)
        weights_low = weights.astype(jnp.bfloat16)
        term = jnp.einsum(
            "gqk,gkd->gqd", weights_low, entry_values, preferred_element_type=jnp.float32
        )
        term = term.reshape(rows_here, entry_values.shape[2])
        numerator = term if numerator is None else numerator + term
    return numerator / denominator[:, None]


def local(queries, keys, values, head_temp, norm_gain):
    rows_here = queries.shape[0]
    heads_here = queries.shape[1] // HEAD_DIM
    first_row = lax.axis_index("seq") * rows_here
    total_rows = rows_here * lax.axis_size("seq")
    stacked = jnp.stack((keys, values))
    coarse_one = coarsen(stacked, 4)
    fine_ext = padded(stacked, (("seq", 1),), BLK)
    one_ext = padded(coarse_one, (("seq", 1),), BLK)
    coarse_two = coarsen(coarse_one, 4)
    span_two = 16 * BLK
    reach_devices = max(1, 2 * span_two // rows_here - 1)
    pieces = []
    for offset in range(reach_devices, -reach_devices - 1, -1):
        if offset == 0:
            pieces.append(coarse_two)
        else:
            pieces.append(from_behind(coarse_two, "seq", offset))
    two_ext = jnp.concatenate(pieces, axis=1)
    two_start = first_row - reach_devices * rows_here
    farthest = lax.all_gather(coarsen(coarse_two, 4), "seq", axis=1, tiled=True)

    def one_head(head_index):
        column = head_index * HEAD_DIM
        query_rows = lax.dynamic_slice_in_dim(queries, column, HEAD_DIM, 1)

        def select_head(array):
            return lax.dynamic_slice_in_dim(array, column, HEAD_DIM, 2)

        score_scale = head_temp[head_index] / math.sqrt(HEAD_DIM)
        levels = [
            level_scores(
                query_rows,
                select_head(fine_ext),
                first_row - BLK,
                first_row,
                BLK,
                1,
                0,
                score_scale,
                total_rows,
            ),
            level_scores(
                query_rows,
                select_head(one_ext),
                first_row - 4 * BLK,
                first_row,
                4 * BLK,
                4,
                1,
                score_scale,
                total_rows,
            ),
            level_scores(
                query_rows,
                select_head(two_ext),
                two_start,
                first_row,
                span_two,
                16,
                2,
                score_scale,
                total_rows,
            ),
            far_scores(query_rows, select_head(farthest), first_row, score_scale, total_rows),
        ]
        return attend(levels, rows_here)

    per_head = lax.map(one_head, jnp.arange(heads_here, dtype=jnp.int32))
    attended = jnp.transpose(per_head, (1, 0, 2)).reshape(rows_here, heads_here * HEAD_DIM)
    local_sum = jnp.sum(attended * attended, axis=1)
    summed = lax.psum(local_sum, "head")
    inverse = lax.rsqrt(summed / (HEADS * HEAD_DIM) + EPS)
    return (attended * inverse[:, None] * norm_gain[None, :]).astype(jnp.bfloat16)


def solution(mesh):
    return jax.shard_map(
        local,
        mesh=mesh,
        in_specs=(P("seq", "head"), P("seq", "head"), P("seq", "head"), P("head"), P("head")),
        out_specs=P("seq", "head"),
        check_vma=False,
    )
```

profile of v0, /device:TPU:1, one launch (start us, length us, event | category | flops | bytes accessed | tf_op | source)
XLA Modules:
  0.0 326.5 jit_solution(15481094661513954896)
XLA Ops:
  6.5 1.4 stack.18
  8.1 1.1 stack.19
  9.2 4.1 %convert_reduce_fusion = f32[2,256,512]{2,1,0:T(8,128)S(1)} fusion(bf16[1,256,4,512]{3,2,1,0:T(4,128)(2,1)} %stack.19, bf16[1,256,4,512]{3,2,1,0:T(4,128)(2,1)S(1)} %stack.18), kind=kLoop, calls=%fused_computation.107 | loop fusion | flops 2883584 | bytes 3145728 | tf_op jit(solution)/shard_map/reduce_sum | solution.py:39
  13.4 1.3 reshape.603
  14.7 1.9 reduce_sum.81
  17.6 6.1 %collective-permute-start.4 = (bf16[2,64,512]{2,1,0:T(8,128)(2,1)S(1)}, bf16[2,64,512]{2,1,0:T(8,128)(2,1)}, u32[]{:S(2)}, u32[]{:S(2)}) collective-permute-start(bf16[2,64,512]{2,1,0:T(8,128)(2,1)S(1)} %multiply_convert_fusion.1), channel_id=1, source_target_pairs={{0,24},{8,32},{16,40},{24,48},{32,56},{40,64},{48,72},{56,80},{64,... | collective-permute-start | bytes 393224 | tf_op jit(solution)/shard_map/ppermute | solution.py:33
  23.7 4.3 %collective-permute-start.5 = (bf16[2,64,512]{2,1,0:T(8,128)(2,1)S(1)}, bf16[2,64,512]{2,1,0:T(8,128)(2,1)}, u32[]{:S(2)}, u32[]{:S(2)}) collective-permute-start(bf16[2,64,512]{2,1,0:T(8,128)(2,1)S(1)} %multiply_convert_fusion.1), channel_id=1, source_target_pairs={{0,16},{8,24},{16,32},{24,40},{32,48},{40,56},{48,64},{56,72},{64,... | collective-permute-start | bytes 393224 | tf_op jit(solution)/shard_map/ppermute | solution.py:33
  28.0 2.6 collective-permute-start.6
  30.6 1.3 collective-permute-start.7
  31.9 1.3 collective-permute-start.8
  34.2 1.3 collective-permute-start.9
  35.5 1.6 constant_dynamic-update-slice_fusion.6
  37.1 4.0 %collective-permute-start.2 = (bf16[2,128,512]{2,1,0:T(8,128)(2,1)}, bf16[2,128,512]{2,1,0:T(8,128)(2,1)S(1)}, u32[]{:S(2)}, u32[]{:S(2)}) collective-permute-start(bf16[2,128,512]{2,1,0:T(8,128)(2,1)} %get-tuple-element.663), channel_id=1, source_target_pairs={{0,8},{8,16},{16,24},{24,32},{32,40},{40,48},{48,56},{56,64},{64,7... | collective-permute-start | bytes 786440 | tf_op jit(solution)/shard_map/ppermute | solution.py:24
  41.1 1.6 constant_dynamic-update-slice_fusion.5
  42.7 1.3 collective-permute-start.3
  44.0 1.6 constant_dynamic-update-slice_fusion.4
  46.2 4.0 %collective-permute-start = (bf16[2,128,512]{2,1,0:T(8,128)(2,1)S(1)}, bf16[2,128,512]{2,1,0:T(8,128)(2,1)S(1)}, u32[]{:S(2)}, u32[]{:S(2)}) collective-permute-start(bf16[2,128,512]{2,1,0:T(8,128)(2,1)S(1)} %get-tuple-element.661), channel_id=1, source_target_pairs={{0,8},{8,16},{16,24},{24,32},{32,40},{40,48},{48,56},{56,64},{64,7... | collective-permute-start | bytes 786440 | tf_op jit(solution)/shard_map/ppermute | solution.py:24
  50.2 1.6 constant_dynamic-update-slice_fusion.2
  51.8 1.3 collective-permute-start.1
  53.1 1.6 constant_dynamic-update-slice_fusion.1
  55.3 1.0 pad_maximum_fusion.4
  56.4 4.5 %collective-permute-done.1 = bf16[2,128,512]{2,1,0:T(8,128)(2,1)S(1)} collective-permute-done((bf16[2,128,512]{2,1,0:T(8,128)(2,1)S(1)}, bf16[2,128,512]{2,1,0:T(8,128)(2,1)S(1)}, u32[]{:S(2)}, u32[]{:S(2)}) %collective-permute-start.1) | collective-permute-done | bytes 262176 | tf_op jit(solution)/shard_map/ppermute | solution.py:25
  60.9 1.6 pad_maximum_fusion.3
  62.5 92.7 %all-gather.2.cloned.1.call-done = bf16[2,1024,512]{2,1,0:T(8,128)(2,1)} async-done(((bf16[2,16,512]{2,1,0:T(8,128)(2,1)}), bf16[2,1024,512]{2,1,0:T(8,128)(2,1)}) %all-gather.2.cloned.1.call-update) | async-done | bytes 2097168 | tf_op jit(solution)/shard_map/all_gather | solution.py:141
  155.2 138.5 %while.13 = (s32[]{:T(128)}, f32[4,1024,128]{2,1,0:T(8,128)}, s32[]{:T(128)}, s32[4]{0:T(128)S(1)}, bf16[1024,512]{1,0:T(8,128)(2,1)}, /*index=5*/bf16[2,1280,51...) while((s32[]{:T(128)}, f32[4,1024,128]{2,1,0:T(8,128)}, ...), condition=%wide.region_12.13_spmd, body=%wide.region_3.12_spmd.sunk | while | flops 1203681152 | bytes 91520496 | solution.py:189
  163.2 1.9 fusion.107
  165.1 1.2 constant_dynamic-slice_fusion.9
  167.0 1.8 fusion.105
  168.9 4.5 %fusion.103 = (f32[1024]{0:T(1024)S(1)}, f32[1024,1024]{0,1:T(8,128)}) fusion(f32[]{:T(128)} %bitcast.138, pred[1024]{0:T(1024)(128)(4,1)S(1)} %broadcast_compare_fusion.2, s32[1024]{0:T(1024)S(1)} %get-tuple-element.773, s32[1024]{0:T(1024)S(1)} %get-tuple-element.774, s32[1024]{0:T(1024)S(1)} %iota_multiply_fusion.2, ...), kind=kOutput, calls=%fused_computation.3.clone.1 | convolution fusion | flops 277871616 | bytes 4736516 | tf_op jit(solution)/shard_map/while/body/eval_jaxpr/qd,kd->qk/dot_general | solution.py:85
  173.9 2.2 fusion.117
  176.8 3.9 %fusion.115 = f32[1024]{0:T(1024)S(1)} fusion(f32[1024,1024]{0,1:T(8,128)} %get-tuple-element.775, f32[1024]{0:T(1024)S(1)} %fusion.111, f32[]{:T(128)} %bitcast.138, pred[1024]{0:T(1024)(128)(4,1)S(1)} %broadcast_compare_fusion.2, s32[1024]{0:T(1024)S(1)} %get-tuple-element.773, s32[1024]{0:T(1024)S(1)} %get-tuple-element.774, ...), kind=kLoop, calls=%fused_computation.4.clone.1 | loop fusion | flops 11533312 | bytes 4215812 | tf_op jit(solution)/shard_map/while/body/eval_jaxpr/reduce_sum | solution.py:111
  182.2 1.2 fusion.113
  183.5 4.6 %fusion.112 = f32[1024,128]{1,0:T(8,128)S(1)} fusion(f32[1024,1024]{0,1:T(8,128)} %get-tuple-element.775, f32[1024]{0:T(1024)S(1)} %fusion.111, f32[]{:T(128)} %bitcast.138, bf16[2,1024,512]{2,1,0:T(8,128)(2,1)} %get-tuple-element.853, s32[]{:T(128)S(6)} %add.742, s32[]{:T(128)S(6)} %select_n.289, s32[1024]{0:T(1024)S(1)} %get-tuple-element.773, ...), kind=kOutput, calls=%fused_computation.6.clone.1 | convolution fusion | flops 279969792 | bytes 4998664 | tf_op jit(solution)/shard_map/while/body/eval_jaxpr/gqk,gkd->gqd/dot_general | solution.py:113
  188.1 1.8 fusion.120
  197.8 1.9 fusion.107
  199.7 1.2 constant_dynamic-slice_fusion.9
  201.7 1.8 fusion.105
  203.5 4.5 %fusion.103 = (f32[1024]{0:T(1024)S(1)}, f32[1024,1024]{0,1:T(8,128)}) fusion(f32[]{:T(128)} %bitcast.138, pred[1024]{0:T(1024)(128)(4,1)S(1)} %broadcast_compare_fusion.2, s32[1024]{0:T(1024)S(1)} %get-tuple-element.773, s32[1024]{0:T(1024)S(1)} %get-tuple-element.774, s32[1024]{0:T(1024)S(1)} %iota_multiply_fusion.2, ...), kind=kOutput, calls=%fused_computation.3.clone.1 | convolution fusion | flops 277871616 | bytes 4736516 | tf_op jit(solution)/shard_map/while/body/eval_jaxpr/qd,kd->qk/dot_general | solution.py:85
  208.6 2.2 fusion.117
  211.5 3.9 %fusion.115 = f32[1024]{0:T(1024)S(1)} fusion(f32[1024,1024]{0,1:T(8,128)} %get-tuple-element.775, f32[1024]{0:T(1024)S(1)} %fusion.111, f32[]{:T(128)} %bitcast.138, pred[1024]{0:T(1024)(128)(4,1)S(1)} %broadcast_compare_fusion.2, s32[1024]{0:T(1024)S(1)} %get-tuple-element.773, s32[1024]{0:T(1024)S(1)} %get-tuple-element.774, ...), kind=kLoop, calls=%fused_computation.4.clone.1 | loop fusion | flops 11533312 | bytes 4215812 | tf_op jit(solution)/shard_map/while/body/eval_jaxpr/reduce_sum | solution.py:111
  216.9 1.2 fusion.113
  218.2 4.6 %fusion.112 = f32[1024,128]{1,0:T(8,128)S(1)} fusion(f32[1024,1024]{0,1:T(8,128)} %get-tuple-element.775, f32[1024]{0:T(1024)S(1)} %fusion.111, f32[]{:T(128)} %bitcast.138, bf16[2,1024,512]{2,1,0:T(8,128)(2,1)} %get-tuple-element.853, s32[]{:T(128)S(6)} %add.742, s32[]{:T(128)S(6)} %select_n.289, s32[1024]{0:T(1024)S(1)} %get-tuple-element.773, ...), kind=kOutput, calls=%fused_computation.6.clone.1 | convolution fusion | flops 279969792 | bytes 4998664 | tf_op jit(solution)/shard_map/while/body/eval_jaxpr/gqk,gkd->gqd/dot_general | solution.py:113
  222.8 1.7 fusion.120
  232.5 1.9 fusion.107
  234.4 1.2 constant_dynamic-slice_fusion.9
  236.3 1.8 fusion.105
  238.2 4.5 %fusion.103 = (f32[1024]{0:T(1024)S(1)}, f32[1024,1024]{0,1:T(8,128)}) fusion(f32[]{:T(128)} %bitcast.138, pred[1024]{0:T(1024)(128)(4,1)S(1)} %broadcast_compare_fusion.2, s32[1024]{0:T(1024)S(1)} %get-tuple-element.773, s32[1024]{0:T(1024)S(1)} %get-tuple-element.774, s32[1024]{0:T(1024)S(1)} %iota_multiply_fusion.2, ...), kind=kOutput, calls=%fused_computation.3.clone.1 | convolution fusion | flops 277871616 | bytes 4736516 | tf_op jit(solution)/shard_map/while/body/eval_jaxpr/qd,kd->qk/dot_general | solution.py:85
  243.2 2.2 fusion.117
  246.2 3.9 %fusion.115 = f32[1024]{0:T(1024)S(1)} fusion(f32[1024,1024]{0,1:T(8,128)} %get-tuple-element.775, f32[1024]{0:T(1024)S(1)} %fusion.111, f32[]{:T(128)} %bitcast.138, pred[1024]{0:T(1024)(128)(4,1)S(1)} %broadcast_compare_fusion.2, s32[1024]{0:T(1024)S(1)} %get-tuple-element.773, s32[1024]{0:T(1024)S(1)} %get-tuple-element.774, ...), kind=kLoop, calls=%fused_computation.4.clone.1 | loop fusion | flops 11533312 | bytes 4215812 | tf_op jit(solution)/shard_map/while/body/eval_jaxpr/reduce_sum | solution.py:111
  251.5 1.2 fusion.113
  252.8 4.6 %fusion.112 = f32[1024,128]{1,0:T(8,128)S(1)} fusion(f32[1024,1024]{0,1:T(8,128)} %get-tuple-element.775, f32[1024]{0:T(1024)S(1)} %fusion.111, f32[]{:T(128)} %bitcast.138, bf16[2,1024,512]{2,1,0:T(8,128)(2,1)} %get-tuple-element.853, s32[]{:T(128)S(6)} %add.742, s32[]{:T(128)S(6)} %select_n.289, s32[1024]{0:T(1024)S(1)} %get-tuple-element.773, ...), kind=kOutput, calls=%fused_computation.6.clone.1 | convolution fusion | flops 279969792 | bytes 4998664 | tf_op jit(solution)/shard_map/while/body/eval_jaxpr/gqk,gkd->gqd/dot_general | solution.py:113
  257.4 1.7 fusion.120
  267.1 1.9 fusion.107
  269.0 1.1 constant_dynamic-slice_fusion.9
  270.9 1.8 fusion.105
  272.7 4.5 %fusion.103 = (f32[1024]{0:T(1024)S(1)}, f32[1024,1024]{0,1:T(8,128)}) fusion(f32[]{:T(128)} %bitcast.138, pred[1024]{0:T(1024)(128)(4,1)S(1)} %broadcast_compare_fusion.2, s32[1024]{0:T(1024)S(1)} %get-tuple-element.773, s32[1024]{0:T(1024)S(1)} %get-tuple-element.774, s32[1024]{0:T(1024)S(1)} %iota_multiply_fusion.2, ...), kind=kOutput, calls=%fused_computation.3.clone.1 | convolution fusion | flops 277871616 | bytes 4736516 | tf_op jit(solution)/shard_map/while/body/eval_jaxpr/qd,kd->qk/dot_general | solution.py:85
  277.8 2.2 fusion.117
  280.7 3.9 %fusion.115 = f32[1024]{0:T(1024)S(1)} fusion(f32[1024,1024]{0,1:T(8,128)} %get-tuple-element.775, f32[1024]{0:T(1024)S(1)} %fusion.111, f32[]{:T(128)} %bitcast.138, pred[1024]{0:T(1024)(128)(4,1)S(1)} %broadcast_compare_fusion.2, s32[1024]{0:T(1024)S(1)} %get-tuple-element.773, s32[1024]{0:T(1024)S(1)} %get-tuple-element.774, ...), kind=kLoop, calls=%fused_computation.4.clone.1 | loop fusion | flops 11533312 | bytes 4215812 | tf_op jit(solution)/shard_map/while/body/eval_jaxpr/reduce_sum | solution.py:111
  286.1 1.2 fusion.113
  287.4 4.6 %fusion.112 = f32[1024,128]{1,0:T(8,128)S(1)} fusion(f32[1024,1024]{0,1:T(8,128)} %get-tuple-element.775, f32[1024]{0:T(1024)S(1)} %fusion.111, f32[]{:T(128)} %bitcast.138, bf16[2,1024,512]{2,1,0:T(8,128)(2,1)} %get-tuple-element.853, s32[]{:T(128)S(6)} %add.742, s32[]{:T(128)S(6)} %select_n.289, s32[1024]{0:T(1024)S(1)} %get-tuple-element.773, ...), kind=kOutput, calls=%fused_computation.6.clone.1 | convolution fusion | flops 279969792 | bytes 4998664 | tf_op jit(solution)/shard_map/while/body/eval_jaxpr/gqk,gkd->gqd/dot_general | solution.py:113
  292.0 1.7 fusion.120
  293.7 1.8 fusion.54
  295.6 21.3 %psum.7 = f32[1024]{0:T(1024)S(1)} all-reduce(f32[1024]{0:T(1024)S(1)} %fusion.54), channel_id=1, replica_groups=mesh['seq'=64,'head'=8] {'head'}, use_global_device_ids=true, to_apply=%region_14.15 | all-reduce | flops 1024 | bytes 8192 | tf_op jit(solution)/shard_map/psum | solution.py:192
  316.9 2.8 fusion.53
  (255 shorter events, 36.2 us)
Async XLA Ops:
  6.5 1.5 copy-start.7
  6.5 148.7 %all-gather.2.cloned.1.call-start = ((), (), s32[]{:S(2)}) async-start(), calls=%async_computation | async-start | bytes 2129920 | tf_op jit(solution)/shard_map/all_gather | solution.py:141
  14.7 19.3 %copy-start.8 = (bf16[1024,512]{1,0:T(8,128)(2,1)S(1)}, bf16[1024,512]{1,0:T(8,128)(2,1)}, u32[]{:S(2)}) copy-start(bf16[1024,512]{1,0:T(8,128)(2,1)} %param.8) | copy-start | bytes 3145732
  17.6 16.6 %collective-permute-start.4 = (bf16[2,64,512]{2,1,0:T(8,128)(2,1)S(1)}, bf16[2,64,512]{2,1,0:T(8,128)(2,1)}, u32[]{:S(2)}, u32[]{:S(2)}) collective-permute-start(bf16[2,64,512]{2,1,0:T(8,128)(2,1)S(1)} %multiply_convert_fusion.1), channel_id=1, source_target_pairs={{0,24},{8,32},{16,40},{24,48},{32,56},{40,64},{48,72},{56,80},{64,... | collective-permute-start | bytes 393224 | tf_op jit(solution)/shard_map/ppermute | solution.py:33
  23.7 13.4 %collective-permute-start.5 = (bf16[2,64,512]{2,1,0:T(8,128)(2,1)S(1)}, bf16[2,64,512]{2,1,0:T(8,128)(2,1)}, u32[]{:S(2)}, u32[]{:S(2)}) collective-permute-start(bf16[2,64,512]{2,1,0:T(8,128)(2,1)S(1)} %multiply_convert_fusion.1), channel_id=1, source_target_pairs={{0,16},{8,24},{16,32},{24,40},{32,48},{40,56},{48,64},{56,72},{64,... | collective-permute-start | bytes 393224 | tf_op jit(solution)/shard_map/ppermute | solution.py:33
  28.0 14.7 %collective-permute-start.6 = (bf16[2,64,512]{2,1,0:T(8,128)(2,1)S(1)}, bf16[2,64,512]{2,1,0:T(8,128)(2,1)}, u32[]{:S(2)}, u32[]{:S(2)}) collective-permute-start(bf16[2,64,512]{2,1,0:T(8,128)(2,1)S(1)} %multiply_convert_fusion.1), channel_id=1, source_target_pairs={{0,8},{8,16},{16,24},{24,32},{32,40},{40,48},{48,56},{56,64},{64,7... | collective-permute-start | bytes 393224 | tf_op jit(solution)/shard_map/ppermute | solution.py:33
  30.6 15.6 %collective-permute-start.7 = (bf16[2,64,512]{2,1,0:T(8,128)(2,1)S(1)}, bf16[2,64,512]{2,1,0:T(8,128)(2,1)}, u32[]{:S(2)}, u32[]{:S(2)}) collective-permute-start(bf16[2,64,512]{2,1,0:T(8,128)(2,1)S(1)} %multiply_convert_fusion.1), channel_id=1, source_target_pairs={{8,0},{16,8},{24,16},{32,24},{40,32},{48,40},{56,48},{64,56},{72,6... | collective-permute-start | bytes 393224 | tf_op jit(solution)/shard_map/ppermute | solution.py:33
  31.9 20.0 %collective-permute-start.8 = (bf16[2,64,512]{2,1,0:T(8,128)(2,1)S(1)}, bf16[2,64,512]{2,1,0:T(8,128)(2,1)}, u32[]{:S(2)}, u32[]{:S(2)}) collective-permute-start(bf16[2,64,512]{2,1,0:T(8,128)(2,1)S(1)} %multiply_convert_fusion.1), channel_id=1, source_target_pairs={{16,0},{24,8},{32,16},{40,24},{48,32},{56,40},{64,48},{72,56},{80,... | collective-permute-start | bytes 393224 | tf_op jit(solution)/shard_map/ppermute | solution.py:33
  34.2 20.4 %collective-permute-start.9 = (bf16[2,64,512]{2,1,0:T(8,128)(2,1)S(1)}, bf16[2,64,512]{2,1,0:T(8,128)(2,1)S(1)}, u32[]{:S(2)}, u32[]{:S(2)}) collective-permute-start(bf16[2,64,512]{2,1,0:T(8,128)(2,1)S(1)} %multiply_convert_fusion.1), channel_id=1, source_target_pairs={{24,0},{32,8},{40,16},{48,24},{56,32},{64,40},{72,48},{80,56},{88,... | collective-permute-start | bytes 393224 | tf_op jit(solution)/shard_map/ppermute | solution.py:33
  37.1 18.2 %collective-permute-start.2 = (bf16[2,128,512]{2,1,0:T(8,128)(2,1)}, bf16[2,128,512]{2,1,0:T(8,128)(2,1)S(1)}, u32[]{:S(2)}, u32[]{:S(2)}) collective-permute-start(bf16[2,128,512]{2,1,0:T(8,128)(2,1)} %get-tuple-element.663), channel_id=1, source_target_pairs={{0,8},{8,16},{16,24},{24,32},{32,40},{40,48},{48,56},{56,64},{64,7... | collective-permute-start | bytes 786440 | tf_op jit(solution)/shard_map/ppermute | solution.py:24
  42.7 12.7 %collective-permute-start.3 = (bf16[2,128,512]{2,1,0:T(8,128)(2,1)}, bf16[2,128,512]{2,1,0:T(8,128)(2,1)S(1)}, u32[]{:S(2)}, u32[]{:S(2)}) collective-permute-start(bf16[2,128,512]{2,1,0:T(8,128)(2,1)} %get-tuple-element.664), channel_id=1, source_target_pairs={{8,0},{16,8},{24,16},{32,24},{40,32},{48,40},{56,48},{64,56},{72,6... | collective-permute-start | bytes 786440 | tf_op jit(solution)/shard_map/ppermute | solution.py:25
  46.2 10.2 %collective-permute-start = (bf16[2,128,512]{2,1,0:T(8,128)(2,1)S(1)}, bf16[2,128,512]{2,1,0:T(8,128)(2,1)S(1)}, u32[]{:S(2)}, u32[]{:S(2)}) collective-permute-start(bf16[2,128,512]{2,1,0:T(8,128)(2,1)S(1)} %get-tuple-element.661), channel_id=1, source_target_pairs={{0,8},{8,16},{16,24},{24,32},{32,40},{40,48},{48,56},{56,64},{64,7... | collective-permute-start | bytes 786440 | tf_op jit(solution)/shard_map/ppermute | solution.py:24
  51.8 9.1 %collective-permute-start.1 = (bf16[2,128,512]{2,1,0:T(8,128)(2,1)S(1)}, bf16[2,128,512]{2,1,0:T(8,128)(2,1)S(1)}, u32[]{:S(2)}, u32[]{:S(2)}) collective-permute-start(bf16[2,128,512]{2,1,0:T(8,128)(2,1)S(1)} %get-tuple-element.662), channel_id=1, source_target_pairs={{8,0},{16,8},{24,16},{32,24},{40,32},{48,40},{56,48},{64,56},{72,6... | collective-permute-start | bytes 786440 | tf_op jit(solution)/shard_map/ppermute | solution.py:25
  56.4 98.8 %copy-start.12 = (f32[4]{0:T(128)S(1)}, f32[4]{0:T(128)}, u32[]{:S(2)}) copy-start(f32[4]{0:T(128)} %param.10) | copy-start | bytes 52
  155.2 1.8 copy-start.3
  163.0 2.1 copy-start.5
  166.3 0.7 copy-start.9
  173.9 2.3 copy-start.1
  180.8 1.4 copy-start
  180.8 1.5 copy-start.6
  183.5 4.6 %copy-start.2 = (f32[1024,384]{0,1:T(8,128)S(1)}, f32[1024,384]{0,1:T(8,128)}, u32[]{:S(2)}) copy-start(f32[1024,384]{0,1:T(8,128)} %get-tuple-element.795) | copy-start | bytes 4718596 | tf_op jit(solution)/shard_map/while
  183.5 4.6 %copy-start.10 = (bf16[2,1,384,128]{3,2,1,0:T(8,128)(2,1)S(1)}, bf16[2,1,384,128]{3,2,1,0:T(8,128)(2,1)}, u32[]{:S(2)}) copy-start(bf16[2,1,384,128]{3,2,1,0:T(8,128)(2,1)} %copy-done.9) | copy-start | bytes 589828 | tf_op jit(solution)/shard_map/while
  188.1 1.8 copy-start.4
  189.9 1.8 copy-start.3
  197.6 2.1 copy-start.5
  201.0 0.7 copy-start.9
  208.6 2.3 copy-start.1
  215.4 1.4 copy-start
  215.5 1.5 copy-start.6
  218.2 4.6 %copy-start.2 = (f32[1024,384]{0,1:T(8,128)S(1)}, f32[1024,384]{0,1:T(8,128)}, u32[]{:S(2)}) copy-start(f32[1024,384]{0,1:T(8,128)} %get-tuple-element.795) | copy-start | bytes 4718596 | tf_op jit(solution)/shard_map/while
  218.2 4.6 %copy-start.10 = (bf16[2,1,384,128]{3,2,1,0:T(8,128)(2,1)S(1)}, bf16[2,1,384,128]{3,2,1,0:T(8,128)(2,1)}, u32[]{:S(2)}) copy-start(bf16[2,1,384,128]{3,2,1,0:T(8,128)(2,1)} %copy-done.9) | copy-start | bytes 589828 | tf_op jit(solution)/shard_map/while
  222.8 1.7 copy-start.4
  224.5 1.8 copy-start.3
  232.3 2.1 copy-start.5
  235.6 0.7 copy-start.9
  243.2 2.3 copy-start.1
  250.1 1.4 copy-start
  250.1 1.5 copy-start.6
  252.8 4.6 %copy-start.2 = (f32[1024,384]{0,1:T(8,128)S(1)}, f32[1024,384]{0,1:T(8,128)}, u32[]{:S(2)}) copy-start(f32[1024,384]{0,1:T(8,128)} %get-tuple-element.795) | copy-start | bytes 4718596 | tf_op jit(solution)/shard_map/while
  252.8 4.6 %copy-start.10 = (bf16[2,1,384,128]{3,2,1,0:T(8,128)(2,1)S(1)}, bf16[2,1,384,128]{3,2,1,0:T(8,128)(2,1)}, u32[]{:S(2)}) copy-start(bf16[2,1,384,128]{3,2,1,0:T(8,128)(2,1)} %copy-done.9) | copy-start | bytes 589828 | tf_op jit(solution)/shard_map/while
  257.4 1.7 copy-start.4
  259.2 1.8 copy-start.3
  266.9 2.1 copy-start.5
  270.2 0.7 copy-start.9
  277.8 2.3 copy-start.1
  284.6 1.4 copy-start
  284.7 1.5 copy-start.6
  287.4 4.6 %copy-start.2 = (f32[1024,384]{0,1:T(8,128)S(1)}, f32[1024,384]{0,1:T(8,128)}, u32[]{:S(2)}) copy-start(f32[1024,384]{0,1:T(8,128)} %get-tuple-element.795) | copy-start | bytes 4718596 | tf_op jit(solution)/shard_map/while
  287.4 4.6 %copy-start.10 = (bf16[2,1,384,128]{3,2,1,0:T(8,128)(2,1)S(1)}, bf16[2,1,384,128]{3,2,1,0:T(8,128)(2,1)}, u32[]{:S(2)}) copy-start(bf16[2,1,384,128]{3,2,1,0:T(8,128)(2,1)} %copy-done.9) | copy-start | bytes 589828 | tf_op jit(solution)/shard_map/while
  292.0 1.7 copy-start.4
  293.7 23.1 %copy-start.11 = (f32[512]{0:T(512)S(1)}, f32[512]{0:T(512)}, u32[]{:S(2)}) copy-start(f32[512]{0:T(512)} %param.11) | copy-start | bytes 6148
Sparse Core Ops, SparseCore 0:
  17.7 137.4 all-gather.1
where the time goes:
time: 328 us; the launch traced here: 327 us
  waiting for transfers between devices  97.2 us (30%)
  matrix products  66.7 us (20%)
  other arithmetic  46.4 us (14%)
  local copies, waits for them, and re-layouts  40 us (12%)
  starting transfers between devices  27.4 us (8%)
  blocking collectives  21.3 us (6%)
  loops' own time  13.8 us (4%)
  between operations  13.7 us (4%)
    all_gather x1, waiting for transfers between devices, local(): farthest = lax.all_gather(coarsen(coarse_two, 4), 'seq', axis=1, tiled=True)  92.7 us
    dot_general x16, matrix products, attend(): jnp.einsum('gqk,gkd->gqd', weights_low, entry_values, preferred_element_t...  31.7 us
    reduce_sum x16, other arithmetic, attend(): denominator = denominator + jnp.sum(weights, axis=-1).reshape(rows_here)  29.2 us
    psum x1, blocking collectives, local(): summed = lax.psum(local_sum, 'head')  21.3 us
    dot_general x4, matrix products, far_scores(): jnp.einsum('qd,kd->qk', query_rows, farthest[0], preferred_element_type=j...  17.9 us
    dot_general x12, matrix products, level_scores(): jnp.einsum('gqd,gkd->gqk', grouped, windows[0], preferred_element_type=jn...  17.1 us
    ppermute x6, starting transfers between devices, from_behind(): return lax.ppermute(value, axis, pairs)  16.9 us
    another operation x1, loops' own time, local(): per_head = lax.map(one_head, jnp.arange(heads_here, dtype=jnp.int32))  13.8 us
  transfers between devices with their start and end apart: 11, of which 2 were waited for; matrix products, arithmetic and copies ran while one was open for 4% of the time, Pallas kernels for 0%

commit v1 on v0

v1 whole, which is shorter than its diff:
```python
import functools
import math

import jax
import jax.numpy as jnp
from jax import lax
from jax.experimental import pallas as pl
from jax.experimental.pallas import tpu as pltpu
from jax.sharding import PartitionSpec as P

HEADS = 32
HEAD_DIM = 128
BLK = 128
ROWS = 1024
HALF = 512
PAIR = 2 * HEAD_DIM
Y = 4
Z = 16

EPS = 1e-06
GONE = -1e30
NT = (((1,), (1,)), ((), ()))
BF = jnp.bfloat16
F32 = jnp.float32
VMEM_LIMIT = 48 * 1024 * 1024


def params():
    return pltpu.CompilerParams(vmem_limit_bytes=VMEM_LIMIT)


def cost(flops, moved, exps=0):
    return pl.CostEstimate(flops=flops, bytes_accessed=moved, transcendentals=exps)


def sds(shape, dtype):
    return jax.ShapeDtypeStruct(shape, dtype)


def prep_kernel(k_ref, v_ref, up_ref, down_ref, one_ref, two_ref, three_ref):
    rows = lax.broadcasted_iota(jnp.int32, (64, 256), 0)
    cols = lax.broadcasted_iota(jnp.int32, (64, 256), 1)
    pool = jnp.where(cols // 4 == rows, 0.25, 0.0).astype(BF)
    for which, ref in ((0, k_ref), (1, v_ref)):
        for pair in range(2):
            src = slice(pair * PAIR, (pair + 1) * PAIR)
            to = slice((2 * pair + which) * PAIR, (2 * pair + which + 1) * PAIR)
            for j in range(4):
                part = jnp.dot(pool, ref[256 * j : 256 * (j + 1), src], preferred_element_type=F32)
                one_ref[64 * j : 64 * (j + 1), to] = part.astype(BF)
            two = jnp.dot(pool, one_ref[:, to], preferred_element_type=F32).astype(BF)
            three = jnp.dot(pool[:16, :64], two, preferred_element_type=F32).astype(BF)
            two_ref[:, to] = two
            three_ref[:, to] = three
            up_ref[0:128, to] = ref[ROWS - 128 : ROWS, src]
            up_ref[128:256, to] = one_ref[128:256, to]
            down_ref[0:128, to] = ref[0:128, src]
            down_ref[128:256, to] = one_ref[0:128, to]


def prep(keys, values):
    return pl.pallas_call(
        prep_kernel,
        out_shape=(
            sds((256, 1024), BF),
            sds((256, 1024), BF),
            sds((256, 1024), BF),
            sds((64, 1024), BF),
            sds((16, 1024), BF),
        ),
        compiler_params=params(),
        cost_estimate=cost(700_000_000, 5_000_000),
    )(keys, values)


def near_kernel(
    pair, seq_size, dev_ref, temp_ref, q_ref, k_ref, v_ref,
    upk, upv, dnk, dnv, onk, onv, twok, twov, nextk, nextv,
    acc_ref, ml_ref,
):
    dev = dev_ref[0]
    c = temp_ref[2 * pair + pl.program_id(0)]
    z, y = dev // Y, dev % Y

    def gate(ok):
        return jnp.where(ok, 0.0, GONE).astype(F32)

    g_up = gate(dev >= 1)
    g_dn = gate(dev <= seq_size - 2)
    g_next = jnp.where(y < 2, gate(z >= 1), gate(z <= seq_size // Y - 2))

    lane384 = lax.broadcasted_iota(jnp.int32, (1, 384), 1)
    lane128 = lax.broadcasted_iota(jnp.int32, (128, 128), 1)
    k2 = jnp.concatenate([twok[...], nextk[...]], axis=0)
    v2 = jnp.concatenate([twov[...], nextv[...]], axis=0)
    next_first = jnp.where(y < 2, -2 * ROWS, 4 * ROWS) - 256 * 16
    token2 = lane384 * 16 - y * ROWS + jnp.where(lane384 < 256, 0, next_first)
    edge2 = jnp.where(lane384 < 256, 0.0, g_next)

    for g in range(2):
        base = g * HALF
        q = q_ref[base : base + HALF]
        if g == 0:
            k1 = jnp.concatenate([upk[128:256], onk[...]], axis=0)
            v1 = jnp.concatenate([upv[128:256], onv[...]], axis=0)
            edge1 = jnp.where(lane384 < 128, g_up, 0.0)
        else:
            k1 = jnp.concatenate([onk[...], dnk[128:256]], axis=0)
            v1 = jnp.concatenate([onv[...], dnv[128:256]], axis=0)
            edge1 = jnp.where(lane384 >= 256, g_dn, 0.0)
        inside = (token2 >= (g - 1) * HALF) & (token2 < (g + 2) * HALF)
        bias2 = jnp.where(inside, GONE, edge2)
        s1 = lax.dot_general(q, k1, NT, preferred_element_type=F32)
        s2 = lax.dot_general(q, k2, NT, preferred_element_type=F32)
        low1, low2, terms = [], [], []
        for b in range(4):
            block = 4 * g + b
            rows = slice(128 * b, 128 * (b + 1))
            if block == 0:
                k0 = jnp.concatenate([upk[0:128], k_ref[0:256]], axis=0)
                v0 = jnp.concatenate([upv[0:128], v_ref[0:256]], axis=0)
            elif block == 7:
                k0 = jnp.concatenate([k_ref[768:1024], dnk[0:128]], axis=0)
                v0 = jnp.concatenate([v_ref[768:1024], dnv[0:128]], axis=0)
            else:
                k0 = k_ref[128 * (block - 1) : 128 * (block + 2)]
                v0 = v_ref[128 * (block - 1) : 128 * (block + 2)]
            t0 = lax.dot_general(q[rows], k0, NT, preferred_element_type=F32)
            if block == 0:
                t0 = t0 + jnp.where(lane384 < 128, g_up, 0.0)
            if block == 7:
                t0 = t0 + jnp.where(lane384 >= 256, g_dn, 0.0)
            hidden = (lane384 >= 32 * b + 96) & (lane384 < 32 * b + 192)
            t1 = s1[rows] + jnp.where(hidden, GONE, edge1)
            t2 = s2[rows] + bias2
            top = jnp.maximum(
                c * jnp.max(t0, axis=1, keepdims=True),
                jnp.maximum(
                    c * jnp.max(t1, axis=1, keepdims=True) + 2.0,
                    c * jnp.max(t2, axis=1, keepdims=True) + 4.0,
                ),
            )
            w0 = jnp.exp2(c * t0 - top)
            w1 = jnp.exp2(c * t1 - (top - 2.0))
            w2 = jnp.exp2(c * t2 - (top - 4.0))
            total = (
                jnp.sum(w0, axis=1, keepdims=True)
                + jnp.sum(w1, axis=1, keepdims=True)
                + jnp.sum(w2, axis=1, keepdims=True)
            )
            low1.append(w1.astype(BF))
            low2.append(w2.astype(BF))
            terms.append(jnp.dot(w0.astype(BF), v0, preferred_element_type=F32))
            ml_ref[base + 128 * b : base + 128 * (b + 1)] = jnp.where(lane128 < 64, top, total)
        far = jnp.dot(jnp.concatenate(low1, axis=0), v1, preferred_element_type=F32)
        far = far + jnp.dot(jnp.concatenate(low2, axis=0), v2, preferred_element_type=F32)
        acc_ref[base : base + HALF] = jnp.concatenate(terms, axis=0) + far


def near(pair, seq_size, dev, temp, queries, keys, values, up, down, one, two, beyond):
    smem = pl.BlockSpec(memory_space=pltpu.SMEM)

    def own(rows):
        return pl.BlockSpec((rows, HEAD_DIM), lambda i: (0, 2 * pair + i))

    def packed(rows):
        return [
            pl.BlockSpec((rows, HEAD_DIM), lambda i: (0, 4 * pair + i)),
            pl.BlockSpec((rows, HEAD_DIM), lambda i: (0, 4 * pair + 2 + i)),
        ]

    out = pl.BlockSpec((ROWS, HEAD_DIM), lambda i: (0, i))
    return pl.pallas_call(
        functools.partial(near_kernel, pair, seq_size),
        grid=(2,),
        in_specs=[smem, smem, own(ROWS), own(ROWS), own(ROWS)]
        + packed(256) + packed(256) + packed(256) + packed(256) + packed(128),
        out_specs=(out, out),
        out_shape=(sds((ROWS, PAIR), F32), sds((ROWS, PAIR), F32)),
        compiler_params=params(),
        cost_estimate=cost(2_000_000_000, 6_000_000, 2_500_000),
    )(dev, temp, queries, keys, values, up, up, down, down, one, one, two, two, beyond, beyond)


CHUNK = 256


def far_kernel(pair, has_sum, dev_ref, temp_ref, q_ref, acc_ref, ml_ref, f0, f1, f2, f3, *rest):
    if has_sum:
        before_ref, att_ref, sum_ref = rest
    else:
        att_ref, sum_ref = rest
    dev = dev_ref[0]
    y, own_pair = dev % Y, dev // 2
    lane = lax.broadcasted_iota(jnp.int32, (1, 256), 1)
    blocks = (f0, f1, f2, f3)
    biases = []
    for k in range(4):
        src_pair = (lane // 16 * Y + (y + k) % Y) // 2
        seen = (src_pair < own_pair - 1) | (src_pair > own_pair + 1)
        biases.append(jnp.where(seen, 0.0, GONE).astype(F32))
    squares = None
    for i in range(2):
        c = temp_ref[2 * pair + i]
        cols = slice(HEAD_DIM * i, HEAD_DIM * (i + 1))
        vcols = slice(PAIR + HEAD_DIM * i, PAIR + HEAD_DIM * (i + 1))
        q = q_ref[:, cols]
        scores = [
            lax.dot_general(q, f[:, cols], NT, preferred_element_type=F32) + bias
            for f, bias in zip(blocks, biases)
        ]
        best = jnp.maximum(
            jnp.maximum(scores[0], scores[1]), jnp.maximum(scores[2], scores[3])
        )
        best = c * jnp.max(best, axis=1, keepdims=True) + 6.0
        top_near = ml_ref[:, HEAD_DIM * i : HEAD_DIM * i + 1]
        sum_near = ml_ref[:, HEAD_DIM * i + 64 : HEAD_DIM * i + 65]
        top = jnp.maximum(top_near, best)
        alpha = jnp.exp2(top_near - top)
        weights = [jnp.exp2(c * s - (top - 6.0)) for s in scores]
        total = alpha * sum_near + jnp.sum(
            (weights[0] + weights[1]) + (weights[2] + weights[3]), axis=1, keepdims=True
        )
        acc = acc_ref[:, cols] * alpha
        for w, f in zip(weights, blocks):
            acc = acc + jnp.dot(w.astype(BF), f[:, vcols], preferred_element_type=F32)
        att = acc / total
        att_ref[:, cols] = att
        squares = att * att if squares is None else squares + att * att
    for j in range(CHUNK // 128):
        rows = slice(128 * j, 128 * (j + 1))
        line = jnp.sum(jnp.transpose(squares[rows]), axis=0, keepdims=True)
        if has_sum:
            line = line + before_ref[:, rows]
        sum_ref[:, rows] = line


def far(pair, dev, temp, queries, acc, ml, columns, before):
    smem = pl.BlockSpec(memory_space=pltpu.SMEM)
    row = pl.BlockSpec((CHUNK, PAIR), lambda i: (i, 0))
    whole = pl.BlockSpec((256, 512), lambda i: (0, pair))
    part = pl.BlockSpec((256, 512), lambda i: (0, 0))
    line = pl.BlockSpec((1, CHUNK), lambda i: (0, i))
    extra = [] if before is None else [before]
    return pl.pallas_call(
        functools.partial(far_kernel, pair, before is not None),
        grid=(ROWS // CHUNK,),
        in_specs=[smem, smem, pl.BlockSpec((CHUNK, PAIR), lambda i: (i, pair)), row, row]
        + [whole, whole, part, whole] + [line] * len(extra),
        out_specs=(row, line),
        out_shape=(sds((ROWS, PAIR), F32), sds((1, ROWS), F32)),
        compiler_params=params(),
        cost_estimate=cost(1_200_000_000, 5_000_000, 2_100_000),
    )(dev, temp, queries, acc, ml, *columns, *extra)


def norm_kernel(a_ref, b_ref, sum_ref, gain_ref, out_ref):
    mean = jnp.sum(sum_ref[...], axis=0, keepdims=True) / (HEADS * HEAD_DIM)
    inverse = lax.rsqrt(mean + EPS)
    for j in range(CHUNK // 128):
        rows = slice(128 * j, 128 * (j + 1))
        tall = jnp.transpose(jnp.broadcast_to(inverse[:, rows], (128, 128)))
        for h in range(4):
            ref = a_ref if h < 2 else b_ref
            cols = slice(HEAD_DIM * (h % 2), HEAD_DIM * (h % 2 + 1))
            to = slice(HEAD_DIM * h, HEAD_DIM * (h + 1))
            out_ref[rows, to] = (ref[rows, cols] * tall * gain_ref[:, to]).astype(BF)


def norm(att_a, att_b, sums, gain):
    row = pl.BlockSpec((CHUNK, PAIR), lambda i: (i, 0))
    line = pl.BlockSpec((8, CHUNK), lambda i: (0, i))
    return pl.pallas_call(
        norm_kernel,
        grid=(ROWS // CHUNK,),
        in_specs=[row, row, line, pl.BlockSpec((1, 512), lambda i: (0, 0))],
        out_specs=pl.BlockSpec((CHUNK, 512), lambda i: (i, 0)),
        out_shape=sds((ROWS, 512), BF),
        compiler_params=params(),
        cost_estimate=cost(2_000_000, 3_000_000),
    )(att_a, att_b, sums, gain)


def fetch(value, axis, source):
    count = lax.axis_size(axis)
    return lax.ppermute(value, axis, [(source(i) % count, i) for i in range(count)])


def gathered(value, axis):
    size = lax.axis_size(axis)
    many = jnp.broadcast_to(value[None], (size,) + value.shape)
    return lax.all_to_all(many, axis, 0, 0, tiled=True)


Y_RING = [[z * Y + y for y in range(Y)] for z in range(Z)]
Z_RING = [[z * Y + y for z in range(Z)] for y in range(Y)]


def joined(value, groups):
    return lax.all_gather(value, "seq", axis_index_groups=groups, axis=0, tiled=True)


def local(queries, keys, values, head_temp, norm_gain):
    seq_size = lax.axis_size("seq")
    dev = lax.axis_index("seq").astype(jnp.int32).reshape(1)
    temp = head_temp * F32(math.log2(math.e) / math.sqrt(HEAD_DIM))
    up, down, one, two, three = prep(keys, values)

    from_up = fetch(up, "seq", lambda i: i - 1)
    from_down = fetch(down, "seq", lambda i: i + 1)
    group_two = joined(two, Y_RING)
    low_side = dev[0] % Y < 2
    other_half = jnp.where(low_side, group_two[128:], group_two[:128])
    beyond = fetch(other_half, "seq", lambda i: i - Y if i % Y < 2 else i + Y)

    column = joined(three, Z_RING)
    after = fetch(column, "seq", lambda i: i + 1)
    before = fetch(column, "seq", lambda i: i - 1)
    opposite_a = fetch(after[:, :512], "seq", lambda i: i + 1)
    opposite_b = fetch(before[:, 512:], "seq", lambda i: i - 1)

    near_args = (queries, keys, values, from_up, from_down, one, group_two, beyond)
    acc_a, ml_a = near(0, seq_size, dev, temp, *near_args)
    acc_b, ml_b = near(1, seq_size, dev, temp, *near_args)
    att_a, sum_a = far(0, dev, temp, queries, acc_a, ml_a, (column, after, opposite_a, before), None)
    att_b, sums = far(1, dev, temp, queries, acc_b, ml_b, (column, after, opposite_b, before), sum_a)
    sums = gathered(sums, "head").reshape(8, ROWS)
    return norm(att_a, att_b, sums, norm_gain.reshape(1, 512))


def solution(mesh):
    return jax.shard_map(
        local,
        mesh=mesh,
        in_specs=(P("seq", "head"), P("seq", "head"), P("seq", "head"), P("head"), P("head")),
        out_specs=P("seq", "head"),
        check_vma=False,
    )
```

time: 328 us -> 135 us (0.41)
  waiting for transfers between devices: 97.2 us -> 0.02 us
  matrix products: 66.7 us -> 0 us
  blocking collectives: 21.3 us -> 72.9 us
  other arithmetic: 46.4 us -> 0.03 us
  local copies, waits for them, and re-layouts: 40 us -> 5.1 us
  Pallas kernels: 0 us -> 33.7 us
  loops' own time: 13.8 us -> 0 us
  between operations: 13.7 us -> 0.21 us
  starting transfers between devices: 27.4 us -> 22.5 us
    all_gather x1 -> x0, waiting for transfers between devices: 92.7 us -> none  [local(): farthest = lax.all_gather(coarsen(coarse_two, 4), 'seq', axis=1, tiled=True)]
    dot_general x32 -> x0, matrix products: 66.7 us -> none  [the longest x16 31.7 us: attend(): jnp.einsum('gqk,gkd->gqd', weights_low, entry_values, preferred_element_t...]
    all_gather x0 -> x2, blocking collectives: none -> 61.2 us  [joined(): lax.all_gather(value, 'seq', axis_index_groups=groups, axis=0, tiled=True)]
    reduce_sum x20 -> x0, other arithmetic: 37.3 us -> none  [the longest x16 29.2 us: attend(): denominator = denominator + jnp.sum(weights, axis=-1).reshape(rows_here)]
    pallas_call x0 -> x6, Pallas kernels: none -> 33.7 us  [the longest x2 15 us: near(): pl.pallas_call(functools.partial(near_kernel, pair, seq_size), grid=(2,),...]
    psum x1 -> x0, blocking collectives: 21.3 us -> none  [local(): summed = lax.psum(local_sum, 'head')]
    dynamic_slice x24 -> x0, local copies, waits for them, and re-layouts: 18.1 us -> none  [the longest x4 4.71 us: level_scores(): lax.dynamic_slice_in_dim(extended, start_entry, (groups + 2) * BLK, 1)]
    another operation x1 -> x0, loops' own time: 13.8 us -> none  [local(): per_head = lax.map(one_head, jnp.arange(heads_here, dtype=jnp.int32))]
  transfers between devices with their start and end apart: 11 -> 7, of which waited for: 2 -> 0; matrix products, arithmetic and copies ran while one was open for 4% -> 1% of each run, Pallas kernels for 0% -> 17%
where the time goes in v1:
time: 135 us; the launch traced here: 134 us
  blocking collectives  72.9 us (54%)
  Pallas kernels  33.7 us (25%)
  starting transfers between devices  22.5 us (17%)
  local copies, waits for them, and re-layouts  5.1 us (4%)
    all_gather x2, blocking collectives, joined(): lax.all_gather(value, 'seq', axis_index_groups=groups, axis=0, tiled=True)  61.2 us
    ppermute x7, starting transfers between devices, fetch(): lax.ppermute(value, axis, [(source(i) % count, i) for i in range(count)])  22.5 us
    pallas_call x2, Pallas kernels, near(): pl.pallas_call(functools.partial(near_kernel, pair, seq_size), grid=(2,),...  15 us
    pallas_call x2, Pallas kernels, far(): pl.pallas_call(functools.partial(far_kernel, pair, before is not None), g...  14.4 us
    all_to_all x1, blocking collectives, gathered(): return lax.all_to_all(many, axis, 0, 0, tiled=True)  11.7 us
    unnamed x11, local copies, waits for them, and re-layouts  3.14 us
  transfers between devices with their start and end apart: 7, of which 0 were waited for; matrix products, arithmetic and copies ran while one was open for 1% of the time, Pallas kernels for 17%

profile of v1, /device:TPU:1, one launch (start us, length us, event | category | flops | bytes accessed | tf_op | source)
XLA Modules:
  0.0 134.4 jit_solution(12017542391349765393)
XLA Ops:
  0.0 0.0 copy-start.1
  0.0 1.2 copy-done.1
  1.2 0.0 copy-start.2
  1.2 1.2 copy-done.2
  2.5 2.4 %shard_map.55 = (bf16[256,1024]{1,0:T(8,128)(2,1)}, bf16[256,1024]{1,0:T(8,128)(2,1)}, bf16[256,1024]{1,0:T(8,128)(2,1)S(1)}, bf16[64,1024]{1,0:T(8,128)(2,1)S(1)}, bf16[16,1024]{1,0:T(8,128)(2,1)S(1)}) custom-call(bf16[1024,512]{1,0:T(8,128)(2,1)S(1)} %copy-done.1, bf16[1024,512]{1,0:T(8,128)(2,1)S(1)} %copy-done.2), custom_call_target="tpu_custom_call" | custom-call | flops 700000000 | bytes 5000000 | tf_op jit(solution)/shard_map/pallas_call | solution.py:62
  4.8 34.6 %all_gather.7.f0 = bf16[256,1024]{1,0:T(8,128)(2,1)} all-gather(bf16[16,1024]{1,0:T(8,128)(2,1)S(1)} %get-tuple-element.24), channel_id=1, replica_groups={{0,32,64,96,128,160,192,224,256,288,320,352,384,416,448,480},{8,40,72,1..., dimensions={0}, use_global_device_ids=true | all-gather | bytes 557056 | tf_op jit(solution)/shard_map/all_gather | solution.py:300
  39.4 4.1 %collective-permute-start.3 = (bf16[256,1024]{1,0:T(8,128)(2,1)}, bf16[256,1024]{1,0:T(8,128)(2,1)}, u32[]{:S(2)}, u32[]{:S(2)}) collective-permute-start(bf16[256,1024]{1,0:T(8,128)(2,1)} %all_gather.7.f0), channel_id=1, source_target_pairs={{8,0},{16,8},{24,16},{32,24},{40,32},{48,40},{56,48},{64,56},{72,6... | collective-permute-start | bytes 1572872 | tf_op jit(solution)/shard_map/ppermute | solution.py:286
  43.5 1.9 %collective-permute-start.5 = (bf16[256,1024]{1,0:T(8,128)(2,1)}, bf16[256,1024]{1,0:T(8,128)(2,1)}, u32[]{:S(2)}, u32[]{:S(2)}) collective-permute-start(bf16[256,1024]{1,0:T(8,128)(2,1)} %all_gather.7.f0), channel_id=1, source_target_pairs={{504,0},{0,8},{8,16},{16,24},{24,32},{32,40},{40,48},{48,56},{56,6... | collective-permute-start | bytes 1572872 | tf_op jit(solution)/shard_map/ppermute | solution.py:286
  45.4 2.5 %collective-permute-start = (bf16[256,1024]{1,0:T(8,128)(2,1)}, bf16[256,1024]{1,0:T(8,128)(2,1)S(1)}, u32[]{:S(2)}, u32[]{:S(2)}) collective-permute-start(bf16[256,1024]{1,0:T(8,128)(2,1)} %get-tuple-element.18), channel_id=1, source_target_pairs={{504,0},{0,8},{8,16},{16,24},{24,32},{32,40},{40,48},{48,56},{56,6... | collective-permute-start | bytes 1572872 | tf_op jit(solution)/shard_map/ppermute | solution.py:286
  47.9 6.1 %collective-permute-start.1 = (bf16[256,1024]{1,0:T(8,128)(2,1)}, bf16[256,1024]{1,0:T(8,128)(2,1)S(1)}, u32[]{:S(2)}, u32[]{:S(2)}) collective-permute-start(bf16[256,1024]{1,0:T(8,128)(2,1)} %get-tuple-element.19), channel_id=1, source_target_pairs={{8,0},{16,8},{24,16},{32,24},{40,32},{48,40},{56,48},{64,56},{72,6... | collective-permute-start | bytes 1572872 | tf_op jit(solution)/shard_map/ppermute | solution.py:286
  54.0 0.0 copy-start.4
  54.0 26.7 %all_gather.6.twok.twov = bf16[256,1024]{1,0:T(8,128)(2,1)S(1)} all-gather(bf16[64,1024]{1,0:T(8,128)(2,1)S(1)} %get-tuple-element.21), channel_id=1, replica_groups={{0,8,16,24},{32,40,48,56},{64,72,80,88},{96,104,112,120},{128,136,144,1..., dimensions={0}, use_global_device_ids=true | all-gather | bytes 655360 | tf_op jit(solution)/shard_map/all_gather | solution.py:300
  80.7 0.0 copy-start
  80.8 2.6 %collective-permute-start.2 = (bf16[128,1024]{1,0:T(8,128)(2,1)S(1)}, bf16[128,1024]{1,0:T(8,128)(2,1)S(1)}, u32[]{:S(2)}, u32[]{:S(2)}) collective-permute-start(bf16[128,1024]{1,0:T(8,128)(2,1)S(1)} %slice_select_fusion), channel_id=1, source_target_pairs={{480,0},{488,8},{48,16},{56,24},{0,32},{8,40},{80,48},{88,56},{32,... | collective-permute-start | bytes 786440 | tf_op jit(solution)/shard_map/ppermute | solution.py:286
  83.3 0.0 copy-done.4
  83.3 0.0 collective-permute-done.3.f1
  83.4 1.0 slice.18
  84.3 2.2 %collective-permute-start.4 = (bf16[256,512]{1,0:T(8,128)(2,1)S(1)}, bf16[256,512]{1,0:T(8,128)(2,1)S(1)}, u32[]{:S(2)}, u32[]{:S(2)}) collective-permute-start(bf16[256,512]{1,0:T(8,128)(2,1)S(1)} %slice.18), channel_id=1, source_target_pairs={{8,0},{16,8},{24,16},{32,24},{40,32},{48,40},{56,48},{64,56},{72,6... | collective-permute-start | bytes 786440 | tf_op jit(solution)/shard_map/ppermute | solution.py:286
  86.6 0.0 collective-permute-done.5.f3
  86.6 1.0 slice.19
  87.6 3.0 %collective-permute-start.6 = (bf16[256,512]{1,0:T(8,128)(2,1)S(1)}, bf16[256,512]{1,0:T(8,128)(2,1)S(1)}, u32[]{:S(2)}, u32[]{:S(2)}) collective-permute-start(bf16[256,512]{1,0:T(8,128)(2,1)S(1)} %slice.19), channel_id=1, source_target_pairs={{504,0},{0,8},{8,16},{16,24},{24,32},{32,40},{40,48},{48,56},{56,6... | collective-permute-start | bytes 786440 | tf_op jit(solution)/shard_map/ppermute | solution.py:286
  90.6 0.0 collective-permute-done.2.nextk.nextv
  90.6 0.0 collective-permute-done.upk.upv
  90.6 0.0 collective-permute-done.1.dnk.dnv
  90.6 0.0 copy-done
  90.7 7.5 %shard_map.58 = (f32[1024,256]{1,0:T(8,128)S(1)}, f32[1024,256]{1,0:T(8,128)S(1)}) custom-call(s32[1]{0:T(128)} %bitcast.dev_ref, f32[4]{0:T(128)S(1)} %broadcast_multiply_fusion.temp_ref, bf16[1024,512]{1,0:T(8,128)(2,1)S(1)} %copy-done, bf16[1024,512]{1,0:T(8,128)(2,1)} %k_ref.5, bf16[1024,512]{1,0:T(8,128)(2,1)} %v_ref.5, ...), custom_call_target="tpu_custom_call" | custom-call | flops 2000000000 | bytes 6000000 | tf_op jit(solution)/shard_map/pallas_call | solution.py:173
  98.2 7.5 %shard_map.56 = (f32[1024,256]{1,0:T(8,128)S(1)}, f32[1024,256]{1,0:T(8,128)S(1)}) custom-call(s32[1]{0:T(128)} %bitcast.dev_ref, f32[4]{0:T(128)S(1)} %broadcast_multiply_fusion.temp_ref, bf16[1024,512]{1,0:T(8,128)(2,1)S(1)} %copy-done, bf16[1024,512]{1,0:T(8,128)(2,1)} %k_ref.5, bf16[1024,512]{1,0:T(8,128)(2,1)} %v_ref.5, ...), custom_call_target="tpu_custom_call" | custom-call | flops 2000000000 | bytes 6000000 | tf_op jit(solution)/shard_map/pallas_call | solution.py:173
  105.7 0.0 collective-permute-done.4.f2
  105.7 7.3 %shard_map.57 = (f32[1024,256]{1,0:T(8,128)S(1)}, f32[1,1024]{1,0:T(1,128)S(1)}) custom-call(s32[1]{0:T(128)} %bitcast.dev_ref, f32[4]{0:T(128)S(1)} %broadcast_multiply_fusion.temp_ref, bf16[1024,512]{1,0:T(8,128)(2,1)S(1)} %copy-done, f32[1024,256]{1,0:T(8,128)S(1)} %get-tuple-element.22.acc_ref, f32[1024,256]{1,0:T(8,128)S(1)} %get-tuple-element.23.ml_ref, ...), custom_call_target="tpu_custom_call" | custom-call | flops 1200000000 | bytes 5000000 | tf_op jit(solution)/shard_map/pallas_call | solution.py:245
  113.1 0.0 collective-permute-done.6.f2
  113.1 7.1 %shard_map.59 = (f32[1024,256]{1,0:T(8,128)S(1)}, f32[1,1024]{1,0:T(1,128)S(1)}) custom-call(s32[1]{0:T(128)} %bitcast.dev_ref, f32[4]{0:T(128)S(1)} %broadcast_multiply_fusion.temp_ref, bf16[1024,512]{1,0:T(8,128)(2,1)S(1)} %copy-done, f32[1024,256]{1,0:T(8,128)S(1)} %get-tuple-element.26.acc_ref, f32[1024,256]{1,0:T(8,128)S(1)} %get-tuple-element.27.ml_ref, ...), custom_call_target="tpu_custom_call" | custom-call | flops 1200000000 | bytes 5000000 | tf_op jit(solution)/shard_map/pallas_call | solution.py:245
  120.2 11.7 %all_to_all.5 = f32[8,1,1024]{2,1,0:T(1,128)S(1)} all-to-all(f32[8,1,1024]{2,1,0:T(1,128)S(1)} %broadcast_in_dim.9), channel_id=1, replica_groups=mesh['seq'=64,'head'=8] {'head'}, dimensions={0} | all-to-all | bytes 65536 | tf_op jit(solution)/shard_map/all_to_all | solution.py:292
  131.9 0.0 copy-start.3
  131.9 0.7 copy-done.3
  132.5 1.9 %shard_map.60 = bf16[1024,512]{1,0:T(8,128)(2,1)} custom-call(f32[1024,256]{1,0:T(8,128)S(1)} %get-tuple-element.25.a_ref, f32[1024,256]{1,0:T(8,128)S(1)} %get-tuple-element.29.b_ref, f32[8,1024]{1,0:T(8,128)S(1)} %bitcast.6, f32[1,512]{1,0:T(1,128)S(1)} %bitcast.8), custom_call_target="tpu_custom_call" | custom-call | flops 2000000 | bytes 3000000 | tf_op jit(solution)/shard_map/pallas_call | solution.py:273
  (4 shorter events, 0.1 us)
Async XLA Ops:
  0.0 1.2 copy-start.1
  1.2 1.2 copy-start.2
  39.4 44.0 %collective-permute-start.3 = (bf16[256,1024]{1,0:T(8,128)(2,1)}, bf16[256,1024]{1,0:T(8,128)(2,1)}, u32[]{:S(2)}, u32[]{:S(2)}) collective-permute-start(bf16[256,1024]{1,0:T(8,128)(2,1)} %all_gather.7.f0), channel_id=1, source_target_pairs={{8,0},{16,8},{24,16},{32,24},{40,32},{48,40},{56,48},{64,56},{72,6... | collective-permute-start | bytes 1572872 | tf_op jit(solution)/shard_map/ppermute | solution.py:286
  43.5 43.1 %collective-permute-start.5 = (bf16[256,1024]{1,0:T(8,128)(2,1)}, bf16[256,1024]{1,0:T(8,128)(2,1)}, u32[]{:S(2)}, u32[]{:S(2)}) collective-permute-start(bf16[256,1024]{1,0:T(8,128)(2,1)} %all_gather.7.f0), channel_id=1, source_target_pairs={{504,0},{0,8},{8,16},{16,24},{24,32},{32,40},{40,48},{48,56},{56,6... | collective-permute-start | bytes 1572872 | tf_op jit(solution)/shard_map/ppermute | solution.py:286
  45.4 45.2 %collective-permute-start = (bf16[256,1024]{1,0:T(8,128)(2,1)}, bf16[256,1024]{1,0:T(8,128)(2,1)S(1)}, u32[]{:S(2)}, u32[]{:S(2)}) collective-permute-start(bf16[256,1024]{1,0:T(8,128)(2,1)} %get-tuple-element.18), channel_id=1, source_target_pairs={{504,0},{0,8},{8,16},{16,24},{24,32},{32,40},{40,48},{48,56},{56,6... | collective-permute-start | bytes 1572872 | tf_op jit(solution)/shard_map/ppermute | solution.py:286
  47.9 42.7 %collective-permute-start.1 = (bf16[256,1024]{1,0:T(8,128)(2,1)}, bf16[256,1024]{1,0:T(8,128)(2,1)S(1)}, u32[]{:S(2)}, u32[]{:S(2)}) collective-permute-start(bf16[256,1024]{1,0:T(8,128)(2,1)} %get-tuple-element.19), channel_id=1, source_target_pairs={{8,0},{16,8},{24,16},{32,24},{40,32},{48,40},{56,48},{64,56},{72,6... | collective-permute-start | bytes 1572872 | tf_op jit(solution)/shard_map/ppermute | solution.py:286
  54.0 29.3 %copy-start.4 = (f32[4]{0:T(128)S(1)}, f32[4]{0:T(128)}, u32[]{:S(2)}) copy-start(f32[4]{0:T(128)} %param.8) | copy-start | bytes 52
  80.7 9.9 %copy-start = (bf16[1024,512]{1,0:T(8,128)(2,1)S(1)}, bf16[1024,512]{1,0:T(8,128)(2,1)}, u32[]{:S(2)}) copy-start(bf16[1024,512]{1,0:T(8,128)(2,1)} %q_ref.7) | copy-start | bytes 3145732
  80.8 9.9 %collective-permute-start.2 = (bf16[128,1024]{1,0:T(8,128)(2,1)S(1)}, bf16[128,1024]{1,0:T(8,128)(2,1)S(1)}, u32[]{:S(2)}, u32[]{:S(2)}) collective-permute-start(bf16[128,1024]{1,0:T(8,128)(2,1)S(1)} %slice_select_fusion), channel_id=1, source_target_pairs={{480,0},{488,8},{48,16},{56,24},{0,32},{8,40},{80,48},{88,56},{32,... | collective-permute-start | bytes 786440 | tf_op jit(solution)/shard_map/ppermute | solution.py:286
  84.3 21.4 %collective-permute-start.4 = (bf16[256,512]{1,0:T(8,128)(2,1)S(1)}, bf16[256,512]{1,0:T(8,128)(2,1)S(1)}, u32[]{:S(2)}, u32[]{:S(2)}) collective-permute-start(bf16[256,512]{1,0:T(8,128)(2,1)S(1)} %slice.18), channel_id=1, source_target_pairs={{8,0},{16,8},{24,16},{32,24},{40,32},{48,40},{56,48},{64,56},{72,6... | collective-permute-start | bytes 786440 | tf_op jit(solution)/shard_map/ppermute | solution.py:286
  87.6 25.5 %collective-permute-start.6 = (bf16[256,512]{1,0:T(8,128)(2,1)S(1)}, bf16[256,512]{1,0:T(8,128)(2,1)S(1)}, u32[]{:S(2)}, u32[]{:S(2)}) collective-permute-start(bf16[256,512]{1,0:T(8,128)(2,1)S(1)} %slice.19), channel_id=1, source_target_pairs={{504,0},{0,8},{8,16},{16,24},{24,32},{32,40},{40,48},{48,56},{56,6... | collective-permute-start | bytes 786440 | tf_op jit(solution)/shard_map/ppermute | solution.py:286
  131.9 0.7 copy-start.3

commit v2 on v1

--- a/solution.py
+++ b/solution.py
@@ -76,7 +76,7 @@
 def near_kernel(
     pair, seq_size, dev_ref, temp_ref, q_ref, k_ref, v_ref,
     upk, upv, dnk, dnv, onk, onv, twok, twov, nextk, nextv,
-    acc_ref, ml_ref,
+    acc_ref, ml_ref, sa, sb, pa, pb,
 ):
     dev = dev_ref[0]
     c = temp_ref[2 * pair + pl.program_id(0)]
@@ -91,70 +91,77 @@
 
     lane384 = lax.broadcasted_iota(jnp.int32, (1, 384), 1)
     lane128 = lax.broadcasted_iota(jnp.int32, (128, 128), 1)
-    k2 = jnp.concatenate([twok[...], nextk[...]], axis=0)
-    v2 = jnp.concatenate([twov[...], nextv[...]], axis=0)
+    ones = jnp.ones((1152, 128), BF)
     next_first = jnp.where(y < 2, -2 * ROWS, 4 * ROWS) - 256 * 16
     token2 = lane384 * 16 - y * ROWS + jnp.where(lane384 < 256, 0, next_first)
     edge2 = jnp.where(lane384 < 256, 0.0, g_next)
 
-    for g in range(2):
-        base = g * HALF
-        q = q_ref[base : base + HALF]
+    def window(b, own_ref, up_ref, dn_ref, one_ref, two_ref, next_ref):
+        if b == 0:
+            fine = [up_ref[0:128], own_ref[0:256]]
+        elif b == 7:
+            fine = [own_ref[768:1024], dn_ref[0:128]]
+        else:
+            fine = [own_ref[128 * (b - 1) : 128 * (b + 2)]]
+        if b < 4:
+            first = [up_ref[128:256], one_ref[...]]
+        else:
+            first = [one_ref[...], dn_ref[128:256]]
+        return jnp.concatenate(fine + first + [two_ref[...], next_ref[...]], axis=0)
+
+    def score(b):
+        keys = window(b, k_ref, upk, dnk, onk, twok, nextk)
+        scores = lax.dot_general(
+            q_ref[128 * b : 128 * (b + 1)], keys, NT, preferred_element_type=F32
+        )
+        (sa, sb)[b % 2][...] = scores
+
+    def bias_of(b):
+        g = b // 4
+        fine = None
+        if b == 0:
+            fine = jnp.where(lane384 < 128, g_up, 0.0)
+        if b == 7:
+            fine = jnp.where(lane384 >= 256, g_dn, 0.0)
         if g == 0:
-            k1 = jnp.concatenate([upk[128:256], onk[...]], axis=0)
-            v1 = jnp.concatenate([upv[128:256], onv[...]], axis=0)
             edge1 = jnp.where(lane384 < 128, g_up, 0.0)
         else:
-            k1 = jnp.concatenate([onk[...], dnk[128:256]], axis=0)
-            v1 = jnp.concatenate([onv[...], dnv[128:256]], axis=0)
             edge1 = jnp.where(lane384 >= 256, g_dn, 0.0)
+        start = 32 * (b % 4) + 96
+        hidden = (lane384 >= start) & (lane384 < start + 96)
         inside = (token2 >= (g - 1) * HALF) & (token2 < (g + 2) * HALF)
-        bias2 = jnp.where(inside, GONE, edge2)
-        s1 = lax.dot_general(q, k1, NT, preferred_element_type=F32)
-        s2 = lax.dot_general(q, k2, NT, preferred_element_type=F32)
-        low1, low2, terms = [], [], []
-        for b in range(4):
-            block = 4 * g + b
-            rows = slice(128 * b, 128 * (b + 1))
-            if block == 0:
-                k0 = jnp.concatenate([upk[0:128], k_ref[0:256]], axis=0)
-                v0 = jnp.concatenate([upv[0:128], v_ref[0:256]], axis=0)
-            elif block == 7:
-                k0 = jnp.concatenate([k_ref[768:1024], dnk[0:128]], axis=0)
-                v0 = jnp.concatenate([v_ref[768:1024], dnv[0:128]], axis=0)
-            else:
-                k0 = k_ref[128 * (block - 1) : 128 * (block + 2)]
-                v0 = v_ref[128 * (block - 1) : 128 * (block + 2)]
-            t0 = lax.dot_general(q[rows], k0, NT, preferred_element_type=F32)
-            if block == 0:
-                t0 = t0 + jnp.where(lane384 < 128, g_up, 0.0)
-            if block == 7:
-                t0 = t0 + jnp.where(lane384 >= 256, g_dn, 0.0)
-            hidden = (lane384 >= 32 * b + 96) & (lane384 < 32 * b + 192)
-            t1 = s1[rows] + jnp.where(hidden, GONE, edge1)
-            t2 = s2[rows] + bias2
-            top = jnp.maximum(
-                c * jnp.max(t0, axis=1, keepdims=True),
-                jnp.maximum(
-                    c * jnp.max(t1, axis=1, keepdims=True) + 2.0,
-                    c * jnp.max(t2, axis=1, keepdims=True) + 4.0,
-                ),
+        first = jnp.where(hidden, GONE, edge1) + 2.0 / c
+        second = jnp.where(inside, GONE, edge2) + 4.0 / c
+        return fine, first, second
+
+    score(0)
+    for b in range(8):
+        if b < 7:
+            score(b + 1)
+        s_ref, p_ref = (sa, sb)[b % 2], (pa, pb)[b % 2]
+        fine, first, second = bias_of(b)
+        for r in range(8):
+            rows = slice(16 * r, 16 * (r + 1))
+            parts = []
+            for j in range(9):
+                t = s_ref[rows, 128 * j : 128 * (j + 1)]
+                bias = (fine, first, second)[j // 3]
+                if bias is not None:
+                    t = t + bias[:, 128 * (j % 3) : 128 * (j % 3 + 1)]
+                parts.append(t)
+            top = jnp.max(functools.reduce(jnp.maximum, parts), axis=1, keepdims=True)
+            for j, t in enumerate(parts):
+                p_ref[rows, 128 * j : 128 * (j + 1)] = jnp.exp2((t - top) * c).astype(BF)
+            ml_ref[128 * b + 16 * r : 128 * b + 16 * (r + 1)] = jnp.broadcast_to(
+                top * c, (16, 128)
             )
-            w0 = jnp.exp2(c * t0 - top)
-            w1 = jnp.exp2(c * t1 - (top - 2.0))
-            w2 = jnp.exp2(c * t2 - (top - 4.0))
-            total = (
-                jnp.sum(w0, axis=1, keepdims=True)
-                + jnp.sum(w1, axis=1, keepdims=True)
-                + jnp.sum(w2, axis=1, keepdims=True)
-            )
-            low1.append(w1.astype(BF))
-            low2.append(w2.astype(BF))
-            terms.append(jnp.dot(w0.astype(BF), v0, preferred_element_type=F32))
-            ml_ref[base + 128 * b : base + 128 * (b + 1)] = jnp.where(lane128 < 64, top, total)
-        far = jnp.dot(jnp.concatenate(low1, axis=0), v1, preferred_element_type=F32)
-        far = far + jnp.dot(jnp.concatenate(low2, axis=0), v2, preferred_element_type=F32)
-        acc_ref[base : base + HALF] = jnp.concatenate(terms, axis=0) + far
+        vals = window(b, v_ref, upv, dnv, onv, twov, nextv)
+        both = jnp.dot(
+            p_ref[...], jnp.concatenate([vals, ones], axis=1), preferred_element_type=F32
+        )
+        rows = slice(128 * b, 128 * (b + 1))
+        acc_ref[rows] = both[:, :128]
+        ml_ref[rows] = jnp.where(lane128 < 64, ml_ref[rows], both[:, 128:])
 
 
 def near(pair, seq_size, dev, temp, queries, keys, values, up, down, one, two, beyond):
@@ -177,6 +184,7 @@
         + packed(256) + packed(256) + packed(256) + packed(256) + packed(128),
         out_specs=(out, out),
         out_shape=(sds((ROWS, PAIR), F32), sds((ROWS, PAIR), F32)),
+        scratch_shapes=[pltpu.VMEM((128, 1152), F32)] * 2 + [pltpu.VMEM((128, 1152), BF)] * 2,
         compiler_params=params(),
         cost_estimate=cost(2_000_000_000, 6_000_000, 2_500_000),
     )(dev, temp, queries, keys, values, up, up, down, down, one, one, two, two, beyond, beyond)
@@ -187,9 +195,9 @@
 
 def far_kernel(pair, has_sum, dev_ref, temp_ref, q_ref, acc_ref, ml_ref, f0, f1, f2, f3, *rest):
     if has_sum:
-        before_ref, att_ref, sum_ref = rest
+        before_ref, att_ref, sum_ref, sa, sb, pa, pb, a_ref = rest
     else:
-        att_ref, sum_ref = rest
+        att_ref, sum_ref, sa, sb, pa, pb, a_ref = rest
     dev = dev_ref[0]
     y, own_pair = dev % Y, dev // 2
     lane = lax.broadcasted_iota(jnp.int32, (1, 256), 1)
@@ -199,32 +207,40 @@
         src_pair = (lane // 16 * Y + (y + k) % Y) // 2
         seen = (src_pair < own_pair - 1) | (src_pair > own_pair + 1)
         biases.append(jnp.where(seen, 0.0, GONE).astype(F32))
+    bias = jnp.concatenate(biases, axis=1)
+    ones = jnp.ones((1024, 128), BF)
+    for i in range(2):
+        cols = slice(HEAD_DIM * i, HEAD_DIM * (i + 1))
+        keys = jnp.concatenate([f[:, cols] for f in blocks], axis=0)
+        (sa, sb)[i][...] = lax.dot_general(
+            q_ref[:, cols], keys, NT, preferred_element_type=F32
+        )
     squares = None
     for i in range(2):
         c = temp_ref[2 * pair + i]
         cols = slice(HEAD_DIM * i, HEAD_DIM * (i + 1))
         vcols = slice(PAIR + HEAD_DIM * i, PAIR + HEAD_DIM * (i + 1))
-        q = q_ref[:, cols]
-        scores = [
-            lax.dot_general(q, f[:, cols], NT, preferred_element_type=F32) + bias
-            for f, bias in zip(blocks, biases)
-        ]
-        best = jnp.maximum(
-            jnp.maximum(scores[0], scores[1]), jnp.maximum(scores[2], scores[3])
+        s_ref, p_ref = (sa, sb)[i], (pa, pb)[i]
+        shifted = bias + 6.0 / c
+        for r in range(CHUNK // 16):
+            rows = slice(16 * r, 16 * (r + 1))
+            parts = [
+                s_ref[rows, 128 * j : 128 * (j + 1)] + shifted[:, 128 * j : 128 * (j + 1)]
+                for j in range(8)
+            ]
+            best = jnp.max(functools.reduce(jnp.maximum, parts), axis=1, keepdims=True)
+            top_near = ml_ref[rows, HEAD_DIM * i : HEAD_DIM * i + 1]
+            top = jnp.maximum(top_near, c * best)
+            for j, t in enumerate(parts):
+                p_ref[rows, 128 * j : 128 * (j + 1)] = jnp.exp2(c * t - top).astype(BF)
+            a_ref[rows] = jnp.broadcast_to(jnp.exp2(top_near - top), (16, 128))
+        vals = jnp.concatenate([f[:, vcols] for f in blocks], axis=0)
+        both = jnp.dot(
+            p_ref[...], jnp.concatenate([vals, ones], axis=1), preferred_element_type=F32
         )
-        best = c * jnp.max(best, axis=1, keepdims=True) + 6.0
-        top_near = ml_ref[:, HEAD_DIM * i : HEAD_DIM * i + 1]
-        sum_near = ml_ref[:, HEAD_DIM * i + 64 : HEAD_DIM * i + 65]
-        top = jnp.maximum(top_near, best)
-        alpha = jnp.exp2(top_near - top)
-        weights = [jnp.exp2(c * s - (top - 6.0)) for s in scores]
-        total = alpha * sum_near + jnp.sum(
-            (weights[0] + weights[1]) + (weights[2] + weights[3]), axis=1, keepdims=True
-        )
-        acc = acc_ref[:, cols] * alpha
-        for w, f in zip(weights, blocks):
-            acc = acc + jnp.dot(w.astype(BF), f[:, vcols], preferred_element_type=F32)
-        att = acc / total
+        alpha = a_ref[...]
+        total = alpha * ml_ref[:, HEAD_DIM * i + 64 : HEAD_DIM * i + 65] + both[:, 128:]
+        att = (acc_ref[:, cols] * alpha + both[:, :128]) / total
         att_ref[:, cols] = att
         squares = att * att if squares is None else squares + att * att
     for j in range(CHUNK // 128):
@@ -249,6 +265,9 @@
         + [whole, whole, part, whole] + [line] * len(extra),
         out_specs=(row, line),
         out_shape=(sds((ROWS, PAIR), F32), sds((1, ROWS), F32)),
+        scratch_shapes=[pltpu.VMEM((CHUNK, 1024), F32)] * 2
+        + [pltpu.VMEM((CHUNK, 1024), BF)] * 2
+        + [pltpu.VMEM((CHUNK, 128), F32)],
         compiler_params=params(),
         cost_estimate=cost(1_200_000_000, 5_000_000, 2_100_000),
     )(dev, temp, queries, acc, ml, *columns, *extra)
@@ -313,6 +332,7 @@
     other_half = jnp.where(low_side, group_two[128:], group_two[:128])
     beyond = fetch(other_half, "seq", lambda i: i - Y if i % Y < 2 else i + Y)
 
+    three, beyond = lax.optimization_barrier((three, beyond))
     column = joined(three, Z_RING)
     after = fetch(column, "seq", lambda i: i + 1)
     before = fetch(column, "seq", lambda i: i - 1)

time: 135 us -> 129 us (0.956)
  blocking collectives: 72.9 us -> 58.5 us
  waiting for transfers between devices: 0.02 us -> 13.1 us
  Pallas kernels: 33.7 us -> 26.2 us
  starting transfers between devices: 22.5 us -> 27.7 us
  local copies, waits for them, and re-layouts: 5.1 us -> 3.2 us
    all_gather x2, blocking collectives: 61.2 us -> 34.7 us  [joined(): lax.all_gather(value, 'seq', axis_index_groups=groups, axis=0, tiled=True)]
    ppermute x7, waiting for transfers between devices: 0.02 us -> 13.1 us  [fetch(): lax.ppermute(value, axis, [(source(i) % count, i) for i in range(count)])]
    all_to_all x1, blocking collectives: 11.7 us -> 23.8 us  [gathered(): return lax.all_to_all(many, axis, 0, 0, tiled=True)]
    ppermute x7, starting transfers between devices: 22.5 us -> 27.7 us  [fetch(): lax.ppermute(value, axis, [(source(i) % count, i) for i in range(count)])]
    pallas_call x2, Pallas kernels: 15 us -> 10.7 us  [near(): pl.pallas_call(functools.partial(near_kernel, pair, seq_size), grid=(2,),...]
    pallas_call x2, Pallas kernels: 14.4 us -> 12.1 us  [far(): pl.pallas_call(functools.partial(far_kernel, pair, before is not None), g...]
  transfers between devices with their start and end apart: 7 -> 7, of which waited for: 0 -> 3; matrix products, arithmetic and copies ran while one was open for 1% -> 0% of each run, Pallas kernels for 17% -> 13%
where the time goes in v2:
time: 129 us
  blocking collectives  58.5 us (45%)
  starting transfers between devices  27.7 us (21%)
  Pallas kernels  26.2 us (20%)
  waiting for transfers between devices  13.1 us (10%)
  local copies, waits for them, and re-layouts  3.2 us (2%)
    all_gather x2, blocking collectives, joined(): lax.all_gather(value, 'seq', axis_index_groups=groups, axis=0, tiled=True)  34.7 us
    ppermute x7, starting transfers between devices, fetch(): lax.ppermute(value, axis, [(source(i) % count, i) for i in range(count)])  27.7 us
    all_to_all x1, blocking collectives, gathered(): return lax.all_to_all(many, axis, 0, 0, tiled=True)  23.8 us
    ppermute x7, waiting for transfers between devices, fetch(): lax.ppermute(value, axis, [(source(i) % count, i) for i in range(count)])  13.1 us
    pallas_call x2, Pallas kernels, far(): pl.pallas_call(functools.partial(far_kernel, pair, before is not None), g...  12.1 us
    pallas_call x2, Pallas kernels, near(): pl.pallas_call(functools.partial(near_kernel, pair, seq_size), grid=(2,),...  10.7 us
    unnamed x11, local copies, waits for them, and re-layouts  3.14 us
  transfers between devices with their start and end apart: 7, of which 3 were waited for; matrix products, arithmetic and copies ran while one was open for 0% of the time, Pallas kernels for 13%

profile of v2, /device:TPU:1, one launch (start us, length us, event | category | flops | bytes accessed | tf_op | source)
XLA Modules:
  0.0 128.9 jit_solution(6528263517186506970)
XLA Ops:
  0.0 0.0 copy-start.1
  0.0 1.2 copy-done.1
  1.2 0.0 copy-start.2
  1.2 1.2 copy-done.2
  2.5 1.5 %shard_map.55 = (bf16[256,1024]{1,0:T(8,128)(2,1)S(1)}, bf16[256,1024]{1,0:T(8,128)(2,1)S(1)}, bf16[256,1024]{1,0:T(8,128)(2,1)S(1)}, bf16[64,1024]{1,0:T(8,128)(2,1)S(1)}, bf16[16,1024]{1,0:T(8,128)(2,1)S(1)}) custom-call(bf16[1024,512]{1,0:T(8,128)(2,1)S(1)} %copy-done.1, bf16[1024,512]{1,0:T(8,128)(2,1)S(1)} %copy-done.2), custom_call_target="tpu_custom_call" | custom-call | flops 700000000 | bytes 5000000 | tf_op jit(solution)/shard_map/pallas_call | solution.py:62
  4.0 11.2 %all_gather.6.twok.twov = bf16[256,1024]{1,0:T(8,128)(2,1)S(1)} all-gather(bf16[64,1024]{1,0:T(8,128)(2,1)S(1)} %get-tuple-element.23), channel_id=1, replica_groups={{0,8,16,24},{32,40,48,56},{64,72,80,88},{96,104,112,120},{128,136,144,1..., dimensions={0}, use_global_device_ids=true | all-gather | bytes 655360 | tf_op jit(solution)/shard_map/all_gather | solution.py:319
  15.2 0.0 copy-start
  15.2 5.0 %collective-permute-start.2 = (bf16[128,1024]{1,0:T(8,128)(2,1)S(1)}, bf16[128,1024]{1,0:T(8,128)(2,1)S(1)}, u32[]{:S(2)}, u32[]{:S(2)}) collective-permute-start(bf16[128,1024]{1,0:T(8,128)(2,1)S(1)} %slice_select_fusion), channel_id=1, source_target_pairs={{480,0},{488,8},{48,16},{56,24},{0,32},{8,40},{80,48},{88,56},{32,... | collective-permute-start | bytes 786440 | tf_op jit(solution)/shard_map/ppermute | solution.py:305
  20.3 12.0 %collective-permute-done.2.nextk.nextv = bf16[128,1024]{1,0:T(8,128)(2,1)S(1)} collective-permute-done((bf16[128,1024]{1,0:T(8,128)(2,1)S(1)}, bf16[128,1024]{1,0:T(8,128)(2,1)S(1)}, u32[]{:S(2)}, u32[]{:S(2)}) %collective-permute-start.2) | collective-permute-done | bytes 262176 | tf_op jit(solution)/shard_map/ppermute | solution.py:305
  32.3 23.5 %all_gather.7.f0 = bf16[256,1024]{1,0:T(8,128)(2,1)S(1)} all-gather(bf16[16,1024]{1,0:T(8,128)(2,1)S(1)} %get-tuple-element.28), channel_id=1, replica_groups={{0,32,64,96,128,160,192,224,256,288,320,352,384,416,448,480},{8,40,72,1..., dimensions={0}, use_global_device_ids=true | all-gather | bytes 557056 | tf_op jit(solution)/shard_map/all_gather | solution.py:319
  55.8 3.6 %collective-permute-start.3 = (bf16[256,1024]{1,0:T(8,128)(2,1)S(1)}, bf16[256,1024]{1,0:T(8,128)(2,1)S(1)}, u32[]{:S(2)}, u32[]{:S(2)}) collective-permute-start(bf16[256,1024]{1,0:T(8,128)(2,1)S(1)} %all_gather.7.f0), channel_id=1, source_target_pairs={{8,0},{16,8},{24,16},{32,24},{40,32},{48,40},{56,48},{64,56},{72,6... | collective-permute-start | bytes 1572872 | tf_op jit(solution)/shard_map/ppermute | solution.py:305
  59.3 0.0 copy-start.4
  59.4 1.9 %collective-permute-start = (bf16[256,1024]{1,0:T(8,128)(2,1)S(1)}, bf16[256,1024]{1,0:T(8,128)(2,1)S(1)}, u32[]{:S(2)}, u32[]{:S(2)}) collective-permute-start(bf16[256,1024]{1,0:T(8,128)(2,1)S(1)} %get-tuple-element.20), channel_id=1, source_target_pairs={{504,0},{0,8},{8,16},{16,24},{24,32},{32,40},{40,48},{48,56},{56,6... | collective-permute-start | bytes 1572872 | tf_op jit(solution)/shard_map/ppermute | solution.py:305
  61.3 6.7 %collective-permute-start.1 = (bf16[256,1024]{1,0:T(8,128)(2,1)S(1)}, bf16[256,1024]{1,0:T(8,128)(2,1)S(1)}, u32[]{:S(2)}, u32[]{:S(2)}) collective-permute-start(bf16[256,1024]{1,0:T(8,128)(2,1)S(1)} %get-tuple-element.21), channel_id=1, source_target_pairs={{8,0},{16,8},{24,16},{32,24},{40,32},{48,40},{56,48},{64,56},{72,6... | collective-permute-start | bytes 1572872 | tf_op jit(solution)/shard_map/ppermute | solution.py:305
  68.0 1.9 %collective-permute-start.5 = (bf16[256,1024]{1,0:T(8,128)(2,1)S(1)}, bf16[256,1024]{1,0:T(8,128)(2,1)S(1)}, u32[]{:S(2)}, u32[]{:S(2)}) collective-permute-start(bf16[256,1024]{1,0:T(8,128)(2,1)S(1)} %all_gather.7.f0), channel_id=1, source_target_pairs={{504,0},{0,8},{8,16},{16,24},{24,32},{32,40},{40,48},{48,56},{56,6... | collective-permute-start | bytes 1572872 | tf_op jit(solution)/shard_map/ppermute | solution.py:305
  69.9 0.0 copy-done.4
  69.9 0.0 collective-permute-done.3.f1
  70.0 6.7 %collective-permute-start.4 = (bf16[256,512]{1,0:T(8,128)(2,1)S(1)}, bf16[256,512]{1,0:T(8,128)(2,1)S(1)}, u32[]{:S(2)}, u32[]{:S(2)}) collective-permute-start(bf16[256,512]{1,0:T(8,128)(2,1)S(1)} %slice.18), channel_id=1, source_target_pairs={{8,0},{16,8},{24,16},{32,24},{40,32},{48,40},{56,48},{64,56},{72,6... | collective-permute-start | bytes 786440 | tf_op jit(solution)/shard_map/ppermute | solution.py:305
  76.7 0.0 collective-permute-done.upk.upv
  76.7 0.0 collective-permute-done.1.dnk.dnv
  76.7 0.0 copy-done
  76.7 5.4 %shard_map.58 = (f32[1024,256]{1,0:T(8,128)S(1)}, f32[1024,256]{1,0:T(8,128)S(1)}) custom-call(s32[1]{0:T(128)} %bitcast.dev_ref, f32[4]{0:T(128)S(1)} %broadcast_multiply_fusion.temp_ref, bf16[1024,512]{1,0:T(8,128)(2,1)S(1)} %copy-done, bf16[1024,512]{1,0:T(8,128)(2,1)} %k_ref.5, bf16[1024,512]{1,0:T(8,128)(2,1)} %v_ref.5, ...), custom_call_target="tpu_custom_call" | custom-call | flops 2000000000 | bytes 6000000 | tf_op jit(solution)/shard_map/pallas_call | solution.py:180
  82.1 0.9 collective-permute-done.5.f3
  82.9 1.9 %collective-permute-start.6 = (bf16[256,512]{1,0:T(8,128)(2,1)S(1)}, bf16[256,512]{1,0:T(8,128)(2,1)S(1)}, u32[]{:S(2)}, u32[]{:S(2)}) collective-permute-start(bf16[256,512]{1,0:T(8,128)(2,1)S(1)} %slice.19), channel_id=1, source_target_pairs={{504,0},{0,8},{8,16},{16,24},{24,32},{32,40},{40,48},{48,56},{56,6... | collective-permute-start | bytes 786440 | tf_op jit(solution)/shard_map/ppermute | solution.py:305
  84.9 5.4 %shard_map.56 = (f32[1024,256]{1,0:T(8,128)S(1)}, f32[1024,256]{1,0:T(8,128)S(1)}) custom-call(s32[1]{0:T(128)} %bitcast.dev_ref, f32[4]{0:T(128)S(1)} %broadcast_multiply_fusion.temp_ref, bf16[1024,512]{1,0:T(8,128)(2,1)S(1)} %copy-done, bf16[1024,512]{1,0:T(8,128)(2,1)} %k_ref.5, bf16[1024,512]{1,0:T(8,128)(2,1)} %v_ref.5, ...), custom_call_target="tpu_custom_call" | custom-call | flops 2000000000 | bytes 6000000 | tf_op jit(solution)/shard_map/pallas_call | solution.py:180
  90.2 0.0 collective-permute-done.4.f2
  90.2 6.1 %shard_map.57 = (f32[1024,256]{1,0:T(8,128)S(1)}, f32[1,1024]{1,0:T(1,128)S(1)}) custom-call(s32[1]{0:T(128)} %bitcast.dev_ref, f32[4]{0:T(128)S(1)} %broadcast_multiply_fusion.temp_ref, bf16[1024,512]{1,0:T(8,128)(2,1)S(1)} %copy-done, f32[1024,256]{1,0:T(8,128)S(1)} %get-tuple-element.26.acc_ref, f32[1024,256]{1,0:T(8,128)S(1)} %get-tuple-element.27.ml_ref, ...), custom_call_target="tpu_custom_call" | custom-call | flops 1200000000 | bytes 5000000 | tf_op jit(solution)/shard_map/pallas_call | solution.py:261
  96.3 0.2 collective-permute-done.6.f2
  96.5 6.0 %shard_map.59 = (f32[1024,256]{1,0:T(8,128)S(1)}, f32[1,1024]{1,0:T(1,128)S(1)}) custom-call(s32[1]{0:T(128)} %bitcast.dev_ref, f32[4]{0:T(128)S(1)} %broadcast_multiply_fusion.temp_ref, bf16[1024,512]{1,0:T(8,128)(2,1)S(1)} %copy-done, f32[1024,256]{1,0:T(8,128)S(1)} %get-tuple-element.30.acc_ref, f32[1024,256]{1,0:T(8,128)S(1)} %get-tuple-element.31.ml_ref, ...), custom_call_target="tpu_custom_call" | custom-call | flops 1200000000 | bytes 5000000 | tf_op jit(solution)/shard_map/pallas_call | solution.py:261
  102.6 23.8 %all_to_all.5 = f32[8,1,1024]{2,1,0:T(1,128)S(1)} all-to-all(f32[8,1,1024]{2,1,0:T(1,128)S(1)} %broadcast_in_dim.9), channel_id=1, replica_groups=mesh['seq'=64,'head'=8] {'head'}, dimensions={0} | all-to-all | bytes 65536 | tf_op jit(solution)/shard_map/all_to_all | solution.py:311
  126.4 0.0 copy-start.3
  126.4 0.7 copy-done.3
  127.1 1.9 %shard_map.60 = bf16[1024,512]{1,0:T(8,128)(2,1)} custom-call(f32[1024,256]{1,0:T(8,128)S(1)} %get-tuple-element.29.a_ref, f32[1024,256]{1,0:T(8,128)S(1)} %get-tuple-element.33.b_ref, f32[8,1024]{1,0:T(8,128)S(1)} %bitcast.6, f32[1,512]{1,0:T(1,128)S(1)} %bitcast.8), custom_call_target="tpu_custom_call" | custom-call | flops 2000000 | bytes 3000000 | tf_op jit(solution)/shard_map/pallas_call | solution.py:292
  (6 shorter events, 0.1 us)
Async XLA Ops:
  0.0 1.2 copy-start.1
  1.2 1.2 copy-start.2
  15.2 61.5 %copy-start = (bf16[1024,512]{1,0:T(8,128)(2,1)S(1)}, bf16[1024,512]{1,0:T(8,128)(2,1)}, u32[]{:S(2)}) copy-start(bf16[1024,512]{1,0:T(8,128)(2,1)} %q_ref.7) | copy-start | bytes 3145732
  15.2 17.0 %collective-permute-start.2 = (bf16[128,1024]{1,0:T(8,128)(2,1)S(1)}, bf16[128,1024]{1,0:T(8,128)(2,1)S(1)}, u32[]{:S(2)}, u32[]{:S(2)}) collective-permute-start(bf16[128,1024]{1,0:T(8,128)(2,1)S(1)} %slice_select_fusion), channel_id=1, source_target_pairs={{480,0},{488,8},{48,16},{56,24},{0,32},{8,40},{80,48},{88,56},{32,... | collective-permute-start | bytes 786440 | tf_op jit(solution)/shard_map/ppermute | solution.py:305
  55.8 14.2 %collective-permute-start.3 = (bf16[256,1024]{1,0:T(8,128)(2,1)S(1)}, bf16[256,1024]{1,0:T(8,128)(2,1)S(1)}, u32[]{:S(2)}, u32[]{:S(2)}) collective-permute-start(bf16[256,1024]{1,0:T(8,128)(2,1)S(1)} %all_gather.7.f0), channel_id=1, source_target_pairs={{8,0},{16,8},{24,16},{32,24},{40,32},{48,40},{56,48},{64,56},{72,6... | collective-permute-start | bytes 1572872 | tf_op jit(solution)/shard_map/ppermute | solution.py:305
  59.3 10.6 %copy-start.4 = (f32[4]{0:T(128)S(1)}, f32[4]{0:T(128)}, u32[]{:S(2)}) copy-start(f32[4]{0:T(128)} %param.8) | copy-start | bytes 52
  59.4 17.3 %collective-permute-start = (bf16[256,1024]{1,0:T(8,128)(2,1)S(1)}, bf16[256,1024]{1,0:T(8,128)(2,1)S(1)}, u32[]{:S(2)}, u32[]{:S(2)}) collective-permute-start(bf16[256,1024]{1,0:T(8,128)(2,1)S(1)} %get-tuple-element.20), channel_id=1, source_target_pairs={{504,0},{0,8},{8,16},{16,24},{24,32},{32,40},{40,48},{48,56},{56,6... | collective-permute-start | bytes 1572872 | tf_op jit(solution)/shard_map/ppermute | solution.py:305
  61.3 15.4 %collective-permute-start.1 = (bf16[256,1024]{1,0:T(8,128)(2,1)S(1)}, bf16[256,1024]{1,0:T(8,128)(2,1)S(1)}, u32[]{:S(2)}, u32[]{:S(2)}) collective-permute-start(bf16[256,1024]{1,0:T(8,128)(2,1)S(1)} %get-tuple-element.21), channel_id=1, source_target_pairs={{8,0},{16,8},{24,16},{32,24},{40,32},{48,40},{56,48},{64,56},{72,6... | collective-permute-start | bytes 1572872 | tf_op jit(solution)/shard_map/ppermute | solution.py:305
  68.0 14.9 %collective-permute-start.5 = (bf16[256,1024]{1,0:T(8,128)(2,1)S(1)}, bf16[256,1024]{1,0:T(8,128)(2,1)S(1)}, u32[]{:S(2)}, u32[]{:S(2)}) collective-permute-start(bf16[256,1024]{1,0:T(8,128)(2,1)S(1)} %all_gather.7.f0), channel_id=1, source_target_pairs={{504,0},{0,8},{8,16},{16,24},{24,32},{32,40},{40,48},{48,56},{56,6... | collective-permute-start | bytes 1572872 | tf_op jit(solution)/shard_map/ppermute | solution.py:305
  70.0 20.3 %collective-permute-start.4 = (bf16[256,512]{1,0:T(8,128)(2,1)S(1)}, bf16[256,512]{1,0:T(8,128)(2,1)S(1)}, u32[]{:S(2)}, u32[]{:S(2)}) collective-permute-start(bf16[256,512]{1,0:T(8,128)(2,1)S(1)} %slice.18), channel_id=1, source_target_pairs={{8,0},{16,8},{24,16},{32,24},{40,32},{48,40},{56,48},{64,56},{72,6... | collective-permute-start | bytes 786440 | tf_op jit(solution)/shard_map/ppermute | solution.py:305
  82.9 13.6 %collective-permute-start.6 = (bf16[256,512]{1,0:T(8,128)(2,1)S(1)}, bf16[256,512]{1,0:T(8,128)(2,1)S(1)}, u32[]{:S(2)}, u32[]{:S(2)}) collective-permute-start(bf16[256,512]{1,0:T(8,128)(2,1)S(1)} %slice.19), channel_id=1, source_target_pairs={{504,0},{0,8},{8,16},{16,24},{24,32},{32,40},{40,48},{48,56},{56,6... | collective-permute-start | bytes 786440 | tf_op jit(solution)/shard_map/ppermute | solution.py:305
  126.4 0.7 copy-start.3

commit v3 on v2

--- a/solution.py
+++ b/solution.py
@@ -74,12 +74,33 @@
 
 
 def near_kernel(
-    pair, seq_size, dev_ref, temp_ref, q_ref, k_ref, v_ref,
-    upk, upv, dnk, dnv, onk, onv, twok, twov, nextk, nextv,
-    acc_ref, ml_ref, sa, sb, pa, pb,
+    pair, seq_size, dev_ref, temp_ref, q_all, k_all, v_all, up_all, down_all, one_all, two_all,
+    next_all, acc_all, ml_all, sa, sb, pa, pb,
 ):
+    def one_head(i, carry):
+        near_head(
+            pair, seq_size, i, dev_ref, temp_ref, q_all, k_all, v_all, up_all, down_all, one_all,
+            two_all, next_all, acc_all, ml_all, sa, sb, pa, pb,
+        )
+        return carry
+
+    lax.fori_loop(0, 2, one_head, 0)
+
+
+def near_head(
+    pair, seq_size, i, dev_ref, temp_ref, q_all, k_all, v_all, up_all, down_all, one_all, two_all,
+    next_all, acc_all, ml_all, sa, sb, pa, pb,
+):
+    def head_cols(ref, first):
+        return ref.at[:, pl.ds(pl.multiple_of(HEAD_DIM * (first + i), HEAD_DIM), HEAD_DIM)]
+
+    q_ref, k_ref, v_ref = [head_cols(ref, 2 * pair) for ref in (q_all, k_all, v_all)]
+    acc_ref, ml_ref = head_cols(acc_all, 0), head_cols(ml_all, 0)
+    edges = (up_all, down_all, one_all, two_all, next_all)
+    upk, dnk, onk, twok, nextk = [head_cols(ref, 4 * pair) for ref in edges]
+    upv, dnv, onv, twov, nextv = [head_cols(ref, 4 * pair + 2) for ref in edges]
     dev = dev_ref[0]
-    c = temp_ref[2 * pair + pl.program_id(0)]
+    c = temp_ref[2 * pair + i]
     z, y = dev // Y, dev % Y
 
     def gate(ok):
@@ -167,33 +188,24 @@
 def near(pair, seq_size, dev, temp, queries, keys, values, up, down, one, two, beyond):
     smem = pl.BlockSpec(memory_space=pltpu.SMEM)
 
-    def own(rows):
-        return pl.BlockSpec((rows, HEAD_DIM), lambda i: (0, 2 * pair + i))
-
-    def packed(rows):
-        return [
-            pl.BlockSpec((rows, HEAD_DIM), lambda i: (0, 4 * pair + i)),
-            pl.BlockSpec((rows, HEAD_DIM), lambda i: (0, 4 * pair + 2 + i)),
-        ]
-
-    out = pl.BlockSpec((ROWS, HEAD_DIM), lambda i: (0, i))
+    whole = pl.BlockSpec(memory_space=pltpu.VMEM)
     return pl.pallas_call(
         functools.partial(near_kernel, pair, seq_size),
-        grid=(2,),
-        in_specs=[smem, smem, own(ROWS), own(ROWS), own(ROWS)]
-        + packed(256) + packed(256) + packed(256) + packed(256) + packed(128),
-        out_specs=(out, out),
+        in_specs=[smem, smem] + [whole] * 8,
+        out_specs=(whole, whole),
         out_shape=(sds((ROWS, PAIR), F32), sds((ROWS, PAIR), F32)),
         scratch_shapes=[pltpu.VMEM((128, 1152), F32)] * 2 + [pltpu.VMEM((128, 1152), BF)] * 2,
         compiler_params=params(),
         cost_estimate=cost(2_000_000_000, 6_000_000, 2_500_000),
-    )(dev, temp, queries, keys, values, up, up, down, down, one, one, two, two, beyond, beyond)
+    )(dev, temp, queries, keys, values, up, down, one, two, beyond)
 
 
 CHUNK = 256
 
 
-def far_kernel(pair, has_sum, dev_ref, temp_ref, q_ref, acc_ref, ml_ref, f0, f1, f2, f3, *rest):
+def far_kernel(
+    pair, has_sum, dev_ref, temp_ref, q_ref, acc_ref, ml_ref, gain_ref, f0, f1, f2, f3, *rest
+):
     if has_sum:
         before_ref, att_ref, sum_ref, sa, sb, pa, pb, a_ref = rest
     else:
@@ -201,103 +213,133 @@
     dev = dev_ref[0]
     y, own_pair = dev % Y, dev // 2
     lane = lax.broadcasted_iota(jnp.int32, (1, 256), 1)
-    blocks = (f0, f1, f2, f3)
+    src_z = lane // 64 + 4 * (lane // 16 % 4)
     biases = []
     for k in range(4):
-        src_pair = (lane // 16 * Y + (y + k) % Y) // 2
+        src_pair = (src_z * Y + (y + k) % Y) // 2
         seen = (src_pair < own_pair - 1) | (src_pair > own_pair + 1)
         biases.append(jnp.where(seen, 0.0, GONE).astype(F32))
     bias = jnp.concatenate(biases, axis=1)
     ones = jnp.ones((1024, 128), BF)
-    for i in range(2):
-        cols = slice(HEAD_DIM * i, HEAD_DIM * (i + 1))
-        keys = jnp.concatenate([f[:, cols] for f in blocks], axis=0)
-        (sa, sb)[i][...] = lax.dot_general(
-            q_ref[:, cols], keys, NT, preferred_element_type=F32
+    starts = [0 if f.shape[1] == 512 else 512 * pair for f in (f0, f1, f2, f3)]
+    blocks = list(zip((f0, f1, f2, f3), starts))
+
+    def column(which, i):
+        return jnp.concatenate(
+            [
+                f[:, at + PAIR * which + HEAD_DIM * i : at + PAIR * which + HEAD_DIM * (i + 1)]
+                for f, at in blocks
+            ],
+            axis=0,
         )
-    squares = None
-    for i in range(2):
-        c = temp_ref[2 * pair + i]
-        cols = slice(HEAD_DIM * i, HEAD_DIM * (i + 1))
-        vcols = slice(PAIR + HEAD_DIM * i, PAIR + HEAD_DIM * (i + 1))
-        s_ref, p_ref = (sa, sb)[i], (pa, pb)[i]
-        shifted = bias + 6.0 / c
-        for r in range(CHUNK // 16):
-            rows = slice(16 * r, 16 * (r + 1))
-            parts = [
-                s_ref[rows, 128 * j : 128 * (j + 1)] + shifted[:, 128 * j : 128 * (j + 1)]
-                for j in range(8)
-            ]
-            best = jnp.max(functools.reduce(jnp.maximum, parts), axis=1, keepdims=True)
-            top_near = ml_ref[rows, HEAD_DIM * i : HEAD_DIM * i + 1]
-            top = jnp.maximum(top_near, c * best)
-            for j, t in enumerate(parts):
-                p_ref[rows, 128 * j : 128 * (j + 1)] = jnp.exp2(c * t - top).astype(BF)
-            a_ref[rows] = jnp.broadcast_to(jnp.exp2(top_near - top), (16, 128))
-        vals = jnp.concatenate([f[:, vcols] for f in blocks], axis=0)
-        both = jnp.dot(
-            p_ref[...], jnp.concatenate([vals, ones], axis=1), preferred_element_type=F32
-        )
-        alpha = a_ref[...]
-        total = alpha * ml_ref[:, HEAD_DIM * i + 64 : HEAD_DIM * i + 65] + both[:, 128:]
-        att = (acc_ref[:, cols] * alpha + both[:, :128]) / total
-        att_ref[:, cols] = att
-        squares = att * att if squares is None else squares + att * att
-    for j in range(CHUNK // 128):
-        rows = slice(128 * j, 128 * (j + 1))
-        line = jnp.sum(jnp.transpose(squares[rows]), axis=0, keepdims=True)
-        if has_sum:
-            line = line + before_ref[:, rows]
-        sum_ref[:, rows] = line
-
-
-def far(pair, dev, temp, queries, acc, ml, columns, before):
+
+    def part(step, carry):
+        first = step * HALF
+
+        def place(unit):
+            return pl.ds(pl.multiple_of(first + CHUNK * (unit // 2), CHUNK), CHUNK)
+
+        def score(unit):
+            i = unit % 2
+            q = q_ref[place(unit), PAIR * pair + HEAD_DIM * i : PAIR * pair + HEAD_DIM * (i + 1)]
+            (sa, sb)[i][...] = lax.dot_general(
+                q, column(0, i), NT, preferred_element_type=F32
+            )
+
+        squares = None
+        score(0)
+        for unit in range(4):
+            if unit < 3:
+                score(unit + 1)
+            i = unit % 2
+            c = temp_ref[2 * pair + i]
+            cols = slice(HEAD_DIM * i, HEAD_DIM * (i + 1))
+            s_ref, p_ref = (sa, sb)[i], (pa, pb)[i]
+            shifted = bias + 6.0 / c
+            start = first + CHUNK * (unit // 2)
+            for r in range(CHUNK // 16):
+                rows = slice(16 * r, 16 * (r + 1))
+                parts = [
+                    s_ref[rows, 128 * j : 128 * (j + 1)] + shifted[:, 128 * j : 128 * (j + 1)]
+                    for j in range(8)
+                ]
+                best = jnp.max(functools.reduce(jnp.maximum, parts), axis=1, keepdims=True)
+                there = pl.ds(pl.multiple_of(start + 16 * r, 16), 16)
+                top_near = ml_ref[there, HEAD_DIM * i : HEAD_DIM * i + 1]
+                top = jnp.maximum(top_near, c * best)
+                for j, t in enumerate(parts):
+                    p_ref[rows, 128 * j : 128 * (j + 1)] = jnp.exp2(c * t - top).astype(BF)
+                a_ref[rows] = jnp.broadcast_to(jnp.exp2(top_near - top), (16, 128))
+            both = jnp.dot(
+                p_ref[...],
+                jnp.concatenate([column(1, i), ones], axis=1),
+                preferred_element_type=F32,
+            )
+            alpha = a_ref[...]
+            here = place(unit)
+            total = alpha * ml_ref[here, HEAD_DIM * i + 64 : HEAD_DIM * i + 65] + both[:, 128:]
+            att = (acc_ref[here, cols] * alpha + both[:, :128]) / total
+            att_ref[here, cols] = att * gain_ref[:, PAIR * pair + HEAD_DIM * i : PAIR * pair + HEAD_DIM * (i + 1)]
+            if i == 0:
+                squares = att * att
+                continue
+            squares = squares + att * att
+            for j in range(CHUNK // 128):
+                line = jnp.sum(
+                    jnp.transpose(squares[128 * j : 128 * (j + 1)]), axis=0, keepdims=True
+                )
+                lanes = pl.ds(pl.multiple_of(start + 128 * j, 128), 128)
+                if has_sum:
+                    line = line + before_ref[:, lanes]
+                sum_ref[:, lanes] = line
+        return carry
+
+    lax.fori_loop(0, 2, part, 0)
+
+
+def far(pair, dev, temp, queries, acc, ml, gain, columns, before):
     smem = pl.BlockSpec(memory_space=pltpu.SMEM)
-    row = pl.BlockSpec((CHUNK, PAIR), lambda i: (i, 0))
-    whole = pl.BlockSpec((256, 512), lambda i: (0, pair))
-    part = pl.BlockSpec((256, 512), lambda i: (0, 0))
-    line = pl.BlockSpec((1, CHUNK), lambda i: (0, i))
+    whole = pl.BlockSpec(memory_space=pltpu.VMEM)
     extra = [] if before is None else [before]
     return pl.pallas_call(
         functools.partial(far_kernel, pair, before is not None),
-        grid=(ROWS // CHUNK,),
-        in_specs=[smem, smem, pl.BlockSpec((CHUNK, PAIR), lambda i: (i, pair)), row, row]
-        + [whole, whole, part, whole] + [line] * len(extra),
-        out_specs=(row, line),
+        in_specs=[smem, smem] + [whole] * (8 + len(extra)),
+        out_specs=(whole, whole),
         out_shape=(sds((ROWS, PAIR), F32), sds((1, ROWS), F32)),
         scratch_shapes=[pltpu.VMEM((CHUNK, 1024), F32)] * 2
         + [pltpu.VMEM((CHUNK, 1024), BF)] * 2
         + [pltpu.VMEM((CHUNK, 128), F32)],
         compiler_params=params(),
         cost_estimate=cost(1_200_000_000, 5_000_000, 2_100_000),
-    )(dev, temp, queries, acc, ml, *columns, *extra)
-
-
-def norm_kernel(a_ref, b_ref, sum_ref, gain_ref, out_ref):
-    mean = jnp.sum(sum_ref[...], axis=0, keepdims=True) / (HEADS * HEAD_DIM)
-    inverse = lax.rsqrt(mean + EPS)
+    )(dev, temp, queries, acc, ml, gain, *columns, *extra)
+
+
+def norm_kernel(a_ref, b_ref, sum_ref, out_ref):
+    start = pl.program_id(0) * CHUNK
     for j in range(CHUNK // 128):
         rows = slice(128 * j, 128 * (j + 1))
-        tall = jnp.transpose(jnp.broadcast_to(inverse[:, rows], (128, 128)))
+        there = pl.ds(pl.multiple_of(start + 128 * j, 128), 128)
+        mean = jnp.sum(sum_ref[:, there], axis=0, keepdims=True) / (HEADS * HEAD_DIM)
+        inverse = lax.rsqrt(mean + EPS)
+        tall = jnp.transpose(jnp.broadcast_to(inverse, (128, 128)))
         for h in range(4):
             ref = a_ref if h < 2 else b_ref
             cols = slice(HEAD_DIM * (h % 2), HEAD_DIM * (h % 2 + 1))
             to = slice(HEAD_DIM * h, HEAD_DIM * (h + 1))
-            out_ref[rows, to] = (ref[rows, cols] * tall * gain_ref[:, to]).astype(BF)
-
-
-def norm(att_a, att_b, sums, gain):
-    row = pl.BlockSpec((CHUNK, PAIR), lambda i: (i, 0))
-    line = pl.BlockSpec((8, CHUNK), lambda i: (0, i))
+            out_ref[rows, to] = (ref[there, cols] * tall).astype(BF)
+
+
+def norm(att_a, att_b, sums):
+    whole = pl.BlockSpec(memory_space=pltpu.VMEM)
     return pl.pallas_call(
         norm_kernel,
         grid=(ROWS // CHUNK,),
-        in_specs=[row, row, line, pl.BlockSpec((1, 512), lambda i: (0, 0))],
+        in_specs=[whole, whole, whole],
         out_specs=pl.BlockSpec((CHUNK, 512), lambda i: (i, 0)),
         out_shape=sds((ROWS, 512), BF),
         compiler_params=params(),
         cost_estimate=cost(2_000_000, 3_000_000),
-    )(att_a, att_b, sums, gain)
+    )(att_a, att_b, sums)
 
 
 def fetch(value, axis, source):
@@ -312,7 +354,8 @@
 
 
 Y_RING = [[z * Y + y for y in range(Y)] for z in range(Z)]
-Z_RING = [[z * Y + y for z in range(Z)] for y in range(Y)]
+Z_APART = [[(a + 4 * b) * Y + y for b in range(4)] for a in range(4) for y in range(Y)]
+Z_NEXT = [[(a + 4 * b) * Y + y for a in range(4)] for b in range(4) for y in range(Y)]
 
 
 def joined(value, groups):
@@ -333,7 +376,9 @@
     beyond = fetch(other_half, "seq", lambda i: i - Y if i % Y < 2 else i + Y)
 
     three, beyond = lax.optimization_barrier((three, beyond))
-    column = joined(three, Z_RING)
+    column = joined(three, Z_APART)
+    column, from_up, from_down = lax.optimization_barrier((column, from_up, from_down))
+    column = joined(column, Z_NEXT)
     after = fetch(column, "seq", lambda i: i + 1)
     before = fetch(column, "seq", lambda i: i - 1)
     opposite_a = fetch(after[:, :512], "seq", lambda i: i + 1)
@@ -342,10 +387,11 @@
     near_args = (queries, keys, values, from_up, from_down, one, group_two, beyond)
     acc_a, ml_a = near(0, seq_size, dev, temp, *near_args)
     acc_b, ml_b = near(1, seq_size, dev, temp, *near_args)
-    att_a, sum_a = far(0, dev, temp, queries, acc_a, ml_a, (column, after, opposite_a, before), None)
-    att_b, sums = far(1, dev, temp, queries, acc_b, ml_b, (column, after, opposite_b, before), sum_a)
+    gain = norm_gain.reshape(1, 512)
+    att_a, sum_a = far(0, dev, temp, queries, acc_a, ml_a, gain, (column, after, opposite_a, before), None)
+    att_b, sums = far(1, dev, temp, queries, acc_b, ml_b, gain, (column, after, opposite_b, before), sum_a)
     sums = gathered(sums, "head").reshape(8, ROWS)
-    return norm(att_a, att_b, sums, norm_gain.reshape(1, 512))
+    return norm(att_a, att_b, sums)
 
 
 def solution(mesh):

time: 129 us -> 145 us (1.12)
  blocking collectives: 58.5 us -> 66 us
  starting transfers between devices: 27.7 us -> 34.8 us
    all_gather x2 -> x3, blocking collectives: 34.7 us -> 46.4 us  [joined(): lax.all_gather(value, 'seq', axis_index_groups=groups, axis=0, tiled=True)]
    ppermute x7, starting transfers between devices: 27.7 us -> 34.8 us  [fetch(): lax.ppermute(value, axis, [(source(i) % count, i) for i in range(count)])]
    all_to_all x1, blocking collectives: 23.8 us -> 19.6 us  [gathered(): return lax.all_to_all(many, axis, 0, 0, tiled=True)]
  transfers between devices with their start and end apart: 7 -> 7, of which waited for: 3 -> 2; matrix products, arithmetic and copies ran while one was open for 0% -> 0% of each run, Pallas kernels for 13% -> 12%
where the time goes in v3:
time: 145 us; the launch traced here: 144 us
  blocking collectives  66 us (46%)
  starting transfers between devices  34.8 us (24%)
  Pallas kernels  26 us (18%)
  waiting for transfers between devices  14.2 us (10%)
  local copies, waits for them, and re-layouts  3.2 us (2%)
    all_gather x3, blocking collectives, joined(): lax.all_gather(value, 'seq', axis_index_groups=groups, axis=0, tiled=True)  46.4 us
    ppermute x7, starting transfers between devices, fetch(): lax.ppermute(value, axis, [(source(i) % count, i) for i in range(count)])  34.8 us
    all_to_all x1, blocking collectives, gathered(): return lax.all_to_all(many, axis, 0, 0, tiled=True)  19.6 us
    ppermute x7, waiting for transfers between devices, fetch(): lax.ppermute(value, axis, [(source(i) % count, i) for i in range(count)])  14.2 us
    pallas_call x2, Pallas kernels, near(): pl.pallas_call(functools.partial(near_kernel, pair, seq_size), in_specs=[...  12.5 us
    pallas_call x2, Pallas kernels, far(): pl.pallas_call(functools.partial(far_kernel, pair, before is not None), i...  10.2 us
    unnamed x11, local copies, waits for them, and re-layouts  3.14 us
  transfers between devices with their start and end apart: 7, of which 2 were waited for; matrix products, arithmetic and copies ran while one was open for 0% of the time, Pallas kernels for 12%

profile of v3, /device:TPU:1, one launch (start us, length us, event | category | flops | bytes accessed | tf_op | source)
XLA Modules:
  0.0 144.4 jit_solution(9183217440588599553)
XLA Ops:
  0.0 0.0 copy-start.2
  0.0 1.2 copy-done.2
  1.2 0.0 copy-start.3
  1.2 1.2 copy-done.3
  2.5 1.5 %shard_map.55 = (bf16[256,1024]{1,0:T(8,128)(2,1)S(1)}, bf16[256,1024]{1,0:T(8,128)(2,1)S(1)}, bf16[256,1024]{1,0:T(8,128)(2,1)S(1)}, bf16[64,1024]{1,0:T(8,128)(2,1)S(1)}, bf16[16,1024]{1,0:T(8,128)(2,1)S(1)}) custom-call(bf16[1024,512]{1,0:T(8,128)(2,1)S(1)} %copy-done.2, bf16[1024,512]{1,0:T(8,128)(2,1)S(1)} %copy-done.3), custom_call_target="tpu_custom_call" | custom-call | flops 700000000 | bytes 5000000 | tf_op jit(solution)/shard_map/pallas_call | solution.py:62
  4.0 4.0 %collective-permute-start.1 = (bf16[256,1024]{1,0:T(8,128)(2,1)S(1)}, bf16[256,1024]{1,0:T(8,128)(2,1)S(1)}, u32[]{:S(2)}, u32[]{:S(2)}) collective-permute-start(bf16[256,1024]{1,0:T(8,128)(2,1)S(1)} %get-tuple-element.26), channel_id=1, source_target_pairs={{504,0},{0,8},{8,16},{16,24},{24,32},{32,40},{40,48},{48,56},{56,6... | collective-permute-start | bytes 1572872 | tf_op jit(solution)/shard_map/ppermute | solution.py:347
  8.0 12.3 %collective-permute-start.2 = (bf16[256,1024]{1,0:T(8,128)(2,1)S(1)}, bf16[256,1024]{1,0:T(8,128)(2,1)S(1)}, u32[]{:S(2)}, u32[]{:S(2)}) collective-permute-start(bf16[256,1024]{1,0:T(8,128)(2,1)S(1)} %get-tuple-element.27), channel_id=1, source_target_pairs={{8,0},{16,8},{24,16},{32,24},{40,32},{48,40},{56,48},{64,56},{72,6... | collective-permute-start | bytes 1572872 | tf_op jit(solution)/shard_map/ppermute | solution.py:347
  20.3 17.2 %all_gather.9.two_all = bf16[256,1024]{1,0:T(8,128)(2,1)S(1)} all-gather(bf16[64,1024]{1,0:T(8,128)(2,1)S(1)} %get-tuple-element.24), channel_id=1, replica_groups={{0,8,16,24},{32,40,48,56},{64,72,80,88},{96,104,112,120},{128,136,144,1..., dimensions={0}, use_global_device_ids=true | all-gather | bytes 655360 | tf_op jit(solution)/shard_map/all_gather | solution.py:362
  37.5 0.0 copy-start
  37.5 2.1 %collective-permute-start = (bf16[128,1024]{1,0:T(8,128)(2,1)S(1)}, bf16[128,1024]{1,0:T(8,128)(2,1)S(1)}, u32[]{:S(2)}, u32[]{:S(2)}) collective-permute-start(bf16[128,1024]{1,0:T(8,128)(2,1)S(1)} %slice_select_fusion), channel_id=1, source_target_pairs={{480,0},{488,8},{48,16},{56,24},{0,32},{8,40},{80,48},{88,56},{32,... | collective-permute-start | bytes 786440 | tf_op jit(solution)/shard_map/ppermute | solution.py:347
  39.6 10.0 %collective-permute-done.next_all = bf16[128,1024]{1,0:T(8,128)(2,1)S(1)} collective-permute-done((bf16[128,1024]{1,0:T(8,128)(2,1)S(1)}, bf16[128,1024]{1,0:T(8,128)(2,1)S(1)}, u32[]{:S(2)}, u32[]{:S(2)}) %collective-permute-start) | collective-permute-done | bytes 262176 | tf_op jit(solution)/shard_map/ppermute | solution.py:347
  49.6 16.1 %all_gather.10 = bf16[64,1024]{1,0:T(8,128)(2,1)S(1)} all-gather(bf16[16,1024]{1,0:T(8,128)(2,1)S(1)} %get-tuple-element.25), channel_id=1, replica_groups={{0,128,256,384},{8,136,264,392},{16,144,272,400},{24,152,280,408},{32,1..., dimensions={0}, use_global_device_ids=true | all-gather | bytes 163840 | tf_op jit(solution)/shard_map/all_gather | solution.py:362
  65.7 0.0 copy-start.4
  65.7 0.0 collective-permute-done.1.up_all
  65.7 0.0 collective-permute-done.2.down_all
  65.7 13.1 %all_gather.11.f0 = bf16[256,1024]{1,0:T(8,128)(2,1)S(1)} all-gather(bf16[64,1024]{1,0:T(8,128)(2,1)S(1)} %all_gather.10), channel_id=1, replica_groups={{0,32,64,96},{8,40,72,104},{16,48,80,112},{24,56,88,120},{128,160,192,2..., dimensions={0}, use_global_device_ids=true | all-gather | bytes 655360 | tf_op jit(solution)/shard_map/all_gather | solution.py:362
  78.8 5.5 %collective-permute-start.3 = (bf16[256,1024]{1,0:T(8,128)(2,1)S(1)}, bf16[256,1024]{1,0:T(8,128)(2,1)S(1)}, u32[]{:S(2)}, u32[]{:S(2)}) collective-permute-start(bf16[256,1024]{1,0:T(8,128)(2,1)S(1)} %all_gather.11.f0), channel_id=1, source_target_pairs={{8,0},{16,8},{24,16},{32,24},{40,32},{48,40},{56,48},{64,56},{72,6... | collective-permute-start | bytes 1572872 | tf_op jit(solution)/shard_map/ppermute | solution.py:347
  84.3 1.9 %collective-permute-start.5 = (bf16[256,1024]{1,0:T(8,128)(2,1)S(1)}, bf16[256,1024]{1,0:T(8,128)(2,1)S(1)}, u32[]{:S(2)}, u32[]{:S(2)}) collective-permute-start(bf16[256,1024]{1,0:T(8,128)(2,1)S(1)} %all_gather.11.f0), channel_id=1, source_target_pairs={{504,0},{0,8},{8,16},{16,24},{24,32},{32,40},{40,48},{48,56},{56,6... | collective-permute-start | bytes 1572872 | tf_op jit(solution)/shard_map/ppermute | solution.py:347
  86.2 0.0 copy-done.4
  86.3 4.2 %collective-permute-done.3.f1 = bf16[256,1024]{1,0:T(8,128)(2,1)S(1)} collective-permute-done((bf16[256,1024]{1,0:T(8,128)(2,1)S(1)}, bf16[256,1024]{1,0:T(8,128)(2,1)S(1)}, u32[]{:S(2)}, u32[]{:S(2)}) %collective-permute-start.3) | collective-permute-done | bytes 524320 | tf_op jit(solution)/shard_map/ppermute | solution.py:347
  90.4 7.1 %collective-permute-start.4 = (bf16[256,512]{1,0:T(8,128)(2,1)S(1)}, bf16[256,512]{1,0:T(8,128)(2,1)S(1)}, u32[]{:S(2)}, u32[]{:S(2)}) collective-permute-start(bf16[256,512]{1,0:T(8,128)(2,1)S(1)} %slice.18), channel_id=1, source_target_pairs={{8,0},{16,8},{24,16},{32,24},{40,32},{48,40},{56,48},{64,56},{72,6... | collective-permute-start | bytes 786440 | tf_op jit(solution)/shard_map/ppermute | solution.py:347
  97.6 0.0 copy-done
  97.6 6.3 %shard_map.58 = (f32[1024,256]{1,0:T(8,128)S(1)}, f32[1024,256]{1,0:T(8,128)S(1)}) custom-call(s32[1]{0:T(128)} %bitcast.dev_ref, f32[4]{0:T(128)S(1)} %broadcast_multiply_fusion.temp_ref, bf16[1024,512]{1,0:T(8,128)(2,1)S(1)} %copy-done, bf16[1024,512]{1,0:T(8,128)(2,1)} %k_all.3, bf16[1024,512]{1,0:T(8,128)(2,1)} %v_all.3, ...), custom_call_target="tpu_custom_call" | custom-call | flops 2000000000 | bytes 6000000 | tf_op jit(solution)/shard_map/pallas_call | solution.py:192
  103.9 0.0 collective-permute-done.5.f3
  103.9 1.9 %collective-permute-start.6 = (bf16[256,512]{1,0:T(8,128)(2,1)S(1)}, bf16[256,512]{1,0:T(8,128)(2,1)S(1)}, u32[]{:S(2)}, u32[]{:S(2)}) collective-permute-start(bf16[256,512]{1,0:T(8,128)(2,1)S(1)} %slice.19), channel_id=1, source_target_pairs={{504,0},{0,8},{8,16},{16,24},{24,32},{32,40},{40,48},{48,56},{56,6... | collective-permute-start | bytes 786440 | tf_op jit(solution)/shard_map/ppermute | solution.py:347
  105.9 6.2 %shard_map.56 = (f32[1024,256]{1,0:T(8,128)S(1)}, f32[1024,256]{1,0:T(8,128)S(1)}) custom-call(s32[1]{0:T(128)} %bitcast.dev_ref, f32[4]{0:T(128)S(1)} %broadcast_multiply_fusion.temp_ref, bf16[1024,512]{1,0:T(8,128)(2,1)S(1)} %copy-done, bf16[1024,512]{1,0:T(8,128)(2,1)} %k_all.3, bf16[1024,512]{1,0:T(8,128)(2,1)} %v_all.3, ...), custom_call_target="tpu_custom_call" | custom-call | flops 2000000000 | bytes 6000000 | tf_op jit(solution)/shard_map/pallas_call | solution.py:192
  112.1 0.0 collective-permute-done.4.f2
  112.1 0.0 copy-start.1
  112.1 0.7 copy-done.1
  112.8 5.1 %shard_map.57 = (f32[1024,256]{1,0:T(8,128)S(1)}, f32[1,1024]{1,0:T(1,128)S(1)}) custom-call(s32[1]{0:T(128)} %bitcast.dev_ref, f32[4]{0:T(128)S(1)} %broadcast_multiply_fusion.temp_ref, bf16[1024,512]{1,0:T(8,128)(2,1)S(1)} %copy-done, f32[1024,256]{1,0:T(8,128)S(1)} %get-tuple-element.32.acc_ref, f32[1024,256]{1,0:T(8,128)S(1)} %get-tuple-element.33.ml_ref, ...), custom_call_target="tpu_custom_call" | custom-call | flops 1200000000 | bytes 5000000 | tf_op jit(solution)/shard_map/pallas_call | solution.py:304
  117.8 0.0 collective-permute-done.6.f2
  117.8 5.1 %shard_map.59 = (f32[1024,256]{1,0:T(8,128)S(1)}, f32[1,1024]{1,0:T(1,128)S(1)}) custom-call(s32[1]{0:T(128)} %bitcast.dev_ref, f32[4]{0:T(128)S(1)} %broadcast_multiply_fusion.temp_ref, bf16[1024,512]{1,0:T(8,128)(2,1)S(1)} %copy-done, f32[1024,256]{1,0:T(8,128)S(1)} %get-tuple-element.36.acc_ref, f32[1024,256]{1,0:T(8,128)S(1)} %get-tuple-element.37.ml_ref, ...), custom_call_target="tpu_custom_call" | custom-call | flops 1200000000 | bytes 5000000 | tf_op jit(solution)/shard_map/pallas_call | solution.py:304
  123.0 19.6 %all_to_all.5 = f32[8,1,1024]{2,1,0:T(1,128)S(1)} all-to-all(f32[8,1,1024]{2,1,0:T(1,128)S(1)} %broadcast_in_dim.9), channel_id=1, replica_groups=mesh['seq'=64,'head'=8] {'head'}, dimensions={0} | all-to-all | bytes 65536 | tf_op jit(solution)/shard_map/all_to_all | solution.py:353
  142.6 1.8 %shard_map.60 = bf16[1024,512]{1,0:T(8,128)(2,1)} custom-call(f32[1024,256]{1,0:T(8,128)S(1)} %get-tuple-element.35.a_ref, f32[1024,256]{1,0:T(8,128)S(1)} %get-tuple-element.39.b_ref, f32[8,1024]{1,0:T(8,128)S(1)} %bitcast.6), custom_call_target="tpu_custom_call" | custom-call | flops 2000000 | bytes 3000000 | tf_op jit(solution)/shard_map/pallas_call | solution.py:334
  (6 shorter events, 0.1 us)
Async XLA Ops:
  0.0 1.2 copy-start.2
  1.2 1.2 copy-start.3
  4.0 61.8 %collective-permute-start.1 = (bf16[256,1024]{1,0:T(8,128)(2,1)S(1)}, bf16[256,1024]{1,0:T(8,128)(2,1)S(1)}, u32[]{:S(2)}, u32[]{:S(2)}) collective-permute-start(bf16[256,1024]{1,0:T(8,128)(2,1)S(1)} %get-tuple-element.26), channel_id=1, source_target_pairs={{504,0},{0,8},{8,16},{16,24},{24,32},{32,40},{40,48},{48,56},{56,6... | collective-permute-start | bytes 1572872 | tf_op jit(solution)/shard_map/ppermute | solution.py:347
  8.0 57.7 %collective-permute-start.2 = (bf16[256,1024]{1,0:T(8,128)(2,1)S(1)}, bf16[256,1024]{1,0:T(8,128)(2,1)S(1)}, u32[]{:S(2)}, u32[]{:S(2)}) collective-permute-start(bf16[256,1024]{1,0:T(8,128)(2,1)S(1)} %get-tuple-element.27), channel_id=1, source_target_pairs={{8,0},{16,8},{24,16},{32,24},{40,32},{48,40},{56,48},{64,56},{72,6... | collective-permute-start | bytes 1572872 | tf_op jit(solution)/shard_map/ppermute | solution.py:347
  37.5 60.1 %copy-start = (bf16[1024,512]{1,0:T(8,128)(2,1)S(1)}, bf16[1024,512]{1,0:T(8,128)(2,1)}, u32[]{:S(2)}) copy-start(bf16[1024,512]{1,0:T(8,128)(2,1)} %q_ref.3) | copy-start | bytes 3145732
  37.5 12.1 %collective-permute-start = (bf16[128,1024]{1,0:T(8,128)(2,1)S(1)}, bf16[128,1024]{1,0:T(8,128)(2,1)S(1)}, u32[]{:S(2)}, u32[]{:S(2)}) collective-permute-start(bf16[128,1024]{1,0:T(8,128)(2,1)S(1)} %slice_select_fusion), channel_id=1, source_target_pairs={{480,0},{488,8},{48,16},{56,24},{0,32},{8,40},{80,48},{88,56},{32,... | collective-permute-start | bytes 786440 | tf_op jit(solution)/shard_map/ppermute | solution.py:347
  65.7 20.5 %copy-start.4 = (f32[4]{0:T(128)S(1)}, f32[4]{0:T(128)}, u32[]{:S(2)}) copy-start(f32[4]{0:T(128)} %param.8) | copy-start | bytes 52
  78.8 11.6 %collective-permute-start.3 = (bf16[256,1024]{1,0:T(8,128)(2,1)S(1)}, bf16[256,1024]{1,0:T(8,128)(2,1)S(1)}, u32[]{:S(2)}, u32[]{:S(2)}) collective-permute-start(bf16[256,1024]{1,0:T(8,128)(2,1)S(1)} %all_gather.11.f0), channel_id=1, source_target_pairs={{8,0},{16,8},{24,16},{32,24},{40,32},{48,40},{56,48},{64,56},{72,6... | collective-permute-start | bytes 1572872 | tf_op jit(solution)/shard_map/ppermute | solution.py:347
  84.3 19.6 %collective-permute-start.5 = (bf16[256,1024]{1,0:T(8,128)(2,1)S(1)}, bf16[256,1024]{1,0:T(8,128)(2,1)S(1)}, u32[]{:S(2)}, u32[]{:S(2)}) collective-permute-start(bf16[256,1024]{1,0:T(8,128)(2,1)S(1)} %all_gather.11.f0), channel_id=1, source_target_pairs={{504,0},{0,8},{8,16},{16,24},{24,32},{32,40},{40,48},{48,56},{56,6... | collective-permute-start | bytes 1572872 | tf_op jit(solution)/shard_map/ppermute | solution.py:347
  90.4 21.6 %collective-permute-start.4 = (bf16[256,512]{1,0:T(8,128)(2,1)S(1)}, bf16[256,512]{1,0:T(8,128)(2,1)S(1)}, u32[]{:S(2)}, u32[]{:S(2)}) collective-permute-start(bf16[256,512]{1,0:T(8,128)(2,1)S(1)} %slice.18), channel_id=1, source_target_pairs={{8,0},{16,8},{24,16},{32,24},{40,32},{48,40},{56,48},{64,56},{72,6... | collective-permute-start | bytes 786440 | tf_op jit(solution)/shard_map/ppermute | solution.py:347
  103.9 13.9 %collective-permute-start.6 = (bf16[256,512]{1,0:T(8,128)(2,1)S(1)}, bf16[256,512]{1,0:T(8,128)(2,1)S(1)}, u32[]{:S(2)}, u32[]{:S(2)}) collective-permute-start(bf16[256,512]{1,0:T(8,128)(2,1)S(1)} %slice.19), channel_id=1, source_target_pairs={{504,0},{0,8},{8,16},{16,24},{24,32},{32,40},{40,48},{48,56},{56,6... | collective-permute-start | bytes 786440 | tf_op jit(solution)/shard_map/ppermute | solution.py:347
  112.1 0.7 copy-start.1

commit v4 on v3

v4 whole, which is shorter than its diff:
```python
import functools
import math

import jax
import jax.numpy as jnp
from jax import lax
from jax.experimental import pallas as pl
from jax.experimental.pallas import tpu as pltpu
from jax.sharding import PartitionSpec as P

HEADS = 32
HEAD_DIM = 128
BLK = 128
ROWS = 1024
HALF = 512
PAIR = 2 * HEAD_DIM
Y = 4
Z = 16

EPS = 1e-06
GONE = -1e30
NT = (((1,), (1,)), ((), ()))
BF = jnp.bfloat16
F32 = jnp.float32
VMEM_LIMIT = 48 * 1024 * 1024


def params():
    return pltpu.CompilerParams(vmem_limit_bytes=VMEM_LIMIT)


def cost(flops, moved, exps=0):
    return pl.CostEstimate(flops=flops, bytes_accessed=moved, transcendentals=exps)


def sds(shape, dtype):
    return jax.ShapeDtypeStruct(shape, dtype)


def prep_kernel(k_ref, v_ref, up_ref, down_ref, one_ref, two_ref, three_ref):
    rows = lax.broadcasted_iota(jnp.int32, (64, 256), 0)
    cols = lax.broadcasted_iota(jnp.int32, (64, 256), 1)
    pool = jnp.where(cols // 4 == rows, 0.25, 0.0).astype(BF)
    for which, ref in ((0, k_ref), (1, v_ref)):
        for pair in range(2):
            src = slice(pair * PAIR, (pair + 1) * PAIR)
            to = slice((2 * pair + which) * PAIR, (2 * pair + which + 1) * PAIR)
            for j in range(4):
                part = jnp.dot(pool, ref[256 * j : 256 * (j + 1), src], preferred_element_type=F32)
                one_ref[64 * j : 64 * (j + 1), to] = part.astype(BF)
            two = jnp.dot(pool, one_ref[:, to], preferred_element_type=F32).astype(BF)
            three = jnp.dot(pool[:16, :64], two, preferred_element_type=F32).astype(BF)
            two_ref[:, to] = two
            three_ref[:, to] = three
            up_ref[0:128, to] = ref[ROWS - 128 : ROWS, src]
            up_ref[128:256, to] = one_ref[128:256, to]
            up_ref[256:320, to] = two
            down_ref[0:128, to] = ref[0:128, src]
            down_ref[128:256, to] = one_ref[0:128, to]
            down_ref[256:320, to] = two


def prep(keys, values):
    return pl.pallas_call(
        prep_kernel,
        out_shape=(
            sds((320, 1024), BF),
            sds((320, 1024), BF),
            sds((256, 1024), BF),
            sds((64, 1024), BF),
            sds((16, 1024), BF),
        ),
        compiler_params=params(),
        cost_estimate=cost(700_000_000, 5_000_000),
    )(keys, values)


def near_kernel(
    pair, seq_size, dev_ref, temp_ref, q_ref, k_ref, v_ref,
    upk, upv, dnk, dnv, onk, onv,
    acc_ref, ml_ref, sa, sb, pa, pb,
):
    dev = dev_ref[0]
    c = temp_ref[2 * pair + pl.program_id(0)]
    def gate(ok):
        return jnp.where(ok, 0.0, GONE).astype(F32)

    g_up = gate(dev >= 1)
    g_dn = gate(dev <= seq_size - 2)

    lane384 = lax.broadcasted_iota(jnp.int32, (1, 384), 1)
    lane128 = lax.broadcasted_iota(jnp.int32, (128, 128), 1)
    ones = jnp.ones((768, 128), BF)
    def window(b, own_ref, up_ref, dn_ref, one_ref):
        if b == 0:
            fine = [up_ref[0:128], own_ref[0:256]]
        elif b == 7:
            fine = [own_ref[768:1024], dn_ref[0:128]]
        else:
            fine = [own_ref[128 * (b - 1) : 128 * (b + 2)]]
        if b < 4:
            first = [up_ref[128:256], one_ref[...]]
        else:
            first = [one_ref[...], dn_ref[128:256]]
        return jnp.concatenate(fine + first, axis=0)

    def score(b):
        keys = window(b, k_ref, upk, dnk, onk)
        scores = lax.dot_general(
            q_ref[128 * b : 128 * (b + 1)], keys, NT, preferred_element_type=F32
        )
        (sa, sb)[b % 2][...] = scores

    def bias_of(b):
        g = b // 4
        fine = None
        if b == 0:
            fine = jnp.where(lane384 < 128, g_up, 0.0)
        if b == 7:
            fine = jnp.where(lane384 >= 256, g_dn, 0.0)
        if g == 0:
            edge1 = jnp.where(lane384 < 128, g_up, 0.0)
        else:
            edge1 = jnp.where(lane384 >= 256, g_dn, 0.0)
        start = 32 * (b % 4) + 96
        hidden = (lane384 >= start) & (lane384 < start + 96)
        return fine, jnp.where(hidden, GONE, edge1) + 2.0 / c

    score(0)
    for b in range(8):
        if b < 7:
            score(b + 1)
        s_ref, p_ref = (sa, sb)[b % 2], (pa, pb)[b % 2]
        fine, first = bias_of(b)
        for r in range(8):
            rows = slice(16 * r, 16 * (r + 1))
            parts = []
            for j in range(6):
                t = s_ref[rows, 128 * j : 128 * (j + 1)]
                bias = (fine, first)[j // 3]
                if bias is not None:
                    t = t + bias[:, 128 * (j % 3) : 128 * (j % 3 + 1)]
                parts.append(t)
            top = jnp.max(functools.reduce(jnp.maximum, parts), axis=1, keepdims=True)
            for j, t in enumerate(parts):
                p_ref[rows, 128 * j : 128 * (j + 1)] = jnp.exp2((t - top) * c).astype(BF)
            ml_ref[128 * b + 16 * r : 128 * b + 16 * (r + 1)] = jnp.broadcast_to(
                top * c, (16, 128)
            )
        vals = window(b, v_ref, upv, dnv, onv)
        both = jnp.dot(
            p_ref[...], jnp.concatenate([vals, ones], axis=1), preferred_element_type=F32
        )
        rows = slice(128 * b, 128 * (b + 1))
        acc_ref[rows] = both[:, :128]
        ml_ref[rows] = jnp.where(lane128 < 64, ml_ref[rows], both[:, 128:])


def near(pair, seq_size, dev, temp, queries, keys, values, up, down, one):
    smem = pl.BlockSpec(memory_space=pltpu.SMEM)

    def own(rows):
        return pl.BlockSpec((rows, HEAD_DIM), lambda i: (0, 2 * pair + i))

    def packed(rows):
        return [
            pl.BlockSpec((rows, HEAD_DIM), lambda i: (0, 4 * pair + i)),
            pl.BlockSpec((rows, HEAD_DIM), lambda i: (0, 4 * pair + 2 + i)),
        ]

    out = pl.BlockSpec((ROWS, HEAD_DIM), lambda i: (0, i))
    return pl.pallas_call(
        functools.partial(near_kernel, pair, seq_size),
        grid=(2,),
        in_specs=[smem, smem, own(ROWS), own(ROWS), own(ROWS)]
        + packed(320) + packed(320) + packed(256),
        out_specs=(out, out),
        out_shape=(sds((ROWS, PAIR), F32), sds((ROWS, PAIR), F32)),
        scratch_shapes=[pltpu.VMEM((128, 768), F32)] * 2 + [pltpu.VMEM((128, 768), BF)] * 2,
        compiler_params=params(),
        cost_estimate=cost(4_000_000_000, 6_000_000, 1_600_000),
    )(dev, temp, queries, keys, values, up, up, down, down, one, one)


CHUNK = 256


def far_kernel(
    pair, seq_size, has_sum, dev_ref, temp_ref, q_ref, acc_ref, ml_ref, gain_ref,
    two_ref, up_ref, down_ref, third_ref, own_ref, after_ref, before_ref, high_ref, low_ref, *rest
):
    if has_sum:
        partial_ref, att_ref, sum_ref, sa, sb, pa, pb, a_ref = rest
    else:
        att_ref, sum_ref, sa, sb, pa, pb, a_ref = rest
    dev = dev_ref[0]
    y, own_pair = dev % Y, dev // 2
    lane = lax.broadcasted_iota(jnp.int32, (1, 256), 1)
    order = lane // 16
    doubled = 8 * (order % 2) + 4 * (order // 2 % 2) + 2 * (order // 4 % 2) + order // 8
    far_bias = []
    for ahead in (0, 1, 2 - 4 * pair, -1):
        holder = (dev + ahead + seq_size) % seq_size
        src_pair = ((holder // Y + doubled) % Z * Y + holder % Y) // 2
        seen = (src_pair < own_pair - 1) | (src_pair > own_pair + 1)
        far_bias.append(jnp.where(seen, 0.0, GONE).astype(F32))
    lane64 = lax.broadcasted_iota(jnp.int32, (1, 64), 1)
    third = jnp.where(dev % 2 == 0, 3, -3)
    distances = (-2, -1, 0, 1, 2, third)
    base = 512 * pair
    width = 1408

    def column(which, i):
        offset = PAIR * which + HEAD_DIM * i
        wide = slice(base + offset, base + offset + HEAD_DIM)
        slim = slice(offset, offset + HEAD_DIM)
        relayed = slice(256 + 64 * pair, 320 + 64 * pair)
        opposite = (high_ref, low_ref)[pair]
        return jnp.concatenate(
            [
                own_ref[:, wide],
                after_ref[:, wide],
                opposite[0:256, slim],
                before_ref[:, wide],
                low_ref[relayed, slim],
                up_ref[256:320, wide],
                two_ref[:, wide],
                down_ref[256:320, wide],
                high_ref[relayed, slim],
                third_ref[:, wide],
            ],
            axis=0,
        )

    ones = jnp.ones((width, 128), BF)

    def part(step, carry):
        first = step * HALF

        def place(unit):
            return pl.ds(pl.multiple_of(first + CHUNK * (unit // 2), CHUNK), CHUNK)

        def score(unit):
            i = unit % 2
            q = q_ref[place(unit), PAIR * pair + HEAD_DIM * i : PAIR * pair + HEAD_DIM * (i + 1)]
            (sa, sb)[i][...] = lax.dot_general(
                q, column(0, i), NT, preferred_element_type=F32
            )

        two_bias = []
        for distance in distances:
            token = distance * ROWS + 16 * lane64
            source = dev + distance
            inside = (token >= (step - 1) * HALF) & (token < (step + 2) * HALF)
            there = (source >= 0) & (source < seq_size)
            two_bias.append(jnp.where(inside | jnp.logical_not(there), GONE, 0.0).astype(F32))
        two_bias = jnp.concatenate(two_bias, axis=1)
        squares = None
        score(0)
        for unit in range(4):
            if unit < 3:
                score(unit + 1)
            i = unit % 2
            c = temp_ref[2 * pair + i]
            cols = slice(HEAD_DIM * i, HEAD_DIM * (i + 1))
            s_ref, p_ref = (sa, sb)[i], (pa, pb)[i]
            shifted = jnp.concatenate(
                [b + 6.0 / c for b in far_bias] + [two_bias + 4.0 / c], axis=1
            )
            start = first + CHUNK * (unit // 2)
            for r in range(CHUNK // 16):
                rows = slice(16 * r, 16 * (r + 1))
                parts = [
                    s_ref[rows, 128 * j : 128 * (j + 1)] + shifted[:, 128 * j : 128 * (j + 1)]
                    for j in range(width // 128)
                ]
                best = jnp.max(functools.reduce(jnp.maximum, parts), axis=1, keepdims=True)
                there = pl.ds(pl.multiple_of(start + 16 * r, 16), 16)
                top_near = ml_ref[there, HEAD_DIM * i : HEAD_DIM * i + 1]
                top = jnp.maximum(top_near, c * best)
                for j, t in enumerate(parts):
                    p_ref[rows, 128 * j : 128 * (j + 1)] = jnp.exp2(c * t - top).astype(BF)
                a_ref[rows] = jnp.broadcast_to(jnp.exp2(top_near - top), (16, 128))
            both = jnp.dot(
                p_ref[...],
                jnp.concatenate([column(1, i), ones], axis=1),
                preferred_element_type=F32,
            )
            alpha = a_ref[...]
            here = place(unit)
            total = alpha * ml_ref[here, HEAD_DIM * i + 64 : HEAD_DIM * i + 65] + both[:, 128:]
            att = (acc_ref[here, cols] * alpha + both[:, :128]) / total
            att_ref[here, cols] = att * gain_ref[:, PAIR * pair + HEAD_DIM * i : PAIR * pair + HEAD_DIM * (i + 1)]
            if i == 0:
                squares = att * att
                continue
            squares = squares + att * att
            for j in range(CHUNK // 128):
                line = jnp.sum(
                    jnp.transpose(squares[128 * j : 128 * (j + 1)]), axis=0, keepdims=True
                )
                lanes = pl.ds(pl.multiple_of(start + 128 * j, 128), 128)
                if has_sum:
                    line = line + partial_ref[:, lanes]
                sum_ref[:, lanes] = line
        return carry

    lax.fori_loop(0, 2, part, 0)


def far(pair, seq_size, dev, temp, queries, acc, ml, gain, blocks, partial):
    smem = pl.BlockSpec(memory_space=pltpu.SMEM)
    whole = pl.BlockSpec(memory_space=pltpu.VMEM)
    extra = [] if partial is None else [partial]
    return pl.pallas_call(
        functools.partial(far_kernel, pair, seq_size, partial is not None),
        in_specs=[smem, smem] + [whole] * (4 + len(blocks) + len(extra)),
        out_specs=(whole, whole),
        out_shape=(sds((ROWS, PAIR), F32), sds((1, ROWS), F32)),
        scratch_shapes=[pltpu.VMEM((CHUNK, 1408), F32)] * 2
        + [pltpu.VMEM((CHUNK, 1408), BF)] * 2
        + [pltpu.VMEM((CHUNK, 128), F32)],
        compiler_params=params(),
        cost_estimate=cost(6_000_000_000, 5_000_000, 2_800_000),
    )(dev, temp, queries, acc, ml, gain, *blocks, *extra)


def norm_kernel(a_ref, b_ref, sum_ref, out_ref):
    start = pl.program_id(0) * CHUNK
    for j in range(CHUNK // 128):
        rows = slice(128 * j, 128 * (j + 1))
        there = pl.ds(pl.multiple_of(start + 128 * j, 128), 128)
        mean = jnp.sum(sum_ref[:, there], axis=0, keepdims=True) / (HEADS * HEAD_DIM)
        inverse = lax.rsqrt(mean + EPS)
        tall = jnp.transpose(jnp.broadcast_to(inverse, (128, 128)))
        for h in range(4):
            ref = a_ref if h < 2 else b_ref
            cols = slice(HEAD_DIM * (h % 2), HEAD_DIM * (h % 2 + 1))
            to = slice(HEAD_DIM * h, HEAD_DIM * (h + 1))
            out_ref[rows, to] = (ref[there, cols] * tall).astype(BF)


def norm(att_a, att_b, sums):
    whole = pl.BlockSpec(memory_space=pltpu.VMEM)
    return pl.pallas_call(
        norm_kernel,
        grid=(ROWS // CHUNK,),
        in_specs=[whole, whole, whole],
        out_specs=pl.BlockSpec((CHUNK, 512), lambda i: (i, 0)),
        out_shape=sds((ROWS, 512), BF),
        compiler_params=params(),
        cost_estimate=cost(2_000_000, 3_000_000),
    )(att_a, att_b, sums)


def fetch(value, axis, source):
    count = lax.axis_size(axis)
    return lax.ppermute(value, axis, [(source(i) % count, i) for i in range(count)])


def gathered(value, axis):
    size = lax.axis_size(axis)
    many = jnp.broadcast_to(value[None], (size,) + value.shape)
    return lax.all_to_all(many, axis, 0, 0, tiled=True)


def local(queries, keys, values, head_temp, norm_gain):
    seq_size = lax.axis_size("seq")
    dev = lax.axis_index("seq").astype(jnp.int32).reshape(1)
    temp = head_temp * F32(math.log2(math.e) / math.sqrt(HEAD_DIM))
    up, down, one, two, three = prep(keys, values)

    column = three
    for shift in (8, 4, 2, 1):
        column = jnp.concatenate([column, fetch(column, "seq", lambda i: i + Y * shift)], axis=0)
    from_up = fetch(up, "seq", lambda i: i - 1)
    from_down = fetch(down, "seq", lambda i: i + 1)
    third = fetch(two, "seq", lambda i: i + 3 if i % 2 == 0 else i - 3)
    after = fetch(column, "seq", lambda i: i + 1)
    before = fetch(column, "seq", lambda i: i - 1)

    def relay(half, edge):
        return jnp.concatenate([half, edge[256:, :512], edge[256:, 512:]], axis=0)

    high = fetch(relay(after[:, :512], from_down), "seq", lambda i: i + 1)
    low = fetch(relay(before[:, 512:], from_up), "seq", lambda i: i - 1)

    near_args = (queries, keys, values, from_up, from_down, one)
    acc_a, ml_a = near(0, seq_size, dev, temp, *near_args)
    acc_b, ml_b = near(1, seq_size, dev, temp, *near_args)
    gain = norm_gain.reshape(1, 512)
    blocks = (two, from_up, from_down, third, column, after, before, high, low)
    att_a, sum_a = far(0, seq_size, dev, temp, queries, acc_a, ml_a, gain, blocks, None)
    att_b, sums = far(1, seq_size, dev, temp, queries, acc_b, ml_b, gain, blocks, sum_a)
    sums = gathered(sums, "head").reshape(8, ROWS)
    return norm(att_a, att_b, sums)


def solution(mesh):
    return jax.shard_map(
        local,
        mesh=mesh,
        in_specs=(P("seq", "head"), P("seq", "head"), P("seq", "head"), P("head"), P("head")),
        out_specs=P("seq", "head"),
        check_vma=False,
    )
```

time: 145 us -> 129 us (0.89)
  blocking collectives: 66 us -> 14.8 us
  starting transfers between devices: 34.8 us -> 60.4 us
  waiting for transfers between devices: 14.2 us -> 19.9 us
  local copies, waits for them, and re-layouts: 3.2 us -> 5.27 us
    all_gather x3 -> x0, blocking collectives: 46.4 us -> none  [joined(): lax.all_gather(value, 'seq', axis_index_groups=groups, axis=0, tiled=True)]
    ppermute x7 -> x11, starting transfers between devices: 34.8 us -> 60.4 us  [fetch(): lax.ppermute(value, axis, [(source(i) % count, i) for i in range(count)])]
    ppermute x7 -> x11, waiting for transfers between devices: 14.2 us -> 19.9 us  [fetch(): lax.ppermute(value, axis, [(source(i) % count, i) for i in range(count)])]
    all_to_all x1, blocking collectives: 19.6 us -> 14.8 us  [gathered(): return lax.all_to_all(many, axis, 0, 0, tiled=True)]
    unnamed x11 -> x29, local copies, waits for them, and re-layouts: 3.14 us -> 5.18 us
  transfers between devices with their start and end apart: 7 -> 11, of which waited for: 2 -> 4; matrix products, arithmetic and copies ran while one was open for 0% -> 0% of each run, Pallas kernels for 12% -> 6%
where the time goes in v4:
time: 129 us; the launch traced here: 128 us
  starting transfers between devices  60.4 us (47%)
  Pallas kernels  27.3 us (21%)
  waiting for transfers between devices  19.9 us (15%)
  blocking collectives  14.8 us (11%)
  local copies, waits for them, and re-layouts  5.27 us (4%)
    ppermute x11, starting transfers between devices, fetch(): lax.ppermute(value, axis, [(source(i) % count, i) for i in range(count)])  60.4 us
    ppermute x11, waiting for transfers between devices, fetch(): lax.ppermute(value, axis, [(source(i) % count, i) for i in range(count)])  19.9 us
    pallas_call x2, Pallas kernels, far(): pl.pallas_call(functools.partial(far_kernel, pair, seq_size, partial is n...  15.4 us
    all_to_all x1, blocking collectives, gathered(): return lax.all_to_all(many, axis, 0, 0, tiled=True)  14.8 us
    pallas_call x2, Pallas kernels, near(): pl.pallas_call(functools.partial(near_kernel, pair, seq_size), grid=(2,),...  7.85 us
    unnamed x29, local copies, waits for them, and re-layouts  5.18 us
  transfers between devices with their start and end apart: 11, of which 4 were waited for; matrix products, arithmetic and copies ran while one was open for 0% of the time, Pallas kernels for 6%

profile of v4, /device:TPU:1, one launch (start us, length us, event | category | flops | bytes accessed | tf_op | source)
XLA Modules:
  0.0 128.1 jit_solution(6618753802889617942)
XLA Ops:
  0.0 0.0 copy-start
  0.0 1.2 copy-done
  1.2 0.0 copy-start.2
  1.2 1.2 copy-done.2
  2.5 2.2 %shard_map.55 = (bf16[320,1024]{1,0:T(8,128)(2,1)S(1)}, bf16[320,1024]{1,0:T(8,128)(2,1)}, bf16[256,1024]{1,0:T(8,128)(2,1)S(1)}, bf16[64,1024]{1,0:T(8,128)(2,1)S(1)}, bf16[16,1024]{1,0:T(8,128)(2,1)S(1)}) custom-call(bf16[1024,512]{1,0:T(8,128)(2,1)S(1)} %copy-done, bf16[1024,512]{1,0:T(8,128)(2,1)S(1)} %copy-done.2), custom_call_target="tpu_custom_call" | custom-call | flops 700000000 | bytes 5000000 | tf_op jit(solution)/shard_map/pallas_call | solution.py:64
  4.7 0.0 copy-start.5
  4.7 16.3 %collective-permute-start.3 = (bf16[16,1024]{1,0:T(8,128)(2,1)S(1)}, bf16[16,1024]{1,0:T(8,128)(2,1)S(1)}, u32[]{:S(2)}, u32[]{:S(2)}) collective-permute-start(bf16[16,1024]{1,0:T(8,128)(2,1)S(1)} %get-tuple-element.24), channel_id=1, source_target_pairs={{256,0},{264,8},{272,16},{280,24},{288,32},{296,40},{304,48},{312,... | collective-permute-start | bytes 98312 | tf_op jit(solution)/shard_map/ppermute | solution.py:358
  21.0 1.4 %collective-permute-done.3 = bf16[16,1024]{1,0:T(8,128)(2,1)S(1)} collective-permute-done((bf16[16,1024]{1,0:T(8,128)(2,1)S(1)}, bf16[16,1024]{1,0:T(8,128)(2,1)S(1)}, u32[]{:S(2)}, u32[]{:S(2)}) %collective-permute-start.3) | collective-permute-done | bytes 32800 | tf_op jit(solution)/shard_map/ppermute | solution.py:358
  22.4 9.0 %collective-permute-start.4 = (bf16[32,1024]{1,0:T(8,128)(2,1)S(1)}, bf16[32,1024]{1,0:T(8,128)(2,1)S(1)}, u32[]{:S(2)}, u32[]{:S(2)}) collective-permute-start(bf16[32,1024]{1,0:T(8,128)(2,1)S(1)} %pad_maximum_fusion.4), channel_id=1, source_target_pairs={{128,0},{136,8},{144,16},{152,24},{160,32},{168,40},{176,48},{184,... | collective-permute-start | bytes 196616 | tf_op jit(solution)/shard_map/ppermute | solution.py:358
  31.3 1.3 %collective-permute-done.4 = bf16[32,1024]{1,0:T(8,128)(2,1)S(1)} collective-permute-done((bf16[32,1024]{1,0:T(8,128)(2,1)S(1)}, bf16[32,1024]{1,0:T(8,128)(2,1)S(1)}, u32[]{:S(2)}, u32[]{:S(2)}) %collective-permute-start.4) | collective-permute-done | bytes 65568 | tf_op jit(solution)/shard_map/ppermute | solution.py:358
  32.7 7.1 %collective-permute-start.5 = (bf16[64,1024]{1,0:T(8,128)(2,1)S(1)}, bf16[64,1024]{1,0:T(8,128)(2,1)S(1)}, u32[]{:S(2)}, u32[]{:S(2)}) collective-permute-start(bf16[64,1024]{1,0:T(8,128)(2,1)S(1)} %pad_maximum_fusion.3), channel_id=1, source_target_pairs={{64,0},{72,8},{80,16},{88,24},{96,32},{104,40},{112,48},{120,56},{... | collective-permute-start | bytes 393224 | tf_op jit(solution)/shard_map/ppermute | solution.py:358
  39.7 3.2 %collective-permute-start = (bf16[320,1024]{1,0:T(8,128)(2,1)S(1)}, bf16[320,1024]{1,0:T(8,128)(2,1)S(1)}, u32[]{:S(2)}, u32[]{:S(2)}) collective-permute-start(bf16[320,1024]{1,0:T(8,128)(2,1)S(1)} %get-tuple-element.18), channel_id=1, source_target_pairs={{504,0},{0,8},{8,16},{16,24},{24,32},{32,40},{40,48},{48,56},{56,6... | collective-permute-start | bytes 1966088 | tf_op jit(solution)/shard_map/ppermute | solution.py:358
  42.9 5.4 %collective-permute-start.1 = (bf16[320,1024]{1,0:T(8,128)(2,1)}, bf16[320,1024]{1,0:T(8,128)(2,1)S(1)}, u32[]{:S(2)}, u32[]{:S(2)}) collective-permute-start(bf16[320,1024]{1,0:T(8,128)(2,1)} %get-tuple-element.19), channel_id=1, source_target_pairs={{8,0},{16,8},{24,16},{32,24},{40,32},{48,40},{56,48},{64,56},{72,6... | collective-permute-start | bytes 1966088 | tf_op jit(solution)/shard_map/ppermute | solution.py:358
  48.4 1.9 %collective-permute-start.2 = (bf16[64,1024]{1,0:T(8,128)(2,1)S(1)}, bf16[64,1024]{1,0:T(8,128)(2,1)S(1)}, u32[]{:S(2)}, u32[]{:S(2)}) collective-permute-start(bf16[64,1024]{1,0:T(8,128)(2,1)S(1)} %get-tuple-element.23.two_ref), channel_id=1, source_target_pairs={{24,0},{496,8},{40,16},{0,24},{56,32},{16,40},{72,48},{32,56},{88,... | collective-permute-start | bytes 393224 | tf_op jit(solution)/shard_map/ppermute | solution.py:358
  50.3 0.0 collective-permute-done.5
  50.3 2.8 %collective-permute-start.6 = (bf16[128,1024]{1,0:T(8,128)(2,1)S(1)}, bf16[128,1024]{1,0:T(8,128)(2,1)S(1)}, u32[]{:S(2)}, u32[]{:S(2)}) collective-permute-start(bf16[128,1024]{1,0:T(8,128)(2,1)S(1)} %pad_maximum_fusion.2), channel_id=1, source_target_pairs={{32,0},{40,8},{48,16},{56,24},{64,32},{72,40},{80,48},{88,56},{96,... | collective-permute-start | bytes 786440 | tf_op jit(solution)/shard_map/ppermute | solution.py:358
  53.1 0.0 copy-done.5
  53.2 0.0 copy-start.11
  53.2 11.9 %collective-permute-done.6 = bf16[128,1024]{1,0:T(8,128)(2,1)S(1)} collective-permute-done((bf16[128,1024]{1,0:T(8,128)(2,1)S(1)}, bf16[128,1024]{1,0:T(8,128)(2,1)S(1)}, u32[]{:S(2)}, u32[]{:S(2)}) %collective-permute-start.6) | collective-permute-done | bytes 262176 | tf_op jit(solution)/shard_map/ppermute | solution.py:358
  65.1 1.9 %collective-permute-start.7 = (bf16[256,1024]{1,0:T(8,128)(2,1)S(1)}, bf16[256,1024]{1,0:T(8,128)(2,1)S(1)}, u32[]{:S(2)}, u32[]{:S(2)}) collective-permute-start(bf16[256,1024]{1,0:T(8,128)(2,1)S(1)} %constant_dynamic-update-slice_fusion.own_ref), channel_id=1, source_target_pairs={{8,0},{16,8},{24,16},{32,24},{40,32},{48,40},{56,48},{64,56},{72,6... | collective-permute-start | bytes 1572872 | tf_op jit(solution)/shard_map/ppermute | solution.py:358
  67.1 0.0 copy-done.11
  67.1 3.4 %collective-permute-start.8 = (bf16[256,1024]{1,0:T(8,128)(2,1)S(1)}, bf16[256,1024]{1,0:T(8,128)(2,1)S(1)}, u32[]{:S(2)}, u32[]{:S(2)}) collective-permute-start(bf16[256,1024]{1,0:T(8,128)(2,1)S(1)} %constant_dynamic-update-slice_fusion.own_ref), channel_id=1, source_target_pairs={{504,0},{0,8},{8,16},{16,24},{24,32},{32,40},{40,48},{48,56},{56,6... | collective-permute-start | bytes 1572872 | tf_op jit(solution)/shard_map/ppermute | solution.py:358
  70.4 0.0 collective-permute-done.1.dnk.dnv.down_ref
  70.5 0.0 collective-permute-done.upk.upv.up_ref
  70.5 5.3 %collective-permute-done.7.after_ref = bf16[256,1024]{1,0:T(8,128)(2,1)S(1)} collective-permute-done((bf16[256,1024]{1,0:T(8,128)(2,1)S(1)}, bf16[256,1024]{1,0:T(8,128)(2,1)S(1)}, u32[]{:S(2)}, u32[]{:S(2)}) %collective-permute-start.7) | collective-permute-done | bytes 524320 | tf_op jit(solution)/shard_map/ppermute | solution.py:358
  75.8 0.0 copy-start.6
  75.8 0.0 copy-start.1
  75.8 0.0 copy-start.3
  75.8 7.6 %collective-permute-start.9 = (bf16[384,512]{1,0:T(8,128)(2,1)S(1)}, bf16[384,512]{1,0:T(8,128)(2,1)S(1)}, u32[]{:S(2)}, u32[]{:S(2)}) collective-permute-start(bf16[384,512]{1,0:T(8,128)(2,1)S(1)} %pad_maximum_fusion), channel_id=1, source_target_pairs={{8,0},{16,8},{24,16},{32,24},{40,32},{48,40},{56,48},{64,56},{72,6... | collective-permute-start | bytes 1179656 | tf_op jit(solution)/shard_map/ppermute | solution.py:358
  83.4 0.0 collective-permute-done.8.before_ref
  83.5 1.9 %collective-permute-start.10 = (bf16[384,512]{1,0:T(8,128)(2,1)S(1)}, bf16[384,512]{1,0:T(8,128)(2,1)S(1)}, u32[]{:S(2)}, u32[]{:S(2)}) collective-permute-start(bf16[384,512]{1,0:T(8,128)(2,1)S(1)} %pad_maximum_fusion.1), channel_id=1, source_target_pairs={{504,0},{0,8},{8,16},{16,24},{24,32},{32,40},{40,48},{48,56},{56,6... | collective-permute-start | bytes 1179656 | tf_op jit(solution)/shard_map/ppermute | solution.py:358
  85.4 0.0 copy-done.6
  85.4 0.0 copy-done.1
  85.4 0.0 copy-done.3
  85.4 3.9 %shard_map.56 = (f32[1024,256]{1,0:T(8,128)S(1)}, f32[1024,256]{1,0:T(8,128)S(1)}) custom-call(s32[1]{0:T(128)} %bitcast.dev_ref, f32[4]{0:T(128)S(1)} %broadcast_multiply_fusion.temp_ref, bf16[1024,512]{1,0:T(8,128)(2,1)S(1)} %copy-done.3, bf16[1024,512]{1,0:T(8,128)(2,1)S(1)} %copy-done.1, bf16[1024,512]{1,0:T(8,128)(2,1)} %v_ref.5, ...), custom_call_target="tpu_custom_call" | custom-call | flops 4000000000 | bytes 6000000 | tf_op jit(solution)/shard_map/pallas_call | solution.py:172
  89.4 0.0 copy-start.9
  89.4 1.0 copy-done.9
  90.4 0.0 copy-start.10
  90.4 1.0 copy-done.10
  91.4 3.9 %shard_map.58 = (f32[1024,256]{1,0:T(8,128)S(1)}, f32[1024,256]{1,0:T(8,128)S(1)}) custom-call(s32[1]{0:T(128)} %bitcast.dev_ref, f32[4]{0:T(128)S(1)} %broadcast_multiply_fusion.temp_ref, bf16[1024,512]{1,0:T(8,128)(2,1)S(1)} %copy-done.3, bf16[1024,512]{1,0:T(8,128)(2,1)S(1)} %copy-done.1, bf16[1024,512]{1,0:T(8,128)(2,1)} %v_ref.5, ...), custom_call_target="tpu_custom_call" | custom-call | flops 4000000000 | bytes 6000000 | tf_op jit(solution)/shard_map/pallas_call | solution.py:172
  95.3 0.0 copy-start.7
  95.3 0.0 copy-start.8
  95.3 0.0 collective-permute-done.2.third_ref
  95.3 0.0 collective-permute-done.9.high_ref
  95.3 0.0 collective-permute-done.10.low_ref
  95.3 0.0 copy-start.4
  95.3 0.7 copy-done.4
  96.0 7.6 %shard_map.57 = (f32[1024,256]{1,0:T(8,128)S(1)}, f32[1,1024]{1,0:T(1,128)S(1)}) custom-call(s32[1]{0:T(128)} %bitcast.dev_ref, f32[4]{0:T(128)S(1)} %broadcast_multiply_fusion.temp_ref, bf16[1024,512]{1,0:T(8,128)(2,1)S(1)} %copy-done.3, f32[1024,256]{1,0:T(8,128)} %copy-done.9, f32[1024,256]{1,0:T(8,128)} %copy-done.10, f32[1,512]{1,0:T(1,128)S(1)} %bitcast.8, ...), custom_call_target="tpu_custom_call" | custom-call | flops 6000000000 | bytes 5000000 | tf_op jit(solution)/shard_map/pallas_call | solution.py:315
  103.7 0.0 copy-done.7
  103.7 0.0 copy-done.8
  103.7 7.7 %shard_map.59 = (f32[1024,256]{1,0:T(8,128)S(1)}, f32[1,1024]{1,0:T(1,128)S(1)}) custom-call(s32[1]{0:T(128)} %bitcast.dev_ref, f32[4]{0:T(128)S(1)} %broadcast_multiply_fusion.temp_ref, bf16[1024,512]{1,0:T(8,128)(2,1)S(1)} %copy-done.3, f32[1024,256]{1,0:T(8,128)} %copy-done.7, f32[1024,256]{1,0:T(8,128)} %copy-done.8, f32[1,512]{1,0:T(1,128)S(1)} %bitcast.9, ...), custom_call_target="tpu_custom_call" | custom-call | flops 6000000000 | bytes 5000000 | tf_op jit(solution)/shard_map/pallas_call | solution.py:315
  111.5 14.8 %all_to_all.5 = f32[8,1,1024]{2,1,0:T(1,128)S(1)} all-to-all(f32[8,1,1024]{2,1,0:T(1,128)S(1)} %broadcast_in_dim.9), channel_id=1, replica_groups=mesh['seq'=64,'head'=8] {'head'}, dimensions={0} | all-to-all | bytes 65536 | tf_op jit(solution)/shard_map/all_to_all | solution.py:364
  126.3 1.8 %shard_map.60 = bf16[1024,512]{1,0:T(8,128)(2,1)} custom-call(f32[1024,256]{1,0:T(8,128)S(1)} %get-tuple-element.25.a_ref, f32[1024,256]{1,0:T(8,128)S(1)} %get-tuple-element.29.b_ref, f32[8,1024]{1,0:T(8,128)S(1)} %bitcast.6), custom_call_target="tpu_custom_call" | custom-call | flops 2000000 | bytes 3000000 | tf_op jit(solution)/shard_map/pallas_call | solution.py:345
  (17 shorter events, 0.2 us)
Async XLA Ops:
  0.0 1.2 copy-start
  1.2 1.2 copy-start.2
  4.7 48.4 %copy-start.5 = (bf16[256,1024]{1,0:T(8,128)(2,1)}, bf16[256,1024]{1,0:T(8,128)(2,1)S(1)}, u32[]{:S(2)}) copy-start(bf16[256,1024]{1,0:T(8,128)(2,1)S(1)} %get-tuple-element.20.onk.onv) | copy-start | bytes 1572868
  4.7 17.7 %collective-permute-start.3 = (bf16[16,1024]{1,0:T(8,128)(2,1)S(1)}, bf16[16,1024]{1,0:T(8,128)(2,1)S(1)}, u32[]{:S(2)}, u32[]{:S(2)}) collective-permute-start(bf16[16,1024]{1,0:T(8,128)(2,1)S(1)} %get-tuple-element.24), channel_id=1, source_target_pairs={{256,0},{264,8},{272,16},{280,24},{288,32},{296,40},{304,48},{312,... | collective-permute-start | bytes 98312 | tf_op jit(solution)/shard_map/ppermute | solution.py:358
  22.4 10.3 %collective-permute-start.4 = (bf16[32,1024]{1,0:T(8,128)(2,1)S(1)}, bf16[32,1024]{1,0:T(8,128)(2,1)S(1)}, u32[]{:S(2)}, u32[]{:S(2)}) collective-permute-start(bf16[32,1024]{1,0:T(8,128)(2,1)S(1)} %pad_maximum_fusion.4), channel_id=1, source_target_pairs={{128,0},{136,8},{144,16},{152,24},{160,32},{168,40},{176,48},{184,... | collective-permute-start | bytes 196616 | tf_op jit(solution)/shard_map/ppermute | solution.py:358
  32.7 17.6 %collective-permute-start.5 = (bf16[64,1024]{1,0:T(8,128)(2,1)S(1)}, bf16[64,1024]{1,0:T(8,128)(2,1)S(1)}, u32[]{:S(2)}, u32[]{:S(2)}) collective-permute-start(bf16[64,1024]{1,0:T(8,128)(2,1)S(1)} %pad_maximum_fusion.3), channel_id=1, source_target_pairs={{64,0},{72,8},{80,16},{88,24},{96,32},{104,40},{112,48},{120,56},{... | collective-permute-start | bytes 393224 | tf_op jit(solution)/shard_map/ppermute | solution.py:358
  39.7 30.7 %collective-permute-start = (bf16[320,1024]{1,0:T(8,128)(2,1)S(1)}, bf16[320,1024]{1,0:T(8,128)(2,1)S(1)}, u32[]{:S(2)}, u32[]{:S(2)}) collective-permute-start(bf16[320,1024]{1,0:T(8,128)(2,1)S(1)} %get-tuple-element.18), channel_id=1, source_target_pairs={{504,0},{0,8},{8,16},{16,24},{24,32},{32,40},{40,48},{48,56},{56,6... | collective-permute-start | bytes 1966088 | tf_op jit(solution)/shard_map/ppermute | solution.py:358
  42.9 27.5 %collective-permute-start.1 = (bf16[320,1024]{1,0:T(8,128)(2,1)}, bf16[320,1024]{1,0:T(8,128)(2,1)S(1)}, u32[]{:S(2)}, u32[]{:S(2)}) collective-permute-start(bf16[320,1024]{1,0:T(8,128)(2,1)} %get-tuple-element.19), channel_id=1, source_target_pairs={{8,0},{16,8},{24,16},{32,24},{40,32},{48,40},{56,48},{64,56},{72,6... | collective-permute-start | bytes 1966088 | tf_op jit(solution)/shard_map/ppermute | solution.py:358
  48.4 46.9 %collective-permute-start.2 = (bf16[64,1024]{1,0:T(8,128)(2,1)S(1)}, bf16[64,1024]{1,0:T(8,128)(2,1)S(1)}, u32[]{:S(2)}, u32[]{:S(2)}) collective-permute-start(bf16[64,1024]{1,0:T(8,128)(2,1)S(1)} %get-tuple-element.23.two_ref), channel_id=1, source_target_pairs={{24,0},{496,8},{40,16},{0,24},{56,32},{16,40},{72,48},{32,56},{88,... | collective-permute-start | bytes 393224 | tf_op jit(solution)/shard_map/ppermute | solution.py:358
  50.3 14.8 %collective-permute-start.6 = (bf16[128,1024]{1,0:T(8,128)(2,1)S(1)}, bf16[128,1024]{1,0:T(8,128)(2,1)S(1)}, u32[]{:S(2)}, u32[]{:S(2)}) collective-permute-start(bf16[128,1024]{1,0:T(8,128)(2,1)S(1)} %pad_maximum_fusion.2), channel_id=1, source_target_pairs={{32,0},{40,8},{48,16},{56,24},{64,32},{72,40},{80,48},{88,56},{96,... | collective-permute-start | bytes 786440 | tf_op jit(solution)/shard_map/ppermute | solution.py:358
  53.2 13.9 %copy-start.11 = (f32[4]{0:T(128)S(1)}, f32[4]{0:T(128)}, u32[]{:S(2)}) copy-start(f32[4]{0:T(128)} %param.8) | copy-start | bytes 52
  65.1 10.6 %collective-permute-start.7 = (bf16[256,1024]{1,0:T(8,128)(2,1)S(1)}, bf16[256,1024]{1,0:T(8,128)(2,1)S(1)}, u32[]{:S(2)}, u32[]{:S(2)}) collective-permute-start(bf16[256,1024]{1,0:T(8,128)(2,1)S(1)} %constant_dynamic-update-slice_fusion.own_ref), channel_id=1, source_target_pairs={{8,0},{16,8},{24,16},{32,24},{40,32},{48,40},{56,48},{64,56},{72,6... | collective-permute-start | bytes 1572872 | tf_op jit(solution)/shard_map/ppermute | solution.py:358
  67.1 16.3 %collective-permute-start.8 = (bf16[256,1024]{1,0:T(8,128)(2,1)S(1)}, bf16[256,1024]{1,0:T(8,128)(2,1)S(1)}, u32[]{:S(2)}, u32[]{:S(2)}) collective-permute-start(bf16[256,1024]{1,0:T(8,128)(2,1)S(1)} %constant_dynamic-update-slice_fusion.own_ref), channel_id=1, source_target_pairs={{504,0},{0,8},{8,16},{16,24},{24,32},{32,40},{40,48},{48,56},{56,6... | collective-permute-start | bytes 1572872 | tf_op jit(solution)/shard_map/ppermute | solution.py:358
  75.8 9.7 %copy-start.6 = (bf16[256,1024]{1,0:T(8,128)(2,1)S(1)}, bf16[256,1024]{1,0:T(8,128)(2,1)}, u32[]{:S(2)}) copy-start(bf16[256,1024]{1,0:T(8,128)(2,1)} %copy-done.5) | copy-start | bytes 1572868
  75.8 9.6 %copy-start.1 = (bf16[1024,512]{1,0:T(8,128)(2,1)S(1)}, bf16[1024,512]{1,0:T(8,128)(2,1)}, u32[]{:S(2)}) copy-start(bf16[1024,512]{1,0:T(8,128)(2,1)} %k_ref.5) | copy-start | bytes 3145732
  75.8 9.6 %copy-start.3 = (bf16[1024,512]{1,0:T(8,128)(2,1)S(1)}, bf16[1024,512]{1,0:T(8,128)(2,1)}, u32[]{:S(2)}) copy-start(bf16[1024,512]{1,0:T(8,128)(2,1)} %q_ref.7) | copy-start | bytes 3145732
  75.8 19.5 %collective-permute-start.9 = (bf16[384,512]{1,0:T(8,128)(2,1)S(1)}, bf16[384,512]{1,0:T(8,128)(2,1)S(1)}, u32[]{:S(2)}, u32[]{:S(2)}) collective-permute-start(bf16[384,512]{1,0:T(8,128)(2,1)S(1)} %pad_maximum_fusion), channel_id=1, source_target_pairs={{8,0},{16,8},{24,16},{32,24},{40,32},{48,40},{56,48},{64,56},{72,6... | collective-permute-start | bytes 1179656 | tf_op jit(solution)/shard_map/ppermute | solution.py:358
  83.5 11.8 %collective-permute-start.10 = (bf16[384,512]{1,0:T(8,128)(2,1)S(1)}, bf16[384,512]{1,0:T(8,128)(2,1)S(1)}, u32[]{:S(2)}, u32[]{:S(2)}) collective-permute-start(bf16[384,512]{1,0:T(8,128)(2,1)S(1)} %pad_maximum_fusion.1), channel_id=1, source_target_pairs={{504,0},{0,8},{8,16},{16,24},{24,32},{32,40},{40,48},{48,56},{56,6... | collective-permute-start | bytes 1179656 | tf_op jit(solution)/shard_map/ppermute | solution.py:358
  89.4 1.0 copy-start.9
  90.4 1.0 copy-start.10
  95.3 8.4 %copy-start.7 = (f32[1024,256]{1,0:T(8,128)}, f32[1024,256]{1,0:T(8,128)S(1)}, u32[]{:S(2)}) copy-start(f32[1024,256]{1,0:T(8,128)S(1)} %get-tuple-element.26.acc_ref) | copy-start | bytes 3145732
  95.3 8.4 %copy-start.8 = (f32[1024,256]{1,0:T(8,128)}, f32[1024,256]{1,0:T(8,128)S(1)}, u32[]{:S(2)}) copy-start(f32[1024,256]{1,0:T(8,128)S(1)} %get-tuple-element.27.ml_ref) | copy-start | bytes 3145732
  95.3 0.7 copy-start.4

commit v5 on v4

--- a/solution.py
+++ b/solution.py
@@ -22,7 +22,7 @@
 NT = (((1,), (1,)), ((), ()))
 BF = jnp.bfloat16
 F32 = jnp.float32
-VMEM_LIMIT = 48 * 1024 * 1024
+VMEM_LIMIT = 20 * 1024 * 1024
 
 
 def params():
@@ -196,12 +196,12 @@
     dev = dev_ref[0]
     y, own_pair = dev % Y, dev // 2
     lane = lax.broadcasted_iota(jnp.int32, (1, 256), 1)
-    order = lane // 16
-    doubled = 8 * (order % 2) + 4 * (order // 2 % 2) + 2 * (order // 4 % 2) + order // 8
+    outer, inner = lane // 64, lane // 16 % 4
+    away = jnp.where(outer == 3, -1, outer) + 4 * inner + Z
     far_bias = []
     for ahead in (0, 1, 2 - 4 * pair, -1):
         holder = (dev + ahead + seq_size) % seq_size
-        src_pair = ((holder // Y + doubled) % Z * Y + holder % Y) // 2
+        src_pair = ((holder // Y + away) % Z * Y + holder % Y) // 2
         seen = (src_pair < own_pair - 1) | (src_pair > own_pair + 1)
         far_bias.append(jnp.where(seen, 0.0, GONE).astype(F32))
     lane64 = lax.broadcasted_iota(jnp.int32, (1, 64), 1)
@@ -371,23 +371,29 @@
     up, down, one, two, three = prep(keys, values)
 
     column = three
-    for shift in (8, 4, 2, 1):
-        column = jnp.concatenate([column, fetch(column, "seq", lambda i: i + Y * shift)], axis=0)
+    for shifts in ((4, 8, -4), (1, 2, -1)):
+        parts = [fetch(column, "seq", lambda i, s=s: i + Y * s) for s in shifts]
+        column = jnp.concatenate([column] + parts, axis=0)
     from_up = fetch(up, "seq", lambda i: i - 1)
     from_down = fetch(down, "seq", lambda i: i + 1)
     third = fetch(two, "seq", lambda i: i + 3 if i % 2 == 0 else i - 3)
-    after = fetch(column, "seq", lambda i: i + 1)
-    before = fetch(column, "seq", lambda i: i - 1)
-
-    def relay(half, edge):
-        return jnp.concatenate([half, edge[256:, :512], edge[256:, 512:]], axis=0)
-
-    high = fetch(relay(after[:, :512], from_down), "seq", lambda i: i + 1)
-    low = fetch(relay(before[:, 512:], from_up), "seq", lambda i: i - 1)
-
     near_args = (queries, keys, values, from_up, from_down, one)
     acc_a, ml_a = near(0, seq_size, dev, temp, *near_args)
     acc_b, ml_b = near(1, seq_size, dev, temp, *near_args)
+
+    column, third, acc_a, ml_a = lax.optimization_barrier((column, third, acc_a, ml_a))
+    after = fetch(column, "seq", lambda i: i + 1)
+    before = fetch(column, "seq", lambda i: i - 1)
+
+    def relay(half, edge):
+        return jnp.concatenate([half, edge[256:, :512], edge[256:, 512:]], axis=0)
+
+    high = relay(after[:, :512], from_down)
+    low = relay(before[:, 512:], from_up)
+    high, low, acc_b, ml_b = lax.optimization_barrier((high, low, acc_b, ml_b))
+    high = fetch(high, "seq", lambda i: i + 1)
+    low = fetch(low, "seq", lambda i: i - 1)
+
     gain = norm_gain.reshape(1, 512)
     blocks = (two, from_up, from_down, third, column, after, before, high, low)
     att_a, sum_a = far(0, seq_size, dev, temp, queries, acc_a, ml_a, gain, blocks, None)

time: 129 us -> 148 us (1.15)
  waiting for transfers between devices: 19.9 us -> 31.4 us
  local copies, waits for them, and re-layouts: 5.27 us -> 11.1 us
  starting transfers between devices: 60.4 us -> 62.5 us
  Pallas kernels: 27.3 us -> 25.8 us
    ppermute x11 -> x13, waiting for transfers between devices: 19.9 us -> 31.4 us  [fetch(): lax.ppermute(value, axis, [(source(i) % count, i) for i in range(count)])]
    unnamed x29 -> x26, local copies, waits for them, and re-layouts: 5.18 us -> 10.4 us
    ppermute x11 -> x13, starting transfers between devices: 60.4 us -> 62.5 us  [fetch(): lax.ppermute(value, axis, [(source(i) % count, i) for i in range(count)])]
  transfers between devices with their start and end apart: 11 -> 13, of which waited for: 4 -> 6; matrix products, arithmetic and copies ran while one was open for 0% -> 3% of each run, Pallas kernels for 6% -> 5%
where the time goes in v5:
time: 148 us; the launch traced here: 147 us
  starting transfers between devices  62.5 us (42%)
  waiting for transfers between devices  31.4 us (21%)
  Pallas kernels  25.8 us (17%)
  blocking collectives  15.7 us (11%)
  local copies, waits for them, and re-layouts  11.1 us (8%)
    ppermute x13, starting transfers between devices, fetch(): lax.ppermute(value, axis, [(source(i) % count, i) for i in range(count)])  62.5 us
    ppermute x13, waiting for transfers between devices, fetch(): lax.ppermute(value, axis, [(source(i) % count, i) for i in range(count)])  31.4 us
    all_to_all x1, blocking collectives, gathered(): return lax.all_to_all(many, axis, 0, 0, tiled=True)  15.7 us
    pallas_call x2, Pallas kernels, far(): pl.pallas_call(functools.partial(far_kernel, pair, seq_size, partial is n...  14.3 us
    unnamed x26, local copies, waits for them, and re-layouts  10.4 us
    pallas_call x2, Pallas kernels, near(): pl.pallas_call(functools.partial(near_kernel, pair, seq_size), grid=(2,),...  7.37 us
  transfers between devices with their start and end apart: 13, of which 6 were waited for; matrix products, arithmetic and copies ran while one was open for 3% of the time, Pallas kernels for 5%

profile of v5, /device:TPU:1, one launch (start us, length us, event | category | flops | bytes accessed | tf_op | source)
XLA Modules:
  0.0 146.8 jit_solution(17435329621806354479)
XLA Ops:
  0.0 0.0 copy-start
  0.0 1.2 copy-done
  1.2 0.0 copy-start.2
  1.2 1.2 copy-done.2
  2.5 0.0 copy-start.9
  2.5 2.3 %shard_map.55 = (bf16[320,1024]{1,0:T(8,128)(2,1)}, bf16[320,1024]{1,0:T(8,128)(2,1)S(1)}, bf16[256,1024]{1,0:T(8,128)(2,1)S(1)}, bf16[64,1024]{1,0:T(8,128)(2,1)}, bf16[16,1024]{1,0:T(8,128)(2,1)S(1)}) custom-call(bf16[1024,512]{1,0:T(8,128)(2,1)S(1)} %copy-done, bf16[1024,512]{1,0:T(8,128)(2,1)S(1)} %copy-done.2), custom_call_target="tpu_custom_call" | custom-call | flops 700000000 | bytes 5000000 | tf_op jit(solution)/shard_map/pallas_call | solution.py:64
  4.7 0.0 copy-start.7
  4.7 0.8 copy-done.7
  5.5 0.0 copy-start.1
  5.5 9.8 %collective-permute-start.2 = (bf16[16,1024]{1,0:T(8,128)(2,1)S(1)}, bf16[16,1024]{1,0:T(8,128)(2,1)S(1)}, u32[]{:S(2)}, u32[]{:S(2)}) collective-permute-start(bf16[16,1024]{1,0:T(8,128)(2,1)S(1)} %get-tuple-element.26), channel_id=1, source_target_pairs={{384,0},{392,8},{400,16},{408,24},{416,32},{424,40},{432,48},{440,... | collective-permute-start | bytes 98312 | tf_op jit(solution)/shard_map/ppermute | solution.py:358
  15.3 10.6 %collective-permute-start.1 = (bf16[16,1024]{1,0:T(8,128)(2,1)S(1)}, bf16[16,1024]{1,0:T(8,128)(2,1)S(1)}, u32[]{:S(2)}, u32[]{:S(2)}) collective-permute-start(bf16[16,1024]{1,0:T(8,128)(2,1)S(1)} %get-tuple-element.26), channel_id=1, source_target_pairs={{256,0},{264,8},{272,16},{280,24},{288,32},{296,40},{304,48},{312,... | collective-permute-start | bytes 98312 | tf_op jit(solution)/shard_map/ppermute | solution.py:358
  25.9 5.2 %collective-permute-start = (bf16[16,1024]{1,0:T(8,128)(2,1)S(1)}, bf16[16,1024]{1,0:T(8,128)(2,1)S(1)}, u32[]{:S(2)}, u32[]{:S(2)}) collective-permute-start(bf16[16,1024]{1,0:T(8,128)(2,1)S(1)} %get-tuple-element.26), channel_id=1, source_target_pairs={{128,0},{136,8},{144,16},{152,24},{160,32},{168,40},{176,48},{184,... | collective-permute-start | bytes 98312 | tf_op jit(solution)/shard_map/ppermute | solution.py:358
  31.1 4.6 %collective-permute-start.6 = (bf16[64,1024]{1,0:T(8,128)(2,1)}, bf16[64,1024]{1,0:T(8,128)(2,1)}, u32[]{:S(2)}, u32[]{:S(2)}) collective-permute-start(bf16[64,1024]{1,0:T(8,128)(2,1)} %get-tuple-element.27.two_ref), channel_id=1, source_target_pairs={{24,0},{496,8},{40,16},{0,24},{56,32},{16,40},{72,48},{32,56},{88,... | collective-permute-start | bytes 393224 | tf_op jit(solution)/shard_map/ppermute | solution.py:358
  35.8 1.9 %collective-permute-start.7 = (bf16[320,1024]{1,0:T(8,128)(2,1)}, bf16[320,1024]{1,0:T(8,128)(2,1)S(1)}, u32[]{:S(2)}, u32[]{:S(2)}) collective-permute-start(bf16[320,1024]{1,0:T(8,128)(2,1)} %get-tuple-element.28), channel_id=1, source_target_pairs={{504,0},{0,8},{8,16},{16,24},{24,32},{32,40},{40,48},{48,56},{56,6... | collective-permute-start | bytes 1966088 | tf_op jit(solution)/shard_map/ppermute | solution.py:358
  37.7 0.6 constant_dynamic-update-slice_fusion.3
  38.3 0.0 collective-permute-done
  38.3 6.7 %collective-permute-start.8 = (bf16[320,1024]{1,0:T(8,128)(2,1)S(1)}, bf16[320,1024]{1,0:T(8,128)(2,1)S(1)}, u32[]{:S(2)}, u32[]{:S(2)}) collective-permute-start(bf16[320,1024]{1,0:T(8,128)(2,1)S(1)} %get-tuple-element.29), channel_id=1, source_target_pairs={{8,0},{16,8},{24,16},{32,24},{40,32},{48,40},{56,48},{64,56},{72,6... | collective-permute-start | bytes 1966088 | tf_op jit(solution)/shard_map/ppermute | solution.py:358
  45.0 0.6 constant_dynamic-update-slice_fusion.2
  45.6 0.0 collective-permute-done.1
  45.6 0.6 constant_dynamic-update-slice_fusion.1
  46.2 0.0 collective-permute-done.2
  46.2 0.6 constant_dynamic-update-slice_fusion
  46.8 1.9 %collective-permute-start.4 = (bf16[64,1024]{1,0:T(8,128)(2,1)}, bf16[64,1024]{1,0:T(8,128)(2,1)}, u32[]{:S(2)}, u32[]{:S(2)}) collective-permute-start(bf16[64,1024]{1,0:T(8,128)(2,1)} %get-tuple-element.51), channel_id=1, source_target_pairs={{64,0},{72,8},{80,16},{88,24},{96,32},{104,40},{112,48},{120,56},{... | collective-permute-start | bytes 393224 | tf_op jit(solution)/shard_map/ppermute | solution.py:358
  48.8 1.9 %collective-permute-start.3 = (bf16[64,1024]{1,0:T(8,128)(2,1)}, bf16[64,1024]{1,0:T(8,128)(2,1)}, u32[]{:S(2)}, u32[]{:S(2)}) collective-permute-start(bf16[64,1024]{1,0:T(8,128)(2,1)} %get-tuple-element.51), channel_id=1, source_target_pairs={{32,0},{40,8},{48,16},{56,24},{64,32},{72,40},{80,48},{88,56},{96,... | collective-permute-start | bytes 393224 | tf_op jit(solution)/shard_map/ppermute | solution.py:358
  50.7 0.0 copy-done.9
  50.7 14.6 %collective-permute-done.3 = bf16[64,1024]{1,0:T(8,128)(2,1)} collective-permute-done((bf16[64,1024]{1,0:T(8,128)(2,1)}, bf16[64,1024]{1,0:T(8,128)(2,1)}, u32[]{:S(2)}, u32[]{:S(2)}) %collective-permute-start.3) | collective-permute-done | bytes 131104 | tf_op jit(solution)/shard_map/ppermute | solution.py:358
  65.3 1.9 %collective-permute-start.5 = (bf16[64,1024]{1,0:T(8,128)(2,1)}, bf16[64,1024]{1,0:T(8,128)(2,1)S(1)}, u32[]{:S(2)}, u32[]{:S(2)}) collective-permute-start(bf16[64,1024]{1,0:T(8,128)(2,1)} %get-tuple-element.51), channel_id=1, source_target_pairs={{480,0},{488,8},{496,16},{504,24},{0,32},{8,40},{16,48},{24,56},{3... | collective-permute-start | bytes 393224 | tf_op jit(solution)/shard_map/ppermute | solution.py:358
  67.2 0.9 constant_dynamic-update-slice_fusion.6
  68.2 0.0 collective-permute-done.4
  68.2 0.9 constant_dynamic-update-slice_fusion.5
  69.1 4.0 %collective-permute-done.5 = bf16[64,1024]{1,0:T(8,128)(2,1)S(1)} collective-permute-done((bf16[64,1024]{1,0:T(8,128)(2,1)}, bf16[64,1024]{1,0:T(8,128)(2,1)S(1)}, u32[]{:S(2)}, u32[]{:S(2)}) %collective-permute-start.5) | collective-permute-done | bytes 131104 | tf_op jit(solution)/shard_map/ppermute | solution.py:358
  73.0 0.0 collective-permute-done.7.upk.upv.up_ref
  73.1 0.0 collective-permute-done.8.dnk.dnv.down_ref
  73.1 0.0 copy-done.1
  73.1 0.0 copy-start.3
  73.1 1.2 copy-done.3
  74.3 0.0 copy-start.4
  74.3 1.2 copy-done.4
  75.5 0.0 copy-start.8
  75.5 1.0 copy-done.8
  76.6 3.7 %shard_map.56 = (f32[1024,256]{1,0:T(8,128)S(1)}, f32[1024,256]{1,0:T(8,128)S(1)}) custom-call(s32[1]{0:T(128)} %bitcast.dev_ref, f32[4]{0:T(128)S(1)} %broadcast_multiply_fusion.temp_ref, bf16[1024,512]{1,0:T(8,128)(2,1)S(1)} %copy-done.4, bf16[1024,512]{1,0:T(8,128)(2,1)S(1)} %copy-done.1, bf16[1024,512]{1,0:T(8,128)(2,1)S(1)} %copy-done.3, ...), custom_call_target="tpu_custom_call" | custom-call | flops 4000000000 | bytes 6000000 | tf_op jit(solution)/shard_map/pallas_call | solution.py:172
  80.2 0.0 collective-permute-done.6.third_ref
  80.3 1.9 %collective-permute-start.10 = (bf16[256,1024]{1,0:T(8,128)(2,1)S(1)}, bf16[256,1024]{1,0:T(8,128)(2,1)S(1)}, u32[]{:S(2)}, u32[]{:S(2)}) collective-permute-start(bf16[256,1024]{1,0:T(8,128)(2,1)S(1)} %constant_dynamic-update-slice_fusion.4.own_ref), channel_id=1, source_target_pairs={{504,0},{0,8},{8,16},{16,24},{24,32},{32,40},{40,48},{48,56},{56,6... | collective-permute-start | bytes 1572872 | tf_op jit(solution)/shard_map/ppermute | solution.py:358
  82.2 6.7 %collective-permute-start.9 = (bf16[256,1024]{1,0:T(8,128)(2,1)S(1)}, bf16[256,1024]{1,0:T(8,128)(2,1)S(1)}, u32[]{:S(2)}, u32[]{:S(2)}) collective-permute-start(bf16[256,1024]{1,0:T(8,128)(2,1)S(1)} %constant_dynamic-update-slice_fusion.4.own_ref), channel_id=1, source_target_pairs={{8,0},{16,8},{24,16},{32,24},{40,32},{48,40},{56,48},{64,56},{72,6... | collective-permute-start | bytes 1572872 | tf_op jit(solution)/shard_map/ppermute | solution.py:358
  88.9 3.7 %shard_map.57 = (f32[1024,256]{1,0:T(8,128)S(1)}, f32[1024,256]{1,0:T(8,128)S(1)}) custom-call(s32[1]{0:T(128)} %bitcast.dev_ref, f32[4]{0:T(128)S(1)} %broadcast_multiply_fusion.temp_ref, bf16[1024,512]{1,0:T(8,128)(2,1)S(1)} %copy-done.4, bf16[1024,512]{1,0:T(8,128)(2,1)S(1)} %copy-done.1, bf16[1024,512]{1,0:T(8,128)(2,1)S(1)} %copy-done.3, ...), custom_call_target="tpu_custom_call" | custom-call | flops 4000000000 | bytes 6000000 | tf_op jit(solution)/shard_map/pallas_call | solution.py:172
  92.6 2.1 %collective-permute-done.10.before_ref = bf16[256,1024]{1,0:T(8,128)(2,1)S(1)} collective-permute-done((bf16[256,1024]{1,0:T(8,128)(2,1)S(1)}, bf16[256,1024]{1,0:T(8,128)(2,1)S(1)}, u32[]{:S(2)}, u32[]{:S(2)}) %collective-permute-start.10) | collective-permute-done | bytes 524320 | tf_op jit(solution)/shard_map/ppermute | solution.py:358
  94.7 0.0 copy-start.5
  94.8 0.8 collective-permute-done.9.after_ref
  95.7 0.0 copy-start.6
  95.7 7.4 %collective-permute-start.11 = (bf16[384,512]{1,0:T(8,128)(2,1)S(1)}, bf16[384,512]{1,0:T(8,128)(2,1)S(1)}, u32[]{:S(2)}, u32[]{:S(2)}) collective-permute-start(bf16[384,512]{1,0:T(8,128)(2,1)S(1)} %pad_maximum_fusion), channel_id=1, source_target_pairs={{8,0},{16,8},{24,16},{32,24},{40,32},{48,40},{56,48},{64,56},{72,6... | collective-permute-start | bytes 1179656 | tf_op jit(solution)/shard_map/ppermute | solution.py:358
  103.1 1.9 %collective-permute-start.12 = (bf16[384,512]{1,0:T(8,128)(2,1)S(1)}, bf16[384,512]{1,0:T(8,128)(2,1)S(1)}, u32[]{:S(2)}, u32[]{:S(2)}) collective-permute-start(bf16[384,512]{1,0:T(8,128)(2,1)S(1)} %pad_maximum_fusion.1), channel_id=1, source_target_pairs={{504,0},{0,8},{8,16},{16,24},{24,32},{32,40},{40,48},{48,56},{56,6... | collective-permute-start | bytes 1179656 | tf_op jit(solution)/shard_map/ppermute | solution.py:358
  105.0 2.8 %collective-permute-done.11.high_ref = bf16[384,512]{1,0:T(8,128)(2,1)S(1)} collective-permute-done((bf16[384,512]{1,0:T(8,128)(2,1)S(1)}, bf16[384,512]{1,0:T(8,128)(2,1)S(1)}, u32[]{:S(2)}, u32[]{:S(2)}) %collective-permute-start.11) | collective-permute-done | bytes 393248 | tf_op jit(solution)/shard_map/ppermute | solution.py:358
  107.8 7.1 %collective-permute-done.12.low_ref = bf16[384,512]{1,0:T(8,128)(2,1)S(1)} collective-permute-done((bf16[384,512]{1,0:T(8,128)(2,1)S(1)}, bf16[384,512]{1,0:T(8,128)(2,1)S(1)}, u32[]{:S(2)}, u32[]{:S(2)}) %collective-permute-start.12) | collective-permute-done | bytes 393248 | tf_op jit(solution)/shard_map/ppermute | solution.py:358
  114.9 0.0 copy-done.5
  114.9 0.0 copy-done.6
  115.0 7.2 %shard_map.58 = (f32[1024,256]{1,0:T(8,128)S(1)}, f32[1,1024]{1,0:T(1,128)S(1)}) custom-call(s32[1]{0:T(128)} %bitcast.dev_ref, f32[4]{0:T(128)S(1)} %broadcast_multiply_fusion.temp_ref, bf16[1024,512]{1,0:T(8,128)(2,1)S(1)} %copy-done.5, f32[1024,256]{1,0:T(8,128)S(1)} %get-tuple-element.33.acc_ref, f32[1024,256]{1,0:T(8,128)S(1)} %get-tuple-element.34.ml_ref, ...), custom_call_target="tpu_custom_call" | custom-call | flops 6000000000 | bytes 5000000 | tf_op jit(solution)/shard_map/pallas_call | solution.py:315
  122.1 7.1 %shard_map.59 = (f32[1024,256]{1,0:T(8,128)S(1)}, f32[1,1024]{1,0:T(1,128)S(1)}) custom-call(s32[1]{0:T(128)} %bitcast.dev_ref, f32[4]{0:T(128)S(1)} %broadcast_multiply_fusion.temp_ref, bf16[1024,512]{1,0:T(8,128)(2,1)S(1)} %copy-done.5, f32[1024,256]{1,0:T(8,128)S(1)} %get-tuple-element.42.acc_ref, f32[1024,256]{1,0:T(8,128)S(1)} %get-tuple-element.43.ml_ref, ...), custom_call_target="tpu_custom_call" | custom-call | flops 6000000000 | bytes 5000000 | tf_op jit(solution)/shard_map/pallas_call | solution.py:315
  129.3 15.7 %all_to_all.5 = f32[8,1,1024]{2,1,0:T(1,128)S(1)} all-to-all(f32[8,1,1024]{2,1,0:T(1,128)S(1)} %broadcast_in_dim.9), channel_id=1, replica_groups=mesh['seq'=64,'head'=8] {'head'}, dimensions={0} | all-to-all | bytes 65536 | tf_op jit(solution)/shard_map/all_to_all | solution.py:364
  144.9 1.8 %shard_map.60 = bf16[1024,512]{1,0:T(8,128)(2,1)} custom-call(f32[1024,256]{1,0:T(8,128)S(1)} %get-tuple-element.41.a_ref, f32[1024,256]{1,0:T(8,128)S(1)} %get-tuple-element.45.b_ref, f32[8,1024]{1,0:T(8,128)S(1)} %bitcast.6), custom_call_target="tpu_custom_call" | custom-call | flops 2000000 | bytes 3000000 | tf_op jit(solution)/shard_map/pallas_call | solution.py:345
  (10 shorter events, 0.2 us)
Async XLA Ops:
  0.0 1.2 copy-start
  1.2 1.2 copy-start.2
  2.5 48.2 %copy-start.9 = (f32[4]{0:T(128)S(1)}, f32[4]{0:T(128)}, u32[]{:S(2)}) copy-start(f32[4]{0:T(128)} %param.8) | copy-start | bytes 52
  4.7 0.8 copy-start.7
  5.5 67.5 %copy-start.1 = (bf16[1024,512]{1,0:T(8,128)(2,1)S(1)}, bf16[1024,512]{1,0:T(8,128)(2,1)}, u32[]{:S(2)}) copy-start(bf16[1024,512]{1,0:T(8,128)(2,1)} %k_ref.5) | copy-start | bytes 3145732
  5.5 40.7 %collective-permute-start.2 = (bf16[16,1024]{1,0:T(8,128)(2,1)S(1)}, bf16[16,1024]{1,0:T(8,128)(2,1)S(1)}, u32[]{:S(2)}, u32[]{:S(2)}) collective-permute-start(bf16[16,1024]{1,0:T(8,128)(2,1)S(1)} %get-tuple-element.26), channel_id=1, source_target_pairs={{384,0},{392,8},{400,16},{408,24},{416,32},{424,40},{432,48},{440,... | collective-permute-start | bytes 98312 | tf_op jit(solution)/shard_map/ppermute | solution.py:358
  15.3 30.3 %collective-permute-start.1 = (bf16[16,1024]{1,0:T(8,128)(2,1)S(1)}, bf16[16,1024]{1,0:T(8,128)(2,1)S(1)}, u32[]{:S(2)}, u32[]{:S(2)}) collective-permute-start(bf16[16,1024]{1,0:T(8,128)(2,1)S(1)} %get-tuple-element.26), channel_id=1, source_target_pairs={{256,0},{264,8},{272,16},{280,24},{288,32},{296,40},{304,48},{312,... | collective-permute-start | bytes 98312 | tf_op jit(solution)/shard_map/ppermute | solution.py:358
  25.9 12.4 %collective-permute-start = (bf16[16,1024]{1,0:T(8,128)(2,1)S(1)}, bf16[16,1024]{1,0:T(8,128)(2,1)S(1)}, u32[]{:S(2)}, u32[]{:S(2)}) collective-permute-start(bf16[16,1024]{1,0:T(8,128)(2,1)S(1)} %get-tuple-element.26), channel_id=1, source_target_pairs={{128,0},{136,8},{144,16},{152,24},{160,32},{168,40},{176,48},{184,... | collective-permute-start | bytes 98312 | tf_op jit(solution)/shard_map/ppermute | solution.py:358
  31.1 49.1 %collective-permute-start.6 = (bf16[64,1024]{1,0:T(8,128)(2,1)}, bf16[64,1024]{1,0:T(8,128)(2,1)}, u32[]{:S(2)}, u32[]{:S(2)}) collective-permute-start(bf16[64,1024]{1,0:T(8,128)(2,1)} %get-tuple-element.27.two_ref), channel_id=1, source_target_pairs={{24,0},{496,8},{40,16},{0,24},{56,32},{16,40},{72,48},{32,56},{88,... | collective-permute-start | bytes 393224 | tf_op jit(solution)/shard_map/ppermute | solution.py:358
  35.8 37.3 %collective-permute-start.7 = (bf16[320,1024]{1,0:T(8,128)(2,1)}, bf16[320,1024]{1,0:T(8,128)(2,1)S(1)}, u32[]{:S(2)}, u32[]{:S(2)}) collective-permute-start(bf16[320,1024]{1,0:T(8,128)(2,1)} %get-tuple-element.28), channel_id=1, source_target_pairs={{504,0},{0,8},{8,16},{16,24},{24,32},{32,40},{40,48},{48,56},{56,6... | collective-permute-start | bytes 1966088 | tf_op jit(solution)/shard_map/ppermute | solution.py:358
  38.3 34.7 %collective-permute-start.8 = (bf16[320,1024]{1,0:T(8,128)(2,1)S(1)}, bf16[320,1024]{1,0:T(8,128)(2,1)S(1)}, u32[]{:S(2)}, u32[]{:S(2)}) collective-permute-start(bf16[320,1024]{1,0:T(8,128)(2,1)S(1)} %get-tuple-element.29), channel_id=1, source_target_pairs={{8,0},{16,8},{24,16},{32,24},{40,32},{48,40},{56,48},{64,56},{72,6... | collective-permute-start | bytes 1966088 | tf_op jit(solution)/shard_map/ppermute | solution.py:358
  46.8 21.3 %collective-permute-start.4 = (bf16[64,1024]{1,0:T(8,128)(2,1)}, bf16[64,1024]{1,0:T(8,128)(2,1)}, u32[]{:S(2)}, u32[]{:S(2)}) collective-permute-start(bf16[64,1024]{1,0:T(8,128)(2,1)} %get-tuple-element.51), channel_id=1, source_target_pairs={{64,0},{72,8},{80,16},{88,24},{96,32},{104,40},{112,48},{120,56},{... | collective-permute-start | bytes 393224 | tf_op jit(solution)/shard_map/ppermute | solution.py:358
  48.8 16.6 %collective-permute-start.3 = (bf16[64,1024]{1,0:T(8,128)(2,1)}, bf16[64,1024]{1,0:T(8,128)(2,1)}, u32[]{:S(2)}, u32[]{:S(2)}) collective-permute-start(bf16[64,1024]{1,0:T(8,128)(2,1)} %get-tuple-element.51), channel_id=1, source_target_pairs={{32,0},{40,8},{48,16},{56,24},{64,32},{72,40},{80,48},{88,56},{96,... | collective-permute-start | bytes 393224 | tf_op jit(solution)/shard_map/ppermute | solution.py:358
  65.3 7.7 %collective-permute-start.5 = (bf16[64,1024]{1,0:T(8,128)(2,1)}, bf16[64,1024]{1,0:T(8,128)(2,1)S(1)}, u32[]{:S(2)}, u32[]{:S(2)}) collective-permute-start(bf16[64,1024]{1,0:T(8,128)(2,1)} %get-tuple-element.51), channel_id=1, source_target_pairs={{480,0},{488,8},{496,16},{504,24},{0,32},{8,40},{16,48},{24,56},{3... | collective-permute-start | bytes 393224 | tf_op jit(solution)/shard_map/ppermute | solution.py:358
  73.1 1.2 copy-start.3
  74.3 1.2 copy-start.4
  75.5 1.0 copy-start.8
  80.3 14.4 %collective-permute-start.10 = (bf16[256,1024]{1,0:T(8,128)(2,1)S(1)}, bf16[256,1024]{1,0:T(8,128)(2,1)S(1)}, u32[]{:S(2)}, u32[]{:S(2)}) collective-permute-start(bf16[256,1024]{1,0:T(8,128)(2,1)S(1)} %constant_dynamic-update-slice_fusion.4.own_ref), channel_id=1, source_target_pairs={{504,0},{0,8},{8,16},{16,24},{24,32},{32,40},{40,48},{48,56},{56,6... | collective-permute-start | bytes 1572872 | tf_op jit(solution)/shard_map/ppermute | solution.py:358
  82.2 13.4 %collective-permute-start.9 = (bf16[256,1024]{1,0:T(8,128)(2,1)S(1)}, bf16[256,1024]{1,0:T(8,128)(2,1)S(1)}, u32[]{:S(2)}, u32[]{:S(2)}) collective-permute-start(bf16[256,1024]{1,0:T(8,128)(2,1)S(1)} %constant_dynamic-update-slice_fusion.4.own_ref), channel_id=1, source_target_pairs={{8,0},{16,8},{24,16},{32,24},{40,32},{48,40},{56,48},{64,56},{72,6... | collective-permute-start | bytes 1572872 | tf_op jit(solution)/shard_map/ppermute | solution.py:358
  94.7 20.2 %copy-start.5 = (bf16[1024,512]{1,0:T(8,128)(2,1)S(1)}, bf16[1024,512]{1,0:T(8,128)(2,1)}, u32[]{:S(2)}) copy-start(bf16[1024,512]{1,0:T(8,128)(2,1)} %q_ref.7) | copy-start | bytes 3145732
  95.7 19.3 %copy-start.6 = (f32[512]{0:T(512)S(1)}, f32[512]{0:T(512)}, u32[]{:S(2)}) copy-start(f32[512]{0:T(512)} %param.9) | copy-start | bytes 6148
  95.7 12.1 %collective-permute-start.11 = (bf16[384,512]{1,0:T(8,128)(2,1)S(1)}, bf16[384,512]{1,0:T(8,128)(2,1)S(1)}, u32[]{:S(2)}, u32[]{:S(2)}) collective-permute-start(bf16[384,512]{1,0:T(8,128)(2,1)S(1)} %pad_maximum_fusion), channel_id=1, source_target_pairs={{8,0},{16,8},{24,16},{32,24},{40,32},{48,40},{56,48},{64,56},{72,6... | collective-permute-start | bytes 1179656 | tf_op jit(solution)/shard_map/ppermute | solution.py:358
  103.1 11.8 %collective-permute-start.12 = (bf16[384,512]{1,0:T(8,128)(2,1)S(1)}, bf16[384,512]{1,0:T(8,128)(2,1)S(1)}, u32[]{:S(2)}, u32[]{:S(2)}) collective-permute-start(bf16[384,512]{1,0:T(8,128)(2,1)S(1)} %pad_maximum_fusion.1), channel_id=1, source_target_pairs={{504,0},{0,8},{8,16},{16,24},{24,32},{32,40},{40,48},{48,56},{56,6... | collective-permute-start | bytes 1179656 | tf_op jit(solution)/shard_map/ppermute | solution.py:358

commit v6 on v3

--- a/solution.py
+++ b/solution.py
@@ -74,33 +74,12 @@
 
 
 def near_kernel(
-    pair, seq_size, dev_ref, temp_ref, q_all, k_all, v_all, up_all, down_all, one_all, two_all,
-    next_all, acc_all, ml_all, sa, sb, pa, pb,
+    pair, seq_size, dev_ref, temp_ref, q_ref, k_ref, v_ref,
+    upk, upv, dnk, dnv, onk, onv, twok, twov, nextk, nextv,
+    acc_ref, ml_ref, sa, sb, pa, pb,
 ):
-    def one_head(i, carry):
-        near_head(
-            pair, seq_size, i, dev_ref, temp_ref, q_all, k_all, v_all, up_all, down_all, one_all,
-            two_all, next_all, acc_all, ml_all, sa, sb, pa, pb,
-        )
-        return carry
-
-    lax.fori_loop(0, 2, one_head, 0)
-
-
-def near_head(
-    pair, seq_size, i, dev_ref, temp_ref, q_all, k_all, v_all, up_all, down_all, one_all, two_all,
-    next_all, acc_all, ml_all, sa, sb, pa, pb,
-):
-    def head_cols(ref, first):
-        return ref.at[:, pl.ds(pl.multiple_of(HEAD_DIM * (first + i), HEAD_DIM), HEAD_DIM)]
-
-    q_ref, k_ref, v_ref = [head_cols(ref, 2 * pair) for ref in (q_all, k_all, v_all)]
-    acc_ref, ml_ref = head_cols(acc_all, 0), head_cols(ml_all, 0)
-    edges = (up_all, down_all, one_all, two_all, next_all)
-    upk, dnk, onk, twok, nextk = [head_cols(ref, 4 * pair) for ref in edges]
-    upv, dnv, onv, twov, nextv = [head_cols(ref, 4 * pair + 2) for ref in edges]
     dev = dev_ref[0]
-    c = temp_ref[2 * pair + i]
+    c = temp_ref[2 * pair + pl.program_id(0)]
     z, y = dev // Y, dev % Y
 
     def gate(ok):
@@ -188,16 +167,27 @@
 def near(pair, seq_size, dev, temp, queries, keys, values, up, down, one, two, beyond):
     smem = pl.BlockSpec(memory_space=pltpu.SMEM)
 
-    whole = pl.BlockSpec(memory_space=pltpu.VMEM)
+    def own(rows):
+        return pl.BlockSpec((rows, HEAD_DIM), lambda i: (0, 2 * pair + i))
+
+    def packed(rows):
+        return [
+            pl.BlockSpec((rows, HEAD_DIM), lambda i: (0, 4 * pair + i)),
+            pl.BlockSpec((rows, HEAD_DIM), lambda i: (0, 4 * pair + 2 + i)),
+        ]
+
+    out = pl.BlockSpec((ROWS, HEAD_DIM), lambda i: (0, i))
     return pl.pallas_call(
         functools.partial(near_kernel, pair, seq_size),
-        in_specs=[smem, smem] + [whole] * 8,
-        out_specs=(whole, whole),
+        grid=(2,),
+        in_specs=[smem, smem, own(ROWS), own(ROWS), own(ROWS)]
+        + packed(256) + packed(256) + packed(256) + packed(256) + packed(128),
+        out_specs=(out, out),
         out_shape=(sds((ROWS, PAIR), F32), sds((ROWS, PAIR), F32)),
         scratch_shapes=[pltpu.VMEM((128, 1152), F32)] * 2 + [pltpu.VMEM((128, 1152), BF)] * 2,
         compiler_params=params(),
         cost_estimate=cost(2_000_000_000, 6_000_000, 2_500_000),
-    )(dev, temp, queries, keys, values, up, down, one, two, beyond)
+    )(dev, temp, queries, keys, values, up, up, down, down, one, one, two, two, beyond, beyond)
 
 
 CHUNK = 256
@@ -213,7 +203,7 @@
     dev = dev_ref[0]
     y, own_pair = dev % Y, dev // 2
     lane = lax.broadcasted_iota(jnp.int32, (1, 256), 1)
-    src_z = lane // 64 + 4 * (lane // 16 % 4)
+    src_z = lane // 16
     biases = []
     for k in range(4):
         src_pair = (src_z * Y + (y + k) % Y) // 2
@@ -347,6 +337,10 @@
     return lax.ppermute(value, axis, [(source(i) % count, i) for i in range(count)])
 
 
+def fetch_y(value, step):
+    return fetch(value, "seq", lambda i: i // Y * Y + (i + step) % Y)
+
+
 def gathered(value, axis):
     size = lax.axis_size(axis)
     many = jnp.broadcast_to(value[None], (size,) + value.shape)
@@ -354,8 +348,7 @@
 
 
 Y_RING = [[z * Y + y for y in range(Y)] for z in range(Z)]
-Z_APART = [[(a + 4 * b) * Y + y for b in range(4)] for a in range(4) for y in range(Y)]
-Z_NEXT = [[(a + 4 * b) * Y + y for a in range(4)] for b in range(4) for y in range(Y)]
+Z_RING = [[z * Y + y for z in range(Z)] for y in range(Y)]
 
 
 def joined(value, groups):
@@ -368,25 +361,27 @@
     temp = head_temp * F32(math.log2(math.e) / math.sqrt(HEAD_DIM))
     up, down, one, two, three = prep(keys, values)
 
+    group_two = joined(two, Y_RING)
+    up, down, three, group_two = lax.optimization_barrier((up, down, three, group_two))
     from_up = fetch(up, "seq", lambda i: i - 1)
     from_down = fetch(down, "seq", lambda i: i + 1)
-    group_two = joined(two, Y_RING)
     low_side = dev[0] % Y < 2
     other_half = jnp.where(low_side, group_two[128:], group_two[:128])
     beyond = fetch(other_half, "seq", lambda i: i - Y if i % Y < 2 else i + Y)
 
-    three, beyond = lax.optimization_barrier((three, beyond))
-    column = joined(three, Z_APART)
-    column, from_up, from_down = lax.optimization_barrier((column, from_up, from_down))
-    column = joined(column, Z_NEXT)
-    after = fetch(column, "seq", lambda i: i + 1)
-    before = fetch(column, "seq", lambda i: i - 1)
-    opposite_a = fetch(after[:, :512], "seq", lambda i: i + 1)
-    opposite_b = fetch(before[:, 512:], "seq", lambda i: i - 1)
-
+    column = joined(three, Z_RING)
     near_args = (queries, keys, values, from_up, from_down, one, group_two, beyond)
     acc_a, ml_a = near(0, seq_size, dev, temp, *near_args)
     acc_b, ml_b = near(1, seq_size, dev, temp, *near_args)
+    column, acc_a, ml_a = lax.optimization_barrier((column, acc_a, ml_a))
+    after = fetch_y(column, 1)
+    before = fetch_y(column, -1)
+    half_a, half_b, acc_b, ml_b = lax.optimization_barrier(
+        (after[:, :512], before[:, 512:], acc_b, ml_b)
+    )
+    opposite_a = fetch_y(half_a, 1)
+    opposite_b = fetch_y(half_b, -1)
+
     gain = norm_gain.reshape(1, 512)
     att_a, sum_a = far(0, dev, temp, queries, acc_a, ml_a, gain, (column, after, opposite_a, before), None)
     att_b, sums = far(1, dev, temp, queries, acc_b, ml_b, gain, (column, after, opposite_b, before), sum_a)

time: 145 us -> 126 us (0.87)
  waiting for transfers between devices: 14.2 us -> 4.89 us
  starting transfers between devices: 34.8 us -> 30.3 us
  blocking collectives: 66 us -> 62.3 us
    ppermute x7, waiting for transfers between devices: 14.2 us -> 4.89 us  [fetch(): lax.ppermute(value, axis, [(source(i) % count, i) for i in range(count)])]
    all_gather x3 -> x2, blocking collectives: 46.4 us -> 41.2 us  [joined(): lax.all_gather(value, 'seq', axis_index_groups=groups, axis=0, tiled=True)]
    ppermute x7, starting transfers between devices: 34.8 us -> 30.3 us  [fetch(): lax.ppermute(value, axis, [(source(i) % count, i) for i in range(count)])]
    pallas_call x2, Pallas kernels: 12.5 us -> 10.7 us  [near(): pl.pallas_call(functools.partial(near_kernel, pair, seq_size), grid=(2,),...]
    all_to_all x1, blocking collectives: 19.6 us -> 21.1 us  [gathered(): return lax.all_to_all(many, axis, 0, 0, tiled=True)]
  transfers between devices with their start and end apart: 7 -> 7, of which waited for: 2 -> 2; matrix products, arithmetic and copies ran while one was open for 0% -> 0% of each run, Pallas kernels for 12% -> 8%
where the time goes in v6:
time: 126 us; the launch traced here: 125 us
  blocking collectives  62.3 us (49%)
  starting transfers between devices  30.3 us (24%)
  Pallas kernels  25 us (20%)
  waiting for transfers between devices  4.89 us (4%)
  local copies, waits for them, and re-layouts  2.53 us (2%)
    all_gather x2, blocking collectives, joined(): lax.all_gather(value, 'seq', axis_index_groups=groups, axis=0, tiled=True)  41.2 us
    ppermute x7, starting transfers between devices, fetch(): lax.ppermute(value, axis, [(source(i) % count, i) for i in range(count)])  30.3 us
    all_to_all x1, blocking collectives, gathered(): return lax.all_to_all(many, axis, 0, 0, tiled=True)  21.1 us
    pallas_call x2, Pallas kernels, near(): pl.pallas_call(functools.partial(near_kernel, pair, seq_size), grid=(2,),...  10.7 us
    pallas_call x2, Pallas kernels, far(): pl.pallas_call(functools.partial(far_kernel, pair, before is not None), i...  10.1 us
    ppermute x7, waiting for transfers between devices, fetch(): lax.ppermute(value, axis, [(source(i) % count, i) for i in range(count)])  4.89 us
  transfers between devices with their start and end apart: 7, of which 2 were waited for; matrix products, arithmetic and copies ran while one was open for 0% of the time, Pallas kernels for 8%

profile of v6, /device:TPU:1, one launch (start us, length us, event | category | flops | bytes accessed | tf_op | source)
XLA Modules:
  0.0 125.3 jit_solution(3014968484270809093)
XLA Ops:
  0.0 0.0 copy-start.1
  0.0 1.2 copy-done.1
  1.2 0.0 copy-start.2
  1.2 1.2 copy-done.2
  2.5 2.4 %shard_map.55 = (bf16[256,1024]{1,0:T(8,128)(2,1)}, bf16[256,1024]{1,0:T(8,128)(2,1)}, bf16[256,1024]{1,0:T(8,128)(2,1)S(1)}, bf16[64,1024]{1,0:T(8,128)(2,1)S(1)}, bf16[16,1024]{1,0:T(8,128)(2,1)S(1)}) custom-call(bf16[1024,512]{1,0:T(8,128)(2,1)S(1)} %copy-done.1, bf16[1024,512]{1,0:T(8,128)(2,1)S(1)} %copy-done.2), custom_call_target="tpu_custom_call" | custom-call | flops 700000000 | bytes 5000000 | tf_op jit(solution)/shard_map/pallas_call | solution.py:62
  4.8 0.0 copy-start
  4.8 11.4 %all_gather.6.twok.twov = bf16[256,1024]{1,0:T(8,128)(2,1)S(1)} all-gather(bf16[64,1024]{1,0:T(8,128)(2,1)S(1)} %get-tuple-element.32), channel_id=1, replica_groups={{0,8,16,24},{32,40,48,56},{64,72,80,88},{96,104,112,120},{128,136,144,1..., dimensions={0}, use_global_device_ids=true | all-gather | bytes 655360 | tf_op jit(solution)/shard_map/all_gather | solution.py:355
  16.2 2.9 %collective-permute-start = (bf16[256,1024]{1,0:T(8,128)(2,1)}, bf16[256,1024]{1,0:T(8,128)(2,1)S(1)}, u32[]{:S(2)}, u32[]{:S(2)}) collective-permute-start(bf16[256,1024]{1,0:T(8,128)(2,1)} %get-tuple-element.34), channel_id=1, source_target_pairs={{504,0},{0,8},{8,16},{16,24},{24,32},{32,40},{40,48},{48,56},{56,6... | collective-permute-start | bytes 1572872 | tf_op jit(solution)/shard_map/ppermute | solution.py:337
  19.1 12.1 %collective-permute-start.1 = (bf16[256,1024]{1,0:T(8,128)(2,1)}, bf16[256,1024]{1,0:T(8,128)(2,1)S(1)}, u32[]{:S(2)}, u32[]{:S(2)}) collective-permute-start(bf16[256,1024]{1,0:T(8,128)(2,1)} %get-tuple-element.35), channel_id=1, source_target_pairs={{8,0},{16,8},{24,16},{32,24},{40,32},{48,40},{56,48},{64,56},{72,6... | collective-permute-start | bytes 1572872 | tf_op jit(solution)/shard_map/ppermute | solution.py:337
  31.2 0.0 copy-start.4
  31.2 1.9 %collective-permute-start.2 = (bf16[128,1024]{1,0:T(8,128)(2,1)S(1)}, bf16[128,1024]{1,0:T(8,128)(2,1)S(1)}, u32[]{:S(2)}, u32[]{:S(2)}) collective-permute-start(bf16[128,1024]{1,0:T(8,128)(2,1)S(1)} %slice_select_fusion), channel_id=1, source_target_pairs={{480,0},{488,8},{48,16},{56,24},{0,32},{8,40},{80,48},{88,56},{32,... | collective-permute-start | bytes 786440 | tf_op jit(solution)/shard_map/ppermute | solution.py:337
  33.2 0.0 copy-done.4
  33.2 29.8 %all_gather.7.f0 = bf16[256,1024]{1,0:T(8,128)(2,1)S(1)} all-gather(bf16[16,1024]{1,0:T(8,128)(2,1)S(1)} %get-tuple-element.33), channel_id=1, replica_groups={{0,32,64,96,128,160,192,224,256,288,320,352,384,416,448,480},{8,40,72,1..., dimensions={0}, use_global_device_ids=true | all-gather | bytes 557056 | tf_op jit(solution)/shard_map/all_gather | solution.py:355
  63.0 0.0 collective-permute-done.2.nextk.nextv
  63.0 0.0 collective-permute-done.upk.upv
  63.0 0.0 collective-permute-done.1.dnk.dnv
  63.0 0.0 copy-done
  63.0 5.4 %shard_map.56 = (f32[1024,256]{1,0:T(8,128)S(1)}, f32[1024,256]{1,0:T(8,128)S(1)}) custom-call(s32[1]{0:T(128)} %bitcast.dev_ref, f32[4]{0:T(128)S(1)} %broadcast_multiply_fusion.temp_ref, bf16[1024,512]{1,0:T(8,128)(2,1)S(1)} %copy-done, bf16[1024,512]{1,0:T(8,128)(2,1)} %k_ref.5, bf16[1024,512]{1,0:T(8,128)(2,1)} %v_ref.5, ...), custom_call_target="tpu_custom_call" | custom-call | flops 2000000000 | bytes 6000000 | tf_op jit(solution)/shard_map/pallas_call | solution.py:180
  68.4 1.9 %collective-permute-start.4 = (bf16[256,1024]{1,0:T(8,128)(2,1)S(1)}, bf16[256,1024]{1,0:T(8,128)(2,1)S(1)}, u32[]{:S(2)}, u32[]{:S(2)}) collective-permute-start(bf16[256,1024]{1,0:T(8,128)(2,1)S(1)} %all_gather.7.f0), channel_id=1, source_target_pairs={{24,0},{0,8},{8,16},{16,24},{56,32},{32,40},{40,48},{48,56},{88,64... | collective-permute-start | bytes 1572872 | tf_op jit(solution)/shard_map/ppermute | solution.py:337
  70.3 4.6 %collective-permute-start.3 = (bf16[256,1024]{1,0:T(8,128)(2,1)S(1)}, bf16[256,1024]{1,0:T(8,128)(2,1)S(1)}, u32[]{:S(2)}, u32[]{:S(2)}) collective-permute-start(bf16[256,1024]{1,0:T(8,128)(2,1)S(1)} %all_gather.7.f0), channel_id=1, source_target_pairs={{8,0},{16,8},{24,16},{0,24},{40,32},{48,40},{56,48},{32,56},{72,64... | collective-permute-start | bytes 1572872 | tf_op jit(solution)/shard_map/ppermute | solution.py:337
  74.9 5.4 %shard_map.57 = (f32[1024,256]{1,0:T(8,128)S(1)}, f32[1024,256]{1,0:T(8,128)S(1)}) custom-call(s32[1]{0:T(128)} %bitcast.dev_ref, f32[4]{0:T(128)S(1)} %broadcast_multiply_fusion.temp_ref, bf16[1024,512]{1,0:T(8,128)(2,1)S(1)} %copy-done, bf16[1024,512]{1,0:T(8,128)(2,1)} %k_ref.5, bf16[1024,512]{1,0:T(8,128)(2,1)} %v_ref.5, ...), custom_call_target="tpu_custom_call" | custom-call | flops 2000000000 | bytes 6000000 | tf_op jit(solution)/shard_map/pallas_call | solution.py:180
  80.3 0.0 collective-permute-done.4.f3
  80.3 0.7 collective-permute-done.3.f1
  81.0 0.0 copy-start.3
  81.0 5.0 %collective-permute-start.5 = (bf16[256,512]{1,0:T(8,128)(2,1)S(1)}, bf16[256,512]{1,0:T(8,128)(2,1)S(1)}, u32[]{:S(2)}, u32[]{:S(2)}) collective-permute-start(bf16[256,512]{1,0:T(8,128)(2,1)S(1)} %slice.16), channel_id=1, source_target_pairs={{8,0},{16,8},{24,16},{0,24},{40,32},{48,40},{56,48},{32,56},{72,64... | collective-permute-start | bytes 786440 | tf_op jit(solution)/shard_map/ppermute | solution.py:337
  86.1 1.9 %collective-permute-start.6 = (bf16[256,512]{1,0:T(8,128)(2,1)S(1)}, bf16[256,512]{1,0:T(8,128)(2,1)S(1)}, u32[]{:S(2)}, u32[]{:S(2)}) collective-permute-start(bf16[256,512]{1,0:T(8,128)(2,1)S(1)} %slice.17), channel_id=1, source_target_pairs={{24,0},{0,8},{8,16},{16,24},{56,32},{32,40},{40,48},{48,56},{88,64... | collective-permute-start | bytes 786440 | tf_op jit(solution)/shard_map/ppermute | solution.py:337
  88.0 4.2 %collective-permute-done.5.f2 = bf16[256,512]{1,0:T(8,128)(2,1)S(1)} collective-permute-done((bf16[256,512]{1,0:T(8,128)(2,1)S(1)}, bf16[256,512]{1,0:T(8,128)(2,1)S(1)}, u32[]{:S(2)}, u32[]{:S(2)}) %collective-permute-start.5) | collective-permute-done | bytes 262176 | tf_op jit(solution)/shard_map/ppermute | solution.py:337
  92.2 0.0 copy-done.3
  92.2 5.0 %shard_map.58 = (f32[1024,256]{1,0:T(8,128)S(1)}, f32[1,1024]{1,0:T(1,128)S(1)}) custom-call(s32[1]{0:T(128)} %bitcast.dev_ref, f32[4]{0:T(128)S(1)} %broadcast_multiply_fusion.temp_ref, bf16[1024,512]{1,0:T(8,128)(2,1)S(1)} %copy-done, f32[1024,256]{1,0:T(8,128)S(1)} %get-tuple-element.40.acc_ref, f32[1024,256]{1,0:T(8,128)S(1)} %get-tuple-element.41.ml_ref, ...), custom_call_target="tpu_custom_call" | custom-call | flops 1200000000 | bytes 5000000 | tf_op jit(solution)/shard_map/pallas_call | solution.py:294
  97.2 0.0 collective-permute-done.6.f2
  97.2 5.1 %shard_map.59 = (f32[1024,256]{1,0:T(8,128)S(1)}, f32[1,1024]{1,0:T(1,128)S(1)}) custom-call(s32[1]{0:T(128)} %bitcast.dev_ref, f32[4]{0:T(128)S(1)} %broadcast_multiply_fusion.temp_ref, bf16[1024,512]{1,0:T(8,128)(2,1)S(1)} %copy-done, f32[1024,256]{1,0:T(8,128)S(1)} %get-tuple-element.47.acc_ref, f32[1024,256]{1,0:T(8,128)S(1)} %get-tuple-element.48.ml_ref, ...), custom_call_target="tpu_custom_call" | custom-call | flops 1200000000 | bytes 5000000 | tf_op jit(solution)/shard_map/pallas_call | solution.py:294
  102.3 21.1 %all_to_all.5 = f32[8,1,1024]{2,1,0:T(1,128)S(1)} all-to-all(f32[8,1,1024]{2,1,0:T(1,128)S(1)} %broadcast_in_dim.9), channel_id=1, replica_groups=mesh['seq'=64,'head'=8] {'head'}, dimensions={0} | all-to-all | bytes 65536 | tf_op jit(solution)/shard_map/all_to_all | solution.py:347
  123.4 1.8 %shard_map.60 = bf16[1024,512]{1,0:T(8,128)(2,1)} custom-call(f32[1024,256]{1,0:T(8,128)S(1)} %get-tuple-element.46.a_ref, f32[1024,256]{1,0:T(8,128)S(1)} %get-tuple-element.51.b_ref, f32[8,1024]{1,0:T(8,128)S(1)} %bitcast.6), custom_call_target="tpu_custom_call" | custom-call | flops 2000000 | bytes 3000000 | tf_op jit(solution)/shard_map/pallas_call | solution.py:324
  (6 shorter events, 0.1 us)
Async XLA Ops:
  0.0 1.2 copy-start.1
  1.2 1.2 copy-start.2
  4.8 58.2 %copy-start = (bf16[1024,512]{1,0:T(8,128)(2,1)S(1)}, bf16[1024,512]{1,0:T(8,128)(2,1)}, u32[]{:S(2)}) copy-start(bf16[1024,512]{1,0:T(8,128)(2,1)} %q_ref.7) | copy-start | bytes 3145732
  16.2 46.8 %collective-permute-start = (bf16[256,1024]{1,0:T(8,128)(2,1)}, bf16[256,1024]{1,0:T(8,128)(2,1)S(1)}, u32[]{:S(2)}, u32[]{:S(2)}) collective-permute-start(bf16[256,1024]{1,0:T(8,128)(2,1)} %get-tuple-element.34), channel_id=1, source_target_pairs={{504,0},{0,8},{8,16},{16,24},{24,32},{32,40},{40,48},{48,56},{56,6... | collective-permute-start | bytes 1572872 | tf_op jit(solution)/shard_map/ppermute | solution.py:337
  19.1 43.9 %collective-permute-start.1 = (bf16[256,1024]{1,0:T(8,128)(2,1)}, bf16[256,1024]{1,0:T(8,128)(2,1)S(1)}, u32[]{:S(2)}, u32[]{:S(2)}) collective-permute-start(bf16[256,1024]{1,0:T(8,128)(2,1)} %get-tuple-element.35), channel_id=1, source_target_pairs={{8,0},{16,8},{24,16},{32,24},{40,32},{48,40},{56,48},{64,56},{72,6... | collective-permute-start | bytes 1572872 | tf_op jit(solution)/shard_map/ppermute | solution.py:337
  31.2 2.0 %copy-start.4 = (f32[4]{0:T(128)S(1)}, f32[4]{0:T(128)}, u32[]{:S(2)}) copy-start(f32[4]{0:T(128)} %param.8) | copy-start | bytes 52
  31.2 31.8 %collective-permute-start.2 = (bf16[128,1024]{1,0:T(8,128)(2,1)S(1)}, bf16[128,1024]{1,0:T(8,128)(2,1)S(1)}, u32[]{:S(2)}, u32[]{:S(2)}) collective-permute-start(bf16[128,1024]{1,0:T(8,128)(2,1)S(1)} %slice_select_fusion), channel_id=1, source_target_pairs={{480,0},{488,8},{48,16},{56,24},{0,32},{8,40},{80,48},{88,56},{32,... | collective-permute-start | bytes 786440 | tf_op jit(solution)/shard_map/ppermute | solution.py:337
  68.4 11.9 %collective-permute-start.4 = (bf16[256,1024]{1,0:T(8,128)(2,1)S(1)}, bf16[256,1024]{1,0:T(8,128)(2,1)S(1)}, u32[]{:S(2)}, u32[]{:S(2)}) collective-permute-start(bf16[256,1024]{1,0:T(8,128)(2,1)S(1)} %all_gather.7.f0), channel_id=1, source_target_pairs={{24,0},{0,8},{8,16},{16,24},{56,32},{32,40},{40,48},{48,56},{88,64... | collective-permute-start | bytes 1572872 | tf_op jit(solution)/shard_map/ppermute | solution.py:337
  70.3 10.7 %collective-permute-start.3 = (bf16[256,1024]{1,0:T(8,128)(2,1)S(1)}, bf16[256,1024]{1,0:T(8,128)(2,1)S(1)}, u32[]{:S(2)}, u32[]{:S(2)}) collective-permute-start(bf16[256,1024]{1,0:T(8,128)(2,1)S(1)} %all_gather.7.f0), channel_id=1, source_target_pairs={{8,0},{16,8},{24,16},{0,24},{40,32},{48,40},{56,48},{32,56},{72,64... | collective-permute-start | bytes 1572872 | tf_op jit(solution)/shard_map/ppermute | solution.py:337
  81.0 11.2 %copy-start.3 = (f32[512]{0:T(512)S(1)}, f32[512]{0:T(512)}, u32[]{:S(2)}) copy-start(f32[512]{0:T(512)} %param.9) | copy-start | bytes 6148
  81.0 11.1 %collective-permute-start.5 = (bf16[256,512]{1,0:T(8,128)(2,1)S(1)}, bf16[256,512]{1,0:T(8,128)(2,1)S(1)}, u32[]{:S(2)}, u32[]{:S(2)}) collective-permute-start(bf16[256,512]{1,0:T(8,128)(2,1)S(1)} %slice.16), channel_id=1, source_target_pairs={{8,0},{16,8},{24,16},{0,24},{40,32},{48,40},{56,48},{32,56},{72,64... | collective-permute-start | bytes 786440 | tf_op jit(solution)/shard_map/ppermute | solution.py:337
  86.1 11.1 %collective-permute-start.6 = (bf16[256,512]{1,0:T(8,128)(2,1)S(1)}, bf16[256,512]{1,0:T(8,128)(2,1)S(1)}, u32[]{:S(2)}, u32[]{:S(2)}) collective-permute-start(bf16[256,512]{1,0:T(8,128)(2,1)S(1)} %slice.17), channel_id=1, source_target_pairs={{24,0},{0,8},{8,16},{16,24},{56,32},{32,40},{40,48},{48,56},{88,64... | collective-permute-start | bytes 786440 | tf_op jit(solution)/shard_map/ppermute | solution.py:337

commit v7 on v6

--- a/solution.py
+++ b/solution.py
@@ -73,13 +73,25 @@
     )(keys, values)
 
 
-def near_kernel(
-    pair, seq_size, dev_ref, temp_ref, q_ref, k_ref, v_ref,
-    upk, upv, dnk, dnv, onk, onv, twok, twov, nextk, nextv,
-    acc_ref, ml_ref, sa, sb, pa, pb,
+def near_kernel(pair, seq_size, *refs):
+    for i in range(2):
+        near_head(pair, seq_size, i, *refs)
+
+
+def near_head(
+    pair, seq_size, i, dev_ref, temp_ref, q_all, k_all, v_all, up_all, down_all, one_all, two_all,
+    next_all, acc_all, ml_all, sa, sb, pa, pb,
 ):
+    def head_cols(ref, first):
+        return ref.at[:, HEAD_DIM * (first + i) : HEAD_DIM * (first + i + 1)]
+
+    q_ref, k_ref, v_ref = [head_cols(ref, 2 * pair) for ref in (q_all, k_all, v_all)]
+    acc_ref, ml_ref = head_cols(acc_all, 0), head_cols(ml_all, 0)
+    edges = (up_all, down_all, one_all, two_all, next_all)
+    upk, dnk, onk, twok, nextk = [head_cols(ref, 4 * pair) for ref in edges]
+    upv, dnv, onv, twov, nextv = [head_cols(ref, 4 * pair + 2) for ref in edges]
     dev = dev_ref[0]
-    c = temp_ref[2 * pair + pl.program_id(0)]
+    c = temp_ref[2 * pair + i]
     z, y = dev // Y, dev % Y
 
     def gate(ok):
@@ -167,27 +179,16 @@
 def near(pair, seq_size, dev, temp, queries, keys, values, up, down, one, two, beyond):
     smem = pl.BlockSpec(memory_space=pltpu.SMEM)
 
-    def own(rows):
-        return pl.BlockSpec((rows, HEAD_DIM), lambda i: (0, 2 * pair + i))
-
-    def packed(rows):
-        return [
-            pl.BlockSpec((rows, HEAD_DIM), lambda i: (0, 4 * pair + i)),
-            pl.BlockSpec((rows, HEAD_DIM), lambda i: (0, 4 * pair + 2 + i)),
-        ]
-
-    out = pl.BlockSpec((ROWS, HEAD_DIM), lambda i: (0, i))
+    whole = pl.BlockSpec(memory_space=pltpu.VMEM)
     return pl.pallas_call(
         functools.partial(near_kernel, pair, seq_size),
-        grid=(2,),
-        in_specs=[smem, smem, own(ROWS), own(ROWS), own(ROWS)]
-        + packed(256) + packed(256) + packed(256) + packed(256) + packed(128),
-        out_specs=(out, out),
+        in_specs=[smem, smem] + [whole] * 8,
+        out_specs=(whole, whole),
         out_shape=(sds((ROWS, PAIR), F32), sds((ROWS, PAIR), F32)),
         scratch_shapes=[pltpu.VMEM((128, 1152), F32)] * 2 + [pltpu.VMEM((128, 1152), BF)] * 2,
         compiler_params=params(),
         cost_estimate=cost(2_000_000_000, 6_000_000, 2_500_000),
-    )(dev, temp, queries, keys, values, up, up, down, down, one, one, two, two, beyond, beyond)
+    )(dev, temp, queries, keys, values, up, down, one, two, beyond)
 
 
 CHUNK = 256
@@ -352,7 +353,10 @@
 
 
 def joined(value, groups):
-    return lax.all_gather(value, "seq", axis_index_groups=groups, axis=0, tiled=True)
+    rows, columns = value.shape
+    tiles = value.reshape(rows // 8, 8, columns)
+    blocks = lax.all_gather(tiles, "seq", axis_index_groups=groups, axis=0, tiled=True)
+    return blocks.reshape(len(groups[0]) * rows, columns)
 
 
 def local(queries, keys, values, head_temp, norm_gain):

time: 126 us -> 126 us (level)
  transfers between devices with their start and end apart: 7 -> 7, of which waited for: 2 -> 2; matrix products, arithmetic and copies ran while one was open for 0% -> 0% of each run, Pallas kernels for 8% -> 9%
where the time goes in v7:
time: 126 us; the launch traced here: 125 us
  blocking collectives  61.9 us (49%)
  starting transfers between devices  30.6 us (24%)
  Pallas kernels  26 us (21%)
  waiting for transfers between devices  4.13 us (3%)
  local copies, waits for them, and re-layouts  2.53 us (2%)
    all_gather x2, blocking collectives, joined(): lax.all_gather(tiles, 'seq', axis_index_groups=groups, axis=0, tiled=True)  40.9 us
    ppermute x7, starting transfers between devices, fetch(): lax.ppermute(value, axis, [(source(i) % count, i) for i in range(count)])  30.6 us
    all_to_all x1, blocking collectives, gathered(): return lax.all_to_all(many, axis, 0, 0, tiled=True)  21.1 us
    pallas_call x2, Pallas kernels, near(): pl.pallas_call(functools.partial(near_kernel, pair, seq_size), in_specs=[...  11.8 us
    pallas_call x2, Pallas kernels, far(): pl.pallas_call(functools.partial(far_kernel, pair, before is not None), i...  10.1 us
    ppermute x7, waiting for transfers between devices, fetch(): lax.ppermute(value, axis, [(source(i) % count, i) for i in range(count)])  4.13 us
  transfers between devices with their start and end apart: 7, of which 2 were waited for; matrix products, arithmetic and copies ran while one was open for 0% of the time, Pallas kernels for 9%

profile of v7, /device:TPU:1, one launch (start us, length us, event | category | flops | bytes accessed | tf_op | source)
XLA Modules:
  0.0 125.4 jit_solution(4549948414181728472)
XLA Ops:
  0.0 0.0 copy-start.2
  0.0 1.2 copy-done.2
  1.2 0.0 copy-start.3
  1.2 1.2 copy-done.3
  2.5 2.2 %shard_map.55 = (bf16[256,1024]{1,0:T(8,128)(2,1)}, bf16[256,1024]{1,0:T(8,128)(2,1)S(1)}, bf16[256,1024]{1,0:T(8,128)(2,1)S(1)}, bf16[64,1024]{1,0:T(8,128)(2,1)S(1)}, bf16[16,1024]{1,0:T(8,128)(2,1)S(1)}) custom-call(bf16[1024,512]{1,0:T(8,128)(2,1)S(1)} %copy-done.2, bf16[1024,512]{1,0:T(8,128)(2,1)S(1)} %copy-done.3), custom_call_target="tpu_custom_call" | custom-call | flops 700000000 | bytes 5000000 | tf_op jit(solution)/shard_map/pallas_call | solution.py:62
  4.6 0.0 copy-start.4
  4.6 0.0 copy-start
  4.6 0.0 copy-start.6
  4.7 11.4 %all_gather.6 = bf16[32,8,1024]{2,1,0:T(8,128)(2,1)S(1)} all-gather(bf16[8,8,1024]{2,1,0:T(8,128)(2,1)S(1)} %bitcast.18), channel_id=1, replica_groups={{0,8,16,24},{32,40,48,56},{64,72,80,88},{96,104,112,120},{128,136,144,1..., dimensions={0}, use_global_device_ids=true | all-gather | bytes 655360 | tf_op jit(solution)/shard_map/all_gather | solution.py:358
  16.0 2.9 %collective-permute-start = (bf16[256,1024]{1,0:T(8,128)(2,1)}, bf16[256,1024]{1,0:T(8,128)(2,1)S(1)}, u32[]{:S(2)}, u32[]{:S(2)}) collective-permute-start(bf16[256,1024]{1,0:T(8,128)(2,1)} %get-tuple-element.34), channel_id=1, source_target_pairs={{504,0},{0,8},{8,16},{16,24},{24,32},{32,40},{40,48},{48,56},{56,6... | collective-permute-start | bytes 1572872 | tf_op jit(solution)/shard_map/ppermute | solution.py:338
  18.9 12.1 %collective-permute-start.1 = (bf16[256,1024]{1,0:T(8,128)(2,1)S(1)}, bf16[256,1024]{1,0:T(8,128)(2,1)S(1)}, u32[]{:S(2)}, u32[]{:S(2)}) collective-permute-start(bf16[256,1024]{1,0:T(8,128)(2,1)S(1)} %get-tuple-element.35), channel_id=1, source_target_pairs={{8,0},{16,8},{24,16},{32,24},{40,32},{48,40},{56,48},{64,56},{72,6... | collective-permute-start | bytes 1572872 | tf_op jit(solution)/shard_map/ppermute | solution.py:338
  31.0 0.0 copy-done.4
  31.0 0.0 copy-start.5
  31.1 2.1 %collective-permute-start.2 = (bf16[128,1024]{1,0:T(8,128)(2,1)S(1)}, bf16[128,1024]{1,0:T(8,128)(2,1)S(1)}, u32[]{:S(2)}, u32[]{:S(2)}) collective-permute-start(bf16[128,1024]{1,0:T(8,128)(2,1)S(1)} %slice_select_fusion), channel_id=1, source_target_pairs={{480,0},{488,8},{48,16},{56,24},{0,32},{8,40},{80,48},{88,56},{32,... | collective-permute-start | bytes 786440 | tf_op jit(solution)/shard_map/ppermute | solution.py:338
  33.1 0.0 copy-done.6
  33.1 29.5 %all_gather.7 = bf16[32,8,1024]{2,1,0:T(8,128)(2,1)S(1)} all-gather(bf16[2,8,1024]{2,1,0:T(8,128)(2,1)S(1)} %bitcast.19), channel_id=1, replica_groups={{0,32,64,96,128,160,192,224,256,288,320,352,384,416,448,480},{8,40,72,1..., dimensions={0}, use_global_device_ids=true | all-gather | bytes 557056 | tf_op jit(solution)/shard_map/all_gather | solution.py:358
  62.7 0.0 collective-permute-done.2.refs_9_
  62.7 0.0 collective-permute-done.refs_5_
  62.7 0.0 collective-permute-done.1.refs_6_
  62.7 0.0 copy-done
  62.7 0.0 copy-done.5
  62.7 5.9 %shard_map.56 = (f32[1024,256]{1,0:T(8,128)S(1)}, f32[1024,256]{1,0:T(8,128)S(1)}) custom-call(s32[1]{0:T(128)} %bitcast.refs_0_.dev_ref, f32[4]{0:T(128)S(1)} %broadcast_multiply_fusion.refs_1_.temp_ref, bf16[1024,512]{1,0:T(8,128)(2,1)S(1)} %copy-done, bf16[1024,512]{1,0:T(8,128)(2,1)} %refs_3_.3, bf16[1024,512]{1,0:T(8,128)(2,1)} %refs_4_.3, ...), custom_call_target="tpu_custom_call" | custom-call | flops 2000000000 | bytes 6000000 | tf_op jit(solution)/shard_map/pallas_call | solution.py:183
  68.6 1.9 %collective-permute-start.4 = (bf16[256,1024]{1,0:T(8,128)(2,1)S(1)}, bf16[256,1024]{1,0:T(8,128)(2,1)S(1)}, u32[]{:S(2)}, u32[]{:S(2)}) collective-permute-start(bf16[256,1024]{1,0:T(8,128)(2,1)S(1)} %bitcast.10), channel_id=1, source_target_pairs={{24,0},{0,8},{8,16},{16,24},{56,32},{32,40},{40,48},{48,56},{88,64... | collective-permute-start | bytes 1572872 | tf_op jit(solution)/shard_map/ppermute | solution.py:338
  70.5 4.6 %collective-permute-start.3 = (bf16[256,1024]{1,0:T(8,128)(2,1)S(1)}, bf16[256,1024]{1,0:T(8,128)(2,1)S(1)}, u32[]{:S(2)}, u32[]{:S(2)}) collective-permute-start(bf16[256,1024]{1,0:T(8,128)(2,1)S(1)} %bitcast.11), channel_id=1, source_target_pairs={{8,0},{16,8},{24,16},{0,24},{40,32},{48,40},{56,48},{32,56},{72,64... | collective-permute-start | bytes 1572872 | tf_op jit(solution)/shard_map/ppermute | solution.py:338
  75.1 5.9 %shard_map.57 = (f32[1024,256]{1,0:T(8,128)S(1)}, f32[1024,256]{1,0:T(8,128)S(1)}) custom-call(s32[1]{0:T(128)} %bitcast.refs_0_.dev_ref, f32[4]{0:T(128)S(1)} %broadcast_multiply_fusion.refs_1_.temp_ref, bf16[1024,512]{1,0:T(8,128)(2,1)S(1)} %copy-done, bf16[1024,512]{1,0:T(8,128)(2,1)} %refs_3_.3, bf16[1024,512]{1,0:T(8,128)(2,1)} %refs_4_.3, ...), custom_call_target="tpu_custom_call" | custom-call | flops 2000000000 | bytes 6000000 | tf_op jit(solution)/shard_map/pallas_call | solution.py:183
  81.1 0.0 collective-permute-done.4.f3
  81.1 0.1 collective-permute-done.3.f1
  81.2 0.0 copy-start.1
  81.3 5.0 %collective-permute-start.5 = (bf16[256,512]{1,0:T(8,128)(2,1)S(1)}, bf16[256,512]{1,0:T(8,128)(2,1)S(1)}, u32[]{:S(2)}, u32[]{:S(2)}) collective-permute-start(bf16[256,512]{1,0:T(8,128)(2,1)S(1)} %slice.16), channel_id=1, source_target_pairs={{8,0},{16,8},{24,16},{0,24},{40,32},{48,40},{56,48},{32,56},{72,64... | collective-permute-start | bytes 786440 | tf_op jit(solution)/shard_map/ppermute | solution.py:338
  86.3 2.1 %collective-permute-start.6 = (bf16[256,512]{1,0:T(8,128)(2,1)S(1)}, bf16[256,512]{1,0:T(8,128)(2,1)S(1)}, u32[]{:S(2)}, u32[]{:S(2)}) collective-permute-start(bf16[256,512]{1,0:T(8,128)(2,1)S(1)} %slice.17), channel_id=1, source_target_pairs={{24,0},{0,8},{8,16},{16,24},{56,32},{32,40},{40,48},{48,56},{88,64... | collective-permute-start | bytes 786440 | tf_op jit(solution)/shard_map/ppermute | solution.py:338
  88.4 4.0 %collective-permute-done.5.f2 = bf16[256,512]{1,0:T(8,128)(2,1)S(1)} collective-permute-done((bf16[256,512]{1,0:T(8,128)(2,1)S(1)}, bf16[256,512]{1,0:T(8,128)(2,1)S(1)}, u32[]{:S(2)}, u32[]{:S(2)}) %collective-permute-start.5) | collective-permute-done | bytes 262176 | tf_op jit(solution)/shard_map/ppermute | solution.py:338
  92.4 0.0 copy-done.1
  92.4 5.0 %shard_map.58 = (f32[1024,256]{1,0:T(8,128)S(1)}, f32[1,1024]{1,0:T(1,128)S(1)}) custom-call(s32[1]{0:T(128)} %bitcast.refs_0_.dev_ref, f32[4]{0:T(128)S(1)} %broadcast_multiply_fusion.refs_1_.temp_ref, bf16[1024,512]{1,0:T(8,128)(2,1)S(1)} %copy-done, f32[1024,256]{1,0:T(8,128)S(1)} %get-tuple-element.40.acc_ref, f32[1024,256]{1,0:T(8,128)S(1)} %get-tuple-element.41.ml_ref, ...), custom_call_target="tpu_custom_call" | custom-call | flops 1200000000 | bytes 5000000 | tf_op jit(solution)/shard_map/pallas_call | solution.py:295
  97.4 0.0 collective-permute-done.6.f2
  97.4 5.1 %shard_map.59 = (f32[1024,256]{1,0:T(8,128)S(1)}, f32[1,1024]{1,0:T(1,128)S(1)}) custom-call(s32[1]{0:T(128)} %bitcast.refs_0_.dev_ref, f32[4]{0:T(128)S(1)} %broadcast_multiply_fusion.refs_1_.temp_ref, bf16[1024,512]{1,0:T(8,128)(2,1)S(1)} %copy-done, f32[1024,256]{1,0:T(8,128)S(1)} %get-tuple-element.47.acc_ref, f32[1024,256]{1,0:T(8,128)S(1)} %get-tuple-element.48.ml_ref, ...), custom_call_target="tpu_custom_call" | custom-call | flops 1200000000 | bytes 5000000 | tf_op jit(solution)/shard_map/pallas_call | solution.py:295
  102.5 21.1 %all_to_all.5 = f32[8,1,1024]{2,1,0:T(1,128)S(1)} all-to-all(f32[8,1,1024]{2,1,0:T(1,128)S(1)} %broadcast_in_dim.9), channel_id=1, replica_groups=mesh['seq'=64,'head'=8] {'head'}, dimensions={0} | all-to-all | bytes 65536 | tf_op jit(solution)/shard_map/all_to_all | solution.py:348
  123.6 1.8 %shard_map.60 = bf16[1024,512]{1,0:T(8,128)(2,1)} custom-call(f32[1024,256]{1,0:T(8,128)S(1)} %get-tuple-element.46.a_ref, f32[1024,256]{1,0:T(8,128)S(1)} %get-tuple-element.51.b_ref, f32[8,1024]{1,0:T(8,128)S(1)} %bitcast.17), custom_call_target="tpu_custom_call" | custom-call | flops 2000000 | bytes 3000000 | tf_op jit(solution)/shard_map/pallas_call | solution.py:325
  (6 shorter events, 0.1 us)
Async XLA Ops:
  0.0 1.2 copy-start.2
  1.2 1.2 copy-start.3
  4.6 26.4 %copy-start.4 = (bf16[256,1024]{1,0:T(8,128)(2,1)}, bf16[256,1024]{1,0:T(8,128)(2,1)S(1)}, u32[]{:S(2)}) copy-start(bf16[256,1024]{1,0:T(8,128)(2,1)S(1)} %get-tuple-element.36.refs_7_) | copy-start | bytes 1572868
  4.6 58.0 %copy-start = (bf16[1024,512]{1,0:T(8,128)(2,1)S(1)}, bf16[1024,512]{1,0:T(8,128)(2,1)}, u32[]{:S(2)}) copy-start(bf16[1024,512]{1,0:T(8,128)(2,1)} %q_ref.3) | copy-start | bytes 3145732
  4.6 28.5 %copy-start.6 = (f32[4]{0:T(128)S(1)}, f32[4]{0:T(128)}, u32[]{:S(2)}) copy-start(f32[4]{0:T(128)} %param.8) | copy-start | bytes 52
  16.0 46.6 %collective-permute-start = (bf16[256,1024]{1,0:T(8,128)(2,1)}, bf16[256,1024]{1,0:T(8,128)(2,1)S(1)}, u32[]{:S(2)}, u32[]{:S(2)}) collective-permute-start(bf16[256,1024]{1,0:T(8,128)(2,1)} %get-tuple-element.34), channel_id=1, source_target_pairs={{504,0},{0,8},{8,16},{16,24},{24,32},{32,40},{40,48},{48,56},{56,6... | collective-permute-start | bytes 1572872 | tf_op jit(solution)/shard_map/ppermute | solution.py:338
  18.9 43.7 %collective-permute-start.1 = (bf16[256,1024]{1,0:T(8,128)(2,1)S(1)}, bf16[256,1024]{1,0:T(8,128)(2,1)S(1)}, u32[]{:S(2)}, u32[]{:S(2)}) collective-permute-start(bf16[256,1024]{1,0:T(8,128)(2,1)S(1)} %get-tuple-element.35), channel_id=1, source_target_pairs={{8,0},{16,8},{24,16},{32,24},{40,32},{48,40},{56,48},{64,56},{72,6... | collective-permute-start | bytes 1572872 | tf_op jit(solution)/shard_map/ppermute | solution.py:338
  31.0 31.7 %copy-start.5 = (bf16[256,1024]{1,0:T(8,128)(2,1)S(1)}, bf16[256,1024]{1,0:T(8,128)(2,1)}, u32[]{:S(2)}) copy-start(bf16[256,1024]{1,0:T(8,128)(2,1)} %copy-done.4) | copy-start | bytes 1572868
  31.1 31.6 %collective-permute-start.2 = (bf16[128,1024]{1,0:T(8,128)(2,1)S(1)}, bf16[128,1024]{1,0:T(8,128)(2,1)S(1)}, u32[]{:S(2)}, u32[]{:S(2)}) collective-permute-start(bf16[128,1024]{1,0:T(8,128)(2,1)S(1)} %slice_select_fusion), channel_id=1, source_target_pairs={{480,0},{488,8},{48,16},{56,24},{0,32},{8,40},{80,48},{88,56},{32,... | collective-permute-start | bytes 786440 | tf_op jit(solution)/shard_map/ppermute | solution.py:338
  68.6 12.5 %collective-permute-start.4 = (bf16[256,1024]{1,0:T(8,128)(2,1)S(1)}, bf16[256,1024]{1,0:T(8,128)(2,1)S(1)}, u32[]{:S(2)}, u32[]{:S(2)}) collective-permute-start(bf16[256,1024]{1,0:T(8,128)(2,1)S(1)} %bitcast.10), channel_id=1, source_target_pairs={{24,0},{0,8},{8,16},{16,24},{56,32},{32,40},{40,48},{48,56},{88,64... | collective-permute-start | bytes 1572872 | tf_op jit(solution)/shard_map/ppermute | solution.py:338
  70.5 10.7 %collective-permute-start.3 = (bf16[256,1024]{1,0:T(8,128)(2,1)S(1)}, bf16[256,1024]{1,0:T(8,128)(2,1)S(1)}, u32[]{:S(2)}, u32[]{:S(2)}) collective-permute-start(bf16[256,1024]{1,0:T(8,128)(2,1)S(1)} %bitcast.11), channel_id=1, source_target_pairs={{8,0},{16,8},{24,16},{0,24},{40,32},{48,40},{56,48},{32,56},{72,64... | collective-permute-start | bytes 1572872 | tf_op jit(solution)/shard_map/ppermute | solution.py:338
  81.2 11.2 %copy-start.1 = (f32[512]{0:T(512)S(1)}, f32[512]{0:T(512)}, u32[]{:S(2)}) copy-start(f32[512]{0:T(512)} %param.9) | copy-start | bytes 6148
  81.3 11.1 %collective-permute-start.5 = (bf16[256,512]{1,0:T(8,128)(2,1)S(1)}, bf16[256,512]{1,0:T(8,128)(2,1)S(1)}, u32[]{:S(2)}, u32[]{:S(2)}) collective-permute-start(bf16[256,512]{1,0:T(8,128)(2,1)S(1)} %slice.16), channel_id=1, source_target_pairs={{8,0},{16,8},{24,16},{0,24},{40,32},{48,40},{56,48},{32,56},{72,64... | collective-permute-start | bytes 786440 | tf_op jit(solution)/shard_map/ppermute | solution.py:338
  86.3 11.1 %collective-permute-start.6 = (bf16[256,512]{1,0:T(8,128)(2,1)S(1)}, bf16[256,512]{1,0:T(8,128)(2,1)S(1)}, u32[]{:S(2)}, u32[]{:S(2)}) collective-permute-start(bf16[256,512]{1,0:T(8,128)(2,1)S(1)} %slice.17), channel_id=1, source_target_pairs={{24,0},{0,8},{8,16},{16,24},{56,32},{32,40},{40,48},{48,56},{88,64... | collective-permute-start | bytes 786440 | tf_op jit(solution)/shard_map/ppermute | solution.py:338

commit v8 on v6

--- a/solution.py
+++ b/solution.py
@@ -370,14 +370,16 @@
     beyond = fetch(other_half, "seq", lambda i: i - Y if i % Y < 2 else i + Y)
 
     column = joined(three, Z_RING)
+    column, from_up, from_down, beyond = lax.optimization_barrier(
+        (column, from_up, from_down, beyond)
+    )
     near_args = (queries, keys, values, from_up, from_down, one, group_two, beyond)
     acc_a, ml_a = near(0, seq_size, dev, temp, *near_args)
     acc_b, ml_b = near(1, seq_size, dev, temp, *near_args)
-    column, acc_a, ml_a = lax.optimization_barrier((column, acc_a, ml_a))
     after = fetch_y(column, 1)
     before = fetch_y(column, -1)
-    half_a, half_b, acc_b, ml_b = lax.optimization_barrier(
-        (after[:, :512], before[:, 512:], acc_b, ml_b)
+    half_a, half_b, acc_a, ml_a, acc_b, ml_b = lax.optimization_barrier(
+        (after[:, :512], before[:, 512:], acc_a, ml_a, acc_b, ml_b)
     )
     opposite_a = fetch_y(half_a, 1)
     opposite_b = fetch_y(half_b, -1)

time: 126 us -> 119 us (0.944)
  waiting for transfers between devices: 4.89 us -> 1.83 us
  starting transfers between devices: 30.3 us -> 27.5 us
    ppermute x7, waiting for transfers between devices: 4.89 us -> 1.83 us  [fetch(): lax.ppermute(value, axis, [(source(i) % count, i) for i in range(count)])]
    ppermute x7, starting transfers between devices: 30.3 us -> 27.5 us  [fetch(): lax.ppermute(value, axis, [(source(i) % count, i) for i in range(count)])]
  transfers between devices with their start and end apart: 7 -> 7, of which waited for: 2 -> 1; matrix products, arithmetic and copies ran while one was open for 0% -> 0% of each run, Pallas kernels for 8% -> 13%
where the time goes in v8:
time: 119 us; the launch traced here: 118 us
  blocking collectives  61.2 us (51%)
  starting transfers between devices  27.5 us (23%)
  Pallas kernels  25 us (21%)
  local copies, waits for them, and re-layouts  2.53 us (2%)
  waiting for transfers between devices  1.83 us (2%)
    all_gather x2, blocking collectives, joined(): lax.all_gather(value, 'seq', axis_index_groups=groups, axis=0, tiled=True)  41.2 us
    ppermute x7, starting transfers between devices, fetch(): lax.ppermute(value, axis, [(source(i) % count, i) for i in range(count)])  27.5 us
    all_to_all x1, blocking collectives, gathered(): return lax.all_to_all(many, axis, 0, 0, tiled=True)  20 us
    pallas_call x2, Pallas kernels, near(): pl.pallas_call(functools.partial(near_kernel, pair, seq_size), grid=(2,),...  10.7 us
    pallas_call x2, Pallas kernels, far(): pl.pallas_call(functools.partial(far_kernel, pair, before is not None), i...  10.1 us
    unnamed x11, local copies, waits for them, and re-layouts  2.47 us
  transfers between devices with their start and end apart: 7, of which 1 were waited for; matrix products, arithmetic and copies ran while one was open for 0% of the time, Pallas kernels for 13%

profile of v8, /device:TPU:1, one launch (start us, length us, event | category | flops | bytes accessed | tf_op | source)
XLA Modules:
  0.0 118.2 jit_solution(12411810361193176106)
XLA Ops:
  0.0 0.0 copy-start.1
  0.0 1.2 %copy-done.1 = bf16[1024,512]{1,0:T(8,128)(2,1)S(1)} copy-done((bf16[1024,512]{1,0:T(8,128)(2,1)S(1)}, bf16[1024,512]{1,0:T(8,128)(2,1)}, u32[]{:S(2)}) %copy-start.1) | copy-done | bytes 1048600
  1.2 0.0 copy-start.2
  1.2 1.2 %copy-done.2 = bf16[1024,512]{1,0:T(8,128)(2,1)S(1)} copy-done((bf16[1024,512]{1,0:T(8,128)(2,1)S(1)}, bf16[1024,512]{1,0:T(8,128)(2,1)}, u32[]{:S(2)}) %copy-start.2) | copy-done | bytes 1048600
  2.5 2.4 %shard_map.55 = (bf16[256,1024]{1,0:T(8,128)(2,1)}, bf16[256,1024]{1,0:T(8,128)(2,1)}, bf16[256,1024]{1,0:T(8,128)(2,1)S(1)}, bf16[64,1024]{1,0:T(8,128)(2,1)S(1)}, bf16[16,1024]{1,0:T(8,128)(2,1)S(1)}) custom-call(bf16[1024,512]{1,0:T(8,128)(2,1)S(1)} %copy-done.1, bf16[1024,512]{1,0:T(8,128)(2,1)S(1)} %copy-done.2), custom_call_target="tpu_custom_call" | custom-call | flops 700000000 | bytes 5000000 | tf_op jit(solution)/shard_map/pallas_call | solution.py:62
  4.8 0.0 copy-start
  4.8 11.4 %all_gather.6.twok.twov = bf16[256,1024]{1,0:T(8,128)(2,1)S(1)} all-gather(bf16[64,1024]{1,0:T(8,128)(2,1)S(1)} %get-tuple-element.35), channel_id=1, replica_groups={{0,8,16,24},{32,40,48,56},{64,72,80,88},{96,104,112,120},{128,136,144,1..., dimensions={0}, use_global_device_ids=true | all-gather | bytes 655360 | tf_op jit(solution)/shard_map/all_gather | solution.py:355
  16.2 2.9 %collective-permute-start = (bf16[256,1024]{1,0:T(8,128)(2,1)}, bf16[256,1024]{1,0:T(8,128)(2,1)S(1)}, u32[]{:S(2)}, u32[]{:S(2)}) collective-permute-start(bf16[256,1024]{1,0:T(8,128)(2,1)} %get-tuple-element.37), channel_id=1, source_target_pairs={{504,0},{0,8},{8,16},{16,24},{24,32},{32,40},{40,48},{48,56},{56,6... | collective-permute-start | bytes 1572872 | tf_op jit(solution)/shard_map/ppermute | solution.py:337
  19.1 12.1 %collective-permute-start.1 = (bf16[256,1024]{1,0:T(8,128)(2,1)}, bf16[256,1024]{1,0:T(8,128)(2,1)S(1)}, u32[]{:S(2)}, u32[]{:S(2)}) collective-permute-start(bf16[256,1024]{1,0:T(8,128)(2,1)} %get-tuple-element.38), channel_id=1, source_target_pairs={{8,0},{16,8},{24,16},{32,24},{40,32},{48,40},{56,48},{64,56},{72,6... | collective-permute-start | bytes 1572872 | tf_op jit(solution)/shard_map/ppermute | solution.py:337
  31.2 0.0 copy-start.4
  31.2 1.9 %collective-permute-start.2 = (bf16[128,1024]{1,0:T(8,128)(2,1)S(1)}, bf16[128,1024]{1,0:T(8,128)(2,1)S(1)}, u32[]{:S(2)}, u32[]{:S(2)}) collective-permute-start(bf16[128,1024]{1,0:T(8,128)(2,1)S(1)} %slice_select_fusion), channel_id=1, source_target_pairs={{480,0},{488,8},{48,16},{56,24},{0,32},{8,40},{80,48},{88,56},{32,... | collective-permute-start | bytes 786440 | tf_op jit(solution)/shard_map/ppermute | solution.py:337
  33.2 29.8 %all_gather.7.f0 = bf16[256,1024]{1,0:T(8,128)(2,1)S(1)} all-gather(bf16[16,1024]{1,0:T(8,128)(2,1)S(1)} %get-tuple-element.36), channel_id=1, replica_groups={{0,32,64,96,128,160,192,224,256,288,320,352,384,416,448,480},{8,40,72,1..., dimensions={0}, use_global_device_ids=true | all-gather | bytes 557056 | tf_op jit(solution)/shard_map/all_gather | solution.py:355
  63.0 0.0 collective-permute-done.2.nextk.nextv
  63.0 0.0 collective-permute-done.upk.upv
  63.0 0.0 collective-permute-done.1.dnk.dnv
  63.0 1.9 %collective-permute-start.3 = (bf16[256,1024]{1,0:T(8,128)(2,1)S(1)}, bf16[256,1024]{1,0:T(8,128)(2,1)S(1)}, u32[]{:S(2)}, u32[]{:S(2)}) collective-permute-start(bf16[256,1024]{1,0:T(8,128)(2,1)S(1)} %all_gather.7.f0), channel_id=1, source_target_pairs={{8,0},{16,8},{24,16},{0,24},{40,32},{48,40},{56,48},{32,56},{72,64... | collective-permute-start | bytes 1572872 | tf_op jit(solution)/shard_map/ppermute | solution.py:337
  64.9 3.4 %collective-permute-start.4 = (bf16[256,1024]{1,0:T(8,128)(2,1)S(1)}, bf16[256,1024]{1,0:T(8,128)(2,1)S(1)}, u32[]{:S(2)}, u32[]{:S(2)}) collective-permute-start(bf16[256,1024]{1,0:T(8,128)(2,1)S(1)} %all_gather.7.f0), channel_id=1, source_target_pairs={{24,0},{0,8},{8,16},{16,24},{56,32},{32,40},{40,48},{48,56},{88,64... | collective-permute-start | bytes 1572872 | tf_op jit(solution)/shard_map/ppermute | solution.py:337
  68.3 0.0 copy-done.4
  68.3 0.0 copy-done
  68.3 5.4 %shard_map.57 = (f32[1024,256]{1,0:T(8,128)S(1)}, f32[1024,256]{1,0:T(8,128)S(1)}) custom-call(s32[1]{0:T(128)} %bitcast.dev_ref, f32[4]{0:T(128)S(1)} %broadcast_multiply_fusion.temp_ref, bf16[1024,512]{1,0:T(8,128)(2,1)S(1)} %copy-done, bf16[1024,512]{1,0:T(8,128)(2,1)} %k_ref.5, bf16[1024,512]{1,0:T(8,128)(2,1)} %v_ref.5, ...), custom_call_target="tpu_custom_call" | custom-call | flops 2000000000 | bytes 6000000 | tf_op jit(solution)/shard_map/pallas_call | solution.py:180
  73.7 5.4 %shard_map.56 = (f32[1024,256]{1,0:T(8,128)S(1)}, f32[1024,256]{1,0:T(8,128)S(1)}) custom-call(s32[1]{0:T(128)} %bitcast.dev_ref, f32[4]{0:T(128)S(1)} %broadcast_multiply_fusion.temp_ref, bf16[1024,512]{1,0:T(8,128)(2,1)S(1)} %copy-done, bf16[1024,512]{1,0:T(8,128)(2,1)} %k_ref.5, bf16[1024,512]{1,0:T(8,128)(2,1)} %v_ref.5, ...), custom_call_target="tpu_custom_call" | custom-call | flops 2000000000 | bytes 6000000 | tf_op jit(solution)/shard_map/pallas_call | solution.py:180
  79.1 0.0 collective-permute-done.3.f1
  79.1 0.0 collective-permute-done.4.f3
  79.2 0.0 copy-start.3
  79.2 3.1 %collective-permute-start.5 = (bf16[256,512]{1,0:T(8,128)(2,1)S(1)}, bf16[256,512]{1,0:T(8,128)(2,1)S(1)}, u32[]{:S(2)}, u32[]{:S(2)}) collective-permute-start(bf16[256,512]{1,0:T(8,128)(2,1)S(1)} %slice.16), channel_id=1, source_target_pairs={{8,0},{16,8},{24,16},{0,24},{40,32},{48,40},{56,48},{32,56},{72,64... | collective-permute-start | bytes 786440 | tf_op jit(solution)/shard_map/ppermute | solution.py:337
  82.3 2.1 %collective-permute-start.6 = (bf16[256,512]{1,0:T(8,128)(2,1)S(1)}, bf16[256,512]{1,0:T(8,128)(2,1)S(1)}, u32[]{:S(2)}, u32[]{:S(2)}) collective-permute-start(bf16[256,512]{1,0:T(8,128)(2,1)S(1)} %slice.17), channel_id=1, source_target_pairs={{24,0},{0,8},{8,16},{16,24},{56,32},{32,40},{40,48},{48,56},{88,64... | collective-permute-start | bytes 786440 | tf_op jit(solution)/shard_map/ppermute | solution.py:337
  84.5 1.8 %collective-permute-done.5.f2 = bf16[256,512]{1,0:T(8,128)(2,1)S(1)} collective-permute-done((bf16[256,512]{1,0:T(8,128)(2,1)S(1)}, bf16[256,512]{1,0:T(8,128)(2,1)S(1)}, u32[]{:S(2)}, u32[]{:S(2)}) %collective-permute-start.5) | collective-permute-done | bytes 262176 | tf_op jit(solution)/shard_map/ppermute | solution.py:337
  86.3 0.0 copy-done.3
  86.3 5.0 %shard_map.58 = (f32[1024,256]{1,0:T(8,128)S(1)}, f32[1,1024]{1,0:T(1,128)S(1)}) custom-call(s32[1]{0:T(128)} %bitcast.dev_ref, f32[4]{0:T(128)S(1)} %broadcast_multiply_fusion.temp_ref, bf16[1024,512]{1,0:T(8,128)(2,1)S(1)} %copy-done, f32[1024,256]{1,0:T(8,128)S(1)} %get-tuple-element.49.acc_ref, f32[1024,256]{1,0:T(8,128)S(1)} %get-tuple-element.50.ml_ref, ...), custom_call_target="tpu_custom_call" | custom-call | flops 1200000000 | bytes 5000000 | tf_op jit(solution)/shard_map/pallas_call | solution.py:294
  91.3 0.0 collective-permute-done.6.f2
  91.3 5.1 %shard_map.59 = (f32[1024,256]{1,0:T(8,128)S(1)}, f32[1,1024]{1,0:T(1,128)S(1)}) custom-call(s32[1]{0:T(128)} %bitcast.dev_ref, f32[4]{0:T(128)S(1)} %broadcast_multiply_fusion.temp_ref, bf16[1024,512]{1,0:T(8,128)(2,1)S(1)} %copy-done, f32[1024,256]{1,0:T(8,128)S(1)} %get-tuple-element.53.acc_ref, f32[1024,256]{1,0:T(8,128)S(1)} %get-tuple-element.54.ml_ref, ...), custom_call_target="tpu_custom_call" | custom-call | flops 1200000000 | bytes 5000000 | tf_op jit(solution)/shard_map/pallas_call | solution.py:294
  96.4 20.0 %all_to_all.5 = f32[8,1,1024]{2,1,0:T(1,128)S(1)} all-to-all(f32[8,1,1024]{2,1,0:T(1,128)S(1)} %broadcast_in_dim.9), channel_id=1, replica_groups=mesh['seq'=64,'head'=8] {'head'}, dimensions={0} | all-to-all | bytes 65536 | tf_op jit(solution)/shard_map/all_to_all | solution.py:347
  116.4 1.8 %shard_map.60 = bf16[1024,512]{1,0:T(8,128)(2,1)} custom-call(f32[1024,256]{1,0:T(8,128)S(1)} %get-tuple-element.52.a_ref, f32[1024,256]{1,0:T(8,128)S(1)} %get-tuple-element.57.b_ref, f32[8,1024]{1,0:T(8,128)S(1)} %bitcast.6), custom_call_target="tpu_custom_call" | custom-call | flops 2000000 | bytes 3000000 | tf_op jit(solution)/shard_map/pallas_call | solution.py:324
  (6 shorter events, 0.1 us)
Async XLA Ops:
  0.0 1.2 %copy-start.1 = (bf16[1024,512]{1,0:T(8,128)(2,1)S(1)}, bf16[1024,512]{1,0:T(8,128)(2,1)}, u32[]{:S(2)}) copy-start(bf16[1024,512]{1,0:T(8,128)(2,1)} %k_ref.5) | copy-start | bytes 3145732
  1.2 1.2 %copy-start.2 = (bf16[1024,512]{1,0:T(8,128)(2,1)S(1)}, bf16[1024,512]{1,0:T(8,128)(2,1)}, u32[]{:S(2)}) copy-start(bf16[1024,512]{1,0:T(8,128)(2,1)} %v_ref.5) | copy-start | bytes 3145732
  4.8 63.5 %copy-start = (bf16[1024,512]{1,0:T(8,128)(2,1)S(1)}, bf16[1024,512]{1,0:T(8,128)(2,1)}, u32[]{:S(2)}) copy-start(bf16[1024,512]{1,0:T(8,128)(2,1)} %q_ref.7) | copy-start | bytes 3145732
  16.2 46.8 %collective-permute-start = (bf16[256,1024]{1,0:T(8,128)(2,1)}, bf16[256,1024]{1,0:T(8,128)(2,1)S(1)}, u32[]{:S(2)}, u32[]{:S(2)}) collective-permute-start(bf16[256,1024]{1,0:T(8,128)(2,1)} %get-tuple-element.37), channel_id=1, source_target_pairs={{504,0},{0,8},{8,16},{16,24},{24,32},{32,40},{40,48},{48,56},{56,6... | collective-permute-start | bytes 1572872 | tf_op jit(solution)/shard_map/ppermute | solution.py:337
  19.1 43.9 %collective-permute-start.1 = (bf16[256,1024]{1,0:T(8,128)(2,1)}, bf16[256,1024]{1,0:T(8,128)(2,1)S(1)}, u32[]{:S(2)}, u32[]{:S(2)}) collective-permute-start(bf16[256,1024]{1,0:T(8,128)(2,1)} %get-tuple-element.38), channel_id=1, source_target_pairs={{8,0},{16,8},{24,16},{32,24},{40,32},{48,40},{56,48},{64,56},{72,6... | collective-permute-start | bytes 1572872 | tf_op jit(solution)/shard_map/ppermute | solution.py:337
  31.2 37.1 %copy-start.4 = (f32[4]{0:T(128)S(1)}, f32[4]{0:T(128)}, u32[]{:S(2)}) copy-start(f32[4]{0:T(128)} %param.8) | copy-start | bytes 52
  31.2 31.8 %collective-permute-start.2 = (bf16[128,1024]{1,0:T(8,128)(2,1)S(1)}, bf16[128,1024]{1,0:T(8,128)(2,1)S(1)}, u32[]{:S(2)}, u32[]{:S(2)}) collective-permute-start(bf16[128,1024]{1,0:T(8,128)(2,1)S(1)} %slice_select_fusion), channel_id=1, source_target_pairs={{480,0},{488,8},{48,16},{56,24},{0,32},{8,40},{80,48},{88,56},{32,... | collective-permute-start | bytes 786440 | tf_op jit(solution)/shard_map/ppermute | solution.py:337
  63.0 16.1 %collective-permute-start.3 = (bf16[256,1024]{1,0:T(8,128)(2,1)S(1)}, bf16[256,1024]{1,0:T(8,128)(2,1)S(1)}, u32[]{:S(2)}, u32[]{:S(2)}) collective-permute-start(bf16[256,1024]{1,0:T(8,128)(2,1)S(1)} %all_gather.7.f0), channel_id=1, source_target_pairs={{8,0},{16,8},{24,16},{0,24},{40,32},{48,40},{56,48},{32,56},{72,64... | collective-permute-start | bytes 1572872 | tf_op jit(solution)/shard_map/ppermute | solution.py:337
  64.9 14.2 %collective-permute-start.4 = (bf16[256,1024]{1,0:T(8,128)(2,1)S(1)}, bf16[256,1024]{1,0:T(8,128)(2,1)S(1)}, u32[]{:S(2)}, u32[]{:S(2)}) collective-permute-start(bf16[256,1024]{1,0:T(8,128)(2,1)S(1)} %all_gather.7.f0), channel_id=1, source_target_pairs={{24,0},{0,8},{8,16},{16,24},{56,32},{32,40},{40,48},{48,56},{88,64... | collective-permute-start | bytes 1572872 | tf_op jit(solution)/shard_map/ppermute | solution.py:337
  79.2 7.1 %copy-start.3 = (f32[512]{0:T(512)S(1)}, f32[512]{0:T(512)}, u32[]{:S(2)}) copy-start(f32[512]{0:T(512)} %param.9) | copy-start | bytes 6148
  79.2 7.1 %collective-permute-start.5 = (bf16[256,512]{1,0:T(8,128)(2,1)S(1)}, bf16[256,512]{1,0:T(8,128)(2,1)S(1)}, u32[]{:S(2)}, u32[]{:S(2)}) collective-permute-start(bf16[256,512]{1,0:T(8,128)(2,1)S(1)} %slice.16), channel_id=1, source_target_pairs={{8,0},{16,8},{24,16},{0,24},{40,32},{48,40},{56,48},{32,56},{72,64... | collective-permute-start | bytes 786440 | tf_op jit(solution)/shard_map/ppermute | solution.py:337
  82.3 8.9 %collective-permute-start.6 = (bf16[256,512]{1,0:T(8,128)(2,1)S(1)}, bf16[256,512]{1,0:T(8,128)(2,1)S(1)}, u32[]{:S(2)}, u32[]{:S(2)}) collective-permute-start(bf16[256,512]{1,0:T(8,128)(2,1)S(1)} %slice.17), channel_id=1, source_target_pairs={{24,0},{0,8},{8,16},{16,24},{56,32},{32,40},{40,48},{48,56},{88,64... | collective-permute-start | bytes 786440 | tf_op jit(solution)/shard_map/ppermute | solution.py:337
